TPU v7x, 32 devices: a whole 2x2x4 slice. The times are simulated.
32 devices in a mesh: row: 8 (over z, y), col: 4 (over x, core).
Axes of the slice: x: 2, y: 2, z: 4, core: 2. Of those that a mesh axis runs over, the one named last changes fastest.
Arguments:
- coords: float32 [4, 3, 8, 4096], P(None, None, None, ('row', 'col')), may hold values from -6 to 6
- chrom_lengths: int32 [46], replicated, may hold values from 1 to 2048, 32768 in all
- band_counts: int32 [4, 8, 32, 32], P(None, None, ('row', 'col')), may hold values from 16 to 111
- inter_pairs: int32 [4, 1024, 2], replicated, may hold values from 0 to 255, as said below
- inter_counts: int32 [4, 1024], replicated, may hold values from 16 to 111
Outputs:
- grad: float32 [4, 3, 8, 4096], P(None, None, None, ('row', 'col'))
Inputs may be any that keep to these rules, and one draw needn't show every extreme that they name: `inter_pairs`: every entry names two blocks of the structure. for every g in 0 to 7 and h in 0 to 3, at most 64 entries of one structure have (I mod 32) div 4 = g and J mod 4 = h, and one such (g, h) has exactly 64; the same holds with the roles of I and J exchanged.
All inputs are finite; a program needn't handle non-finite values.
Results may differ from a plain program's by a relative error of at most 0.0003.
Values sent between devices are 32-bit elements; how exact they have to be, the bound alone decides.
No kernel may reach another device: no remote copies, remote signals or barrier semaphores. Data moves between devices by JAX's collectives and lax.ppermute only.
A program may use at most 64 MiB of HBM per device.

v0:
```python
import functools

import jax
import jax.numpy as jnp
from jax import lax
from jax.experimental import pallas as pl
from jax.experimental.pallas import tpu as pltpu
from jax.sharding import PartitionSpec as P

CONTACT_SHIFT = 3.0
CONTACT_SLOPE = 0.5
BACKGROUND = 0.5
FAR = 32.0
UNIT = 8
POINT_ROWS = 16
AXES = ("row", "col")
VMEM = pl.BlockSpec(memory_space=pltpu.VMEM)
SMEM = pl.BlockSpec(memory_space=pltpu.SMEM)


def rounded(value):
    return value.astype(jnp.bfloat16).astype(jnp.float32)


def divide(value, by):
    return value >> (by.bit_length() - 1) if by & (by - 1) == 0 else lax.div(value, by)


def modulo(value, by):
    return value & (by - 1) if by & (by - 1) == 0 else lax.rem(value, by)


class Sizes:
    def __init__(self, n_row, n_col, structures, sweeps, width):
        self.n_row, self.n_col, self.structures, self.sweeps = n_row, n_col, structures, sweeps
        self.width = width
        self.share = n_row // structures
        self.plane = self.share * n_col
        self.chips = self.plane // 2
        self.half = n_col // 2
        self.groups = n_row * n_col
        self.blocks = self.groups * sweeps
        self.slots = structures * sweeps
        self.rows = self.slots * 4 + sweeps

    def at(self, block):
        return modulo(block, self.groups) * self.sweeps + divide(block, self.groups)


def pack_kernel(sizes, coords_ref, counts_ref, *out_refs):
    sweeps, width = sizes.sweeps, sizes.width
    family = lax.div(lax.axis_index("row"), sizes.share)
    lane = lax.broadcasted_iota(jnp.int32, (width, 128), 1)
    place = lax.broadcasted_iota(jnp.int32, (width, 128), 0) + family * width
    spread = (lane == place).astype(jnp.float32)
    for k, out_ref in enumerate(out_refs):
        member = lax.rem(family + k, sizes.structures)
        norm = jnp.zeros((sweeps, 128), jnp.float32)
        for place in range(3):
            point = coords_ref[member, place]
            out_ref[pl.ds(place, sweeps, stride=4), :] = point
            high = rounded(point)
            near = high + rounded(point - high)
            norm = norm - 0.5 * CONTACT_SLOPE * near * near
        out_ref[pl.ds(3, sweeps, stride=4), :] = norm
        counts = counts_ref[member][:, 0, :].astype(jnp.float32)
        out_ref[4 * sweeps : 5 * sweeps] = jnp.dot(counts, spread, preferred_element_type=jnp.float32)


def merge_kernel(points, *refs):
    counts = refs[0][points:]
    for k, ref in enumerate(refs[:-1]):
        refs[-1][k * points : (k + 1) * points] = ref[:points]
        counts = counts + ref[points:] if k else counts
    refs[-1][(len(refs) - 1) * points :] = counts


def join_kernel(*refs):
    rows = refs[0].shape[0]
    for k, ref in enumerate(refs[:-1]):
        refs[-1][k * rows : (k + 1) * rows] = ref[...]


def prepare_kernel(sizes, lengths_ref, pairs_ref, own_ref, first_ref, marks_ref, list_ref, starts_ref, ends_ref, digits_ref):
    slots, sweeps, groups = sizes.slots, sizes.sweeps, sizes.groups
    family = lax.div(lax.axis_index("row"), sizes.share)
    here = lax.rem(lax.axis_index("row"), sizes.share) * sizes.n_col + lax.axis_index("col")
    lane = lax.broadcasted_iota(jnp.int32, (1, 128), 1)
    row = lax.broadcasted_iota(jnp.int32, (8, 128), 0)
    labels = starts_ref.shape[0]
    depth = POINT_ROWS + labels

    starts_ref[...] = jnp.zeros_like(starts_ref)
    ends_ref[...] = jnp.zeros_like(ends_ref)
    end = jnp.int32(0)
    for k in range(lengths_ref.shape[0]):
        starts_ref[k : k + 1] = jnp.full((1, 128), end)
        end = end + lengths_ref[k]
        ends_ref[k : k + 1] = jnp.full((1, 128), end)

    def mark(group, carry):
        for u in range(sweeps):
            bead = (u * groups + group) * 128 + lane
            inside = (bead >= starts_ref[...]) & (bead < ends_ref[...])
            marks_ref[group * sweeps + u] = inside.astype(jnp.float32).astype(jnp.bfloat16)
        return carry

    lax.fori_loop(0, groups, mark, 0)

    def fill(turn, carry):
        origin = lax.rem(family + (sizes.structures - turn), sizes.structures)
        for pair in range(sweeps // 2):
            value = own_ref[pl.ds(pl.multiple_of(turn * sweeps * 4 + pair * 8, 8), 8), :]
            for odd in range(2):
                value = pltpu.roll(value, 4, 0) if odd else value
                high = rounded(value)
                low = rounded(value - high)
                shifted = value + 0.5 * CONTACT_SHIFT
                shifted_high = rounded(shifted)
                shifted_low = rounded(shifted - shifted_high)
                both = jnp.where(row < 4, high, pltpu.roll(high, 4, 0))
                near = jnp.where((row & 3) == 3, 1.0, CONTACT_SLOPE * both)
                rest = jnp.where(row == 4, pltpu.roll(shifted_low, 1, 0), 0.0)
                rest = jnp.where(row == 3, shifted_high, rest)
                rest = jnp.where(row < 3, CONTACT_SLOPE * low, rest)
                u = 2 * pair + odd
                bead = (u * groups + origin * sizes.plane + here) * 128 + lane
                inside = (bead >= starts_ref[...]) & (bead < ends_ref[...])
                apart = jnp.where(inside, 0.0, -FAR)
                blank = jnp.zeros((128 - depth, 128), jnp.float32)
                turned = jnp.transpose(jnp.concatenate([near, rest, apart, blank], axis=0))
                slot = origin * sweeps + u
                first_ref[slot] = turned[:, :depth].astype(jnp.bfloat16)
                other = jnp.where(lane < POINT_ROWS, turned, -FAR - turned)
                first_ref[slots + slot] = other[:, :depth].astype(jnp.bfloat16)
        return carry

    lax.fori_loop(0, sizes.structures, fill, 0)

    lines = pairs_ref.shape[0]
    half = lines // 2
    pairs = pairs_ref[...]
    group = modulo(pairs, groups)
    mine = modulo(group, sizes.plane) == here
    slot = jnp.where(mine, divide(group, sizes.plane) * sweeps + divide(pairs, groups), -1)
    other = sizes.at(pairs)
    slot_row = lax.broadcasted_iota(jnp.int32, (slots, 128), 0)
    before = lax.broadcasted_iota(jnp.int32, (128, 256), 0)
    after = lax.broadcasted_iota(jnp.int32, (128, 256), 1)
    count = (before <= after).astype(jnp.float32).astype(jnp.bfloat16)
    running = jnp.zeros((slots, 128), jnp.float32)
    picked = []
    for line in range(lines):
        chosen = (slot[line : line + 1] == slot_row).astype(jnp.float32)
        counted = jnp.dot(chosen.astype(jnp.bfloat16), count, preferred_element_type=jnp.float32)
        inner = jnp.sum(chosen * (counted[:, :128] - 1.0 + running), axis=0, keepdims=True)
        picked.append((chosen, inner))
        running = running + counted[:, 128:]
    doubled = 2.0 * jnp.floor(0.5 * (running + 1.0))
    lower = (
        lax.broadcasted_iota(jnp.int32, (slots, slots), 0) > lax.broadcasted_iota(jnp.int32, (slots, slots), 1)
    ).astype(jnp.float32)
    base = jnp.dot(lower, doubled, precision=lax.Precision.HIGHEST, preferred_element_type=jnp.float32)
    number = jnp.max(base + doubled).astype(jnp.int32)
    digit_row = lax.broadcasted_iota(jnp.int32, (POINT_ROWS, 128), 0)
    ranks = []
    for line in range(lines):
        chosen, inner = picked[line]
        rank = inner + jnp.sum(chosen * base, axis=0, keepdims=True)
        ranks.append(jnp.where(slot[line : line + 1] >= 0, rank.astype(jnp.int32), -1))
        opposite = (line + half) % lines
        partner = other[opposite : opposite + 1]
        digits = jnp.zeros((POINT_ROWS, 128), jnp.int32)
        for place, digit in enumerate(
            (partner & 31, partner >> 5, slot[line : line + 1], lane, line % half + 0 * lane, 1 + 0 * lane)
        ):
            digits = jnp.where(digit_row == place, digit, digits)
        digits_ref[line] = digits.astype(jnp.float32).astype(jnp.bfloat16)
    chunks = (list_ref.shape[0] - 8) // 2
    spot = lax.broadcasted_iota(jnp.int32, (128, 128), 0)

    def compact(chunk, carry):
        found = jnp.zeros((POINT_ROWS, 128), jnp.float32)
        for line in range(0, lines, 2):
            there = jnp.concatenate(
                [(ranks[line + i] == spot + chunk * 128).astype(jnp.float32).astype(jnp.bfloat16) for i in range(2)],
                axis=1,
            )
            found = found + lax.dot_general(
                jnp.concatenate([digits_ref[line], digits_ref[line + 1]], axis=1),
                there,
                (((1,), (1,)), ((), ())),
                preferred_element_type=jnp.float32,
            )
        found = found.astype(jnp.int32)
        at = found[2:3]
        code = found[0:1] + (found[1:2] << 5) + ((slots + at) << 12) + (at << 19)
        list_ref[pl.ds(chunk, 1), :] = jnp.where(found[5:6] > 0, code, slots << 19)
        list_ref[pl.ds(chunks + chunk, 1), :] = (
            sizes.plane * sweeps * 128 + found[3:4] + found[4:5] * 128
        )
        return carry

    lax.fori_loop(0, lax.div(number + 2 * UNIT - 1, 128) + 1, compact, 0)
    list_ref[2 * chunks : 2 * chunks + 8] = jnp.full((8, 128), number)


def tile_kernel(sizes, reach_ref, list_ref, listed_ref, first_ref, marks_ref, same_ref, across_ref, *refs):
    structures, sweeps, slots = sizes.structures, sizes.sweeps, sizes.slots
    out_refs = refs[:structures]
    second_ref, counts_ref, held_ref, sums_ref, picks_ref, diag_ref, total_ref = refs[structures:]
    row_here = lax.axis_index("row")
    column_here = lax.axis_index("col")
    family = lax.div(row_here, sizes.share)
    chip_here = lax.rem(row_here, sizes.share) * sizes.half + lax.div(column_here, 2)
    core_here = lax.rem(column_here, 2)
    lane = lax.broadcasted_iota(jnp.int32, (1, 128), 1)
    row = lax.broadcasted_iota(jnp.int32, (8, 128), 0)
    ones = jnp.where((row == 3) | (row == 4), 1.0, 0.0)

    for core, piece_ref in ((core_here, same_ref), (1 - core_here, across_ref)):
        for k in range(sizes.chips):
            chip = lax.rem(chip_here + (sizes.chips - k), sizes.chips)
            device = chip * 2 + core
            base = k * sizes.rows
            counts_ref[pl.ds(pl.multiple_of(device * sweeps, sweeps), sweeps), :] = piece_ref[
                base + slots * 4 : base + slots * 4 + sweeps
            ]
            for turn in range(structures):
                origin = lax.rem(family + (structures - turn), structures)
                at = (origin * sizes.plane + device) * sweeps
                for pair in range(sweeps // 2):
                    start = base + turn * sweeps * 4 + pair * 8
                    value = piece_ref[start : start + 8]
                    high = rounded(value)
                    low = value - high
                    high_turned = pltpu.roll(high, 4, 0)
                    even = jnp.concatenate(
                        [jnp.where(row < 4, high, pltpu.roll(low, 4, 0)), jnp.where(row < 3, high, ones)],
                        axis=0,
                    )
                    odd = jnp.concatenate(
                        [jnp.where(row < 4, high_turned, low), jnp.where(row < 3, high_turned, ones)],
                        axis=0,
                    )
                    second_ref[at + 2 * pair] = even.astype(jnp.bfloat16)
                    second_ref[at + 2 * pair + 1] = odd.astype(jnp.bfloat16)
    listed_base = sizes.plane * sweeps
    counts_ref[listed_base : listed_base + listed_ref.shape[0]] = listed_ref[...].astype(jnp.float32)

    total_ref[...] = jnp.zeros_like(total_ref)
    spare = 1.0 / (1.0 + jnp.exp(jnp.float32(-CONTACT_SHIFT)))

    here = lax.rem(row_here, sizes.share) * sizes.n_col + column_here
    groups = sizes.groups

    def step(ending, beginning):
        sums = sums_ref[pl.ds(0, UNIT, stride=8), :]
        for k in range(1, 8):
            sums = sums + sums_ref[pl.ds(k, UNIT, stride=8), :]
        chance = 64.0 * 128.0 + 0.5 * jnp.sum(sums, axis=1, keepdims=True)
        count = jnp.sum(picks_ref[...], axis=1, keepdims=True)
        chance = jnp.where(diag_ref[...] > 0.5, 0.5 * (chance - 128.0 * spare), chance)
        weight = 1.0 - count / (BACKGROUND + chance / 128.0)
        for t in range(0, UNIT, 2):
            left, right = (second_ref[ending[t + i] & 4095] for i in range(2))
            product = lax.dot_general(
                jnp.concatenate([left, right], axis=0),
                held_ref[t * 128 : (t + 2) * 128],
                (((1,), (1,)), ((), ())),
                preferred_element_type=jnp.float32,
            )
            for i in range(2):
                gain = product[i * POINT_ROWS : (i + 1) * POINT_ROWS, i * 128 : (i + 1) * 128]
                at = pl.multiple_of((ending[t + i] >> 19) * POINT_ROWS, POINT_ROWS)
                total_ref[pl.ds(at, POINT_ROWS), :] += weight[t + i : t + i + 1] * gain
        for t in range(0, UNIT, 2):
            seconds = [beginning[t + i][0] & 4095 for i in range(2)]
            logit = jnp.dot(
                first_ref[(beginning[t][0] >> 12) & 127],
                jnp.concatenate(
                    [jnp.concatenate([second_ref[at], marks_ref[at]], axis=0) for at in seconds], axis=1
                ),
                preferred_element_type=jnp.float32,
            )
            bend = jnp.tanh(logit)
            rest = 1.0 - bend * bend
            for i in range(2):
                part = bend[:, i * 128 : (i + 1) * 128]
                sums_ref[(t + i) * 8 : (t + i + 1) * 8] = jnp.sum(part.reshape(16, 8, 128), axis=0)
                held_ref[(t + i) * 128 : (t + i + 1) * 128] = rest[:, i * 128 : (i + 1) * 128].astype(
                    jnp.bfloat16
                )
                code, place, diagonal = beginning[t + i]
                picked = counts_ref[pl.ds(place >> 7, 1), :]
                picks_ref[t + i : t + i + 1] = jnp.where(lane == (place & 127), picked, 0.0)
                diag_ref[t + i : t + i + 1] = jnp.full((1, 128), diagonal)
        return tuple(code for code, _, _ in beginning)

    def band_step(turn, carry):
        slot, other, ending = carry
        beginning = []
        for _ in range(UNIT // 2):
            block = modulo(slot, sweeps) * groups + divide(slot, sweeps) * sizes.plane + here
            high = reach_ref[1, slot]
            for i in range(2):
                second = jnp.minimum(other + i, high)
                first = jnp.minimum(block, second)
                group = modulo(first, groups)
                line = modulo(group, sizes.plane) * sweeps + divide(first, groups)
                apart = jnp.abs(block - second)
                place = line * 128 + divide(group, sizes.plane) * sizes.width + apart
                total = jnp.where(other + i <= high, slot, slots)
                code = sizes.at(second) + (jnp.minimum(slot, slots - 1) << 12) + (total << 19)
                beginning.append((code, place, (apart == 0).astype(jnp.float32)))
            over = other + 2 > high
            slot = jnp.minimum(slot + over.astype(jnp.int32), slots)
            other = jnp.where(over, reach_ref[0, slot], other + 2)
        return slot, other, step(ending, beginning)

    def listed_step(turn, ending):
        beginning = []
        for t in range(UNIT):
            at = turn * UNIT + t
            beginning.append(
                (list_ref[at >> 7, at & 127], list_ref[chunks + (at >> 7), at & 127], jnp.float32(0.0))
            )
        return step(ending, beginning)

    chunks = (list_ref.shape[0] - 8) // 2
    idle = (jnp.int32(slots << 19),) * UNIT
    sums_ref[...] = jnp.zeros_like(sums_ref)
    carry = (jnp.int32(0), reach_ref[0, 0], idle)
    ending = lax.fori_loop(0, reach_ref[0, slots + 1], band_step, carry)[2]
    listed_steps = lax.div(list_ref[2 * chunks, 0] + UNIT - 1, UNIT)
    lax.fori_loop(0, listed_steps + 1, listed_step, ending)

    scale = -2.0 * CONTACT_SLOPE / 128.0 / 4.0
    for k in range(structures):
        origin = lax.rem(family + k, structures)
        turn = (structures - k) % structures
        first = origin * sweeps * POINT_ROWS
        mass = total_ref[pl.ds(first + 11, sweeps, stride=POINT_ROWS), :]
        for place in range(3):
            point = same_ref[pl.ds(turn * sweeps * 4 + place, sweeps, stride=4), :]
            high = rounded(point)
            near = high + rounded(point - high)
            pull = (
                total_ref[pl.ds(first + place, sweeps, stride=POINT_ROWS), :]
                + total_ref[pl.ds(first + place + 4, sweeps, stride=POINT_ROWS), :]
            )
            out_refs[k][place] = scale * (near * mass - pull)


def place_kernel(sizes, *refs):
    family = lax.div(lax.axis_index("row"), sizes.share)
    for k, ref in enumerate(refs[:-1]):
        refs[-1][lax.rem(family + (sizes.structures - k), sizes.structures)] = ref[...]


def on_device(n_row, n_col, coords, chrom_lengths, band_counts, inter_pairs, inter_counts):
    structures, _, sweeps, block_size = coords.shape
    width = band_counts.shape[3]
    band_reach = width - 1
    listed = inter_pairs.shape[1]
    sizes = Sizes(n_row, n_col, structures, sweeps, width)
    share, groups, slots, blocks = sizes.share, sizes.groups, sizes.slots, sizes.blocks
    row_here = lax.axis_index("row")
    column_here = lax.axis_index("col")
    member = row_here // share
    here = row_here % share * n_col + column_here

    messages = pl.pallas_call(
        functools.partial(pack_kernel, sizes),
        out_shape=[jax.ShapeDtypeStruct((5 * sweeps, block_size), jnp.float32)] * structures,
        in_specs=[VMEM, VMEM],
        out_specs=[VMEM] * structures,
        name="pack",
    )(coords, band_counts)
    deal = [
        [(i, (i // share + k) % structures * share + i % share) for i in range(n_row)]
        for k in range(structures)
    ]
    received = [messages[0]]
    for k in range(1, structures):
        received.append(lax.ppermute(messages[k], "row", deal[k]))
    own_row = pl.pallas_call(
        functools.partial(merge_kernel, 4 * sweeps),
        out_shape=jax.ShapeDtypeStruct((sizes.rows, block_size), jnp.float32),
        in_specs=[VMEM] * structures,
        out_specs=VMEM,
        name="merge",
    )(*received)

    def device(family, chip, core):
        row = family * share + chip // sizes.half
        return row * n_col + chip % sizes.half * 2 + core

    pieces = [own_row]
    for k in range(1, sizes.chips):
        moves = [
            (device(f, i, core), device(f, (i + k) % sizes.chips, core))
            for f in range(structures)
            for i in range(sizes.chips)
            for core in range(2)
        ]
        pieces.append(lax.ppermute(own_row, AXES, moves))
    same = pl.pallas_call(
        join_kernel,
        out_shape=jax.ShapeDtypeStruct((sizes.chips * sizes.rows, block_size), jnp.float32),
        in_specs=[VMEM] * sizes.chips,
        out_specs=VMEM,
        name="join",
    )(*pieces)
    across = lax.ppermute(same, "col", [(i, i ^ 1) for i in range(n_col)])

    chromosomes = chrom_lengths.shape[0]
    numbers = jnp.arange(chromosomes)
    ends = jnp.sum(jnp.where(numbers[None, :] <= numbers[:, None], chrom_lengths[None, :], 0), axis=1)
    starts = ends - chrom_lengths
    slot = jnp.arange(slots)
    block = slot % sweeps * groups + slot // sweeps * sizes.plane + here
    first_bead = block * block_size
    last_bead = first_bead + block_size - 1
    low = jnp.max(jnp.where(starts[None, :] <= first_bead[:, None], starts[None, :], 0), axis=1)
    high = jnp.min(
        jnp.where(ends[None, :] > last_bead[:, None], ends[None, :], blocks * block_size), axis=1
    )
    low = jnp.maximum(low // block_size, block - band_reach)
    high = jnp.minimum(jnp.minimum((high - 1) // block_size, block + band_reach), blocks - 1)
    steps = (jnp.sum((high - low + 2) // 2) + UNIT // 2 - 1) // (UNIT // 2)
    reach = jnp.stack(
        [
            jnp.concatenate([low, jnp.stack([jnp.zeros_like(steps), steps])]),
            jnp.concatenate([high, jnp.stack([jnp.zeros_like(steps), steps])]),
        ]
    ).astype(jnp.int32)
    pairs = jnp.transpose(lax.dynamic_index_in_dim(inter_pairs, member, 0, keepdims=False))
    pairs = pairs.reshape(2 * listed // block_size, block_size)
    labels = -(-chromosomes // 16) * 16
    depth = POINT_ROWS + labels
    chunks = -(-(2 * listed + slots + 2 * UNIT) // block_size)
    own, marks, tiles = pl.pallas_call(
        functools.partial(prepare_kernel, sizes),
        out_shape=[
            jax.ShapeDtypeStruct((2 * slots, block_size, depth), jnp.bfloat16),
            jax.ShapeDtypeStruct((blocks, labels, block_size), jnp.bfloat16),
            jax.ShapeDtypeStruct((2 * chunks + 8, block_size), jnp.int32),
        ],
        in_specs=[SMEM, VMEM, VMEM],
        out_specs=[VMEM] * 3,
        scratch_shapes=[
            pltpu.VMEM((labels, block_size), jnp.int32),
            pltpu.VMEM((labels, block_size), jnp.int32),
            pltpu.VMEM((2 * listed // block_size, POINT_ROWS, block_size), jnp.bfloat16),
        ],
        cost_estimate=pl.CostEstimate(flops=1 << 30, bytes_accessed=1 << 23, transcendentals=0),
        compiler_params=pltpu.CompilerParams(vmem_limit_bytes=24 * 1024 * 1024),
        name="prepare",
    )(chrom_lengths, pairs, own_row)

    counts = lax.dynamic_index_in_dim(inter_counts, member, 0, keepdims=False)
    counts = counts.reshape(listed // block_size, block_size)
    gains = pl.pallas_call(
        functools.partial(tile_kernel, sizes),
        out_shape=[jax.ShapeDtypeStruct((3, sweeps, block_size), jnp.float32)] * structures,
        in_specs=[SMEM] * 2 + [VMEM] * 5,
        out_specs=[VMEM] * structures,
        scratch_shapes=[
            pltpu.VMEM((blocks, POINT_ROWS, block_size), jnp.bfloat16),
            pltpu.VMEM((sizes.plane * sweeps + listed // block_size, block_size), jnp.float32),
            pltpu.VMEM((UNIT * block_size, block_size), jnp.bfloat16),
            pltpu.VMEM((UNIT * 8, block_size), jnp.float32),
            pltpu.VMEM((UNIT, block_size), jnp.float32),
            pltpu.VMEM((UNIT, block_size), jnp.float32),
            pltpu.VMEM(((slots + 1) * POINT_ROWS, block_size), jnp.float32),
        ],
        compiler_params=pltpu.CompilerParams(vmem_limit_bytes=40 * 1024 * 1024),
        name="tiles",
    )(reach, tiles, counts, own, marks, same, across)

    arrived = [gains[0]]
    for k in range(1, structures):
        arrived.append(lax.ppermute(gains[k], "row", deal[k]))
    return pl.pallas_call(
        functools.partial(place_kernel, sizes),
        out_shape=jax.ShapeDtypeStruct(coords.shape, jnp.float32),
        in_specs=[VMEM] * structures,
        out_specs=VMEM,
        name="place",
    )(*arrived)


def solution(mesh):
    placed = (
        P(None, None, None, ("row", "col")),
        P(),
        P(None, None, ("row", "col"), None),
        P(),
        P(),
    )
    return jax.shard_map(
        functools.partial(on_device, mesh.shape["row"], mesh.shape["col"]),
        mesh=mesh,
        in_specs=placed,
        out_specs=P(None, None, None, ("row", "col")),
        check_vma=False,
    )
```

profile of v0, /device:TPU:0, one launch (start us, length us, event | category | flops | bytes accessed | tf_op | source)
XLA Modules:
  0.0 68.7 jit_solution(5599881425895943981)
XLA Ops:
  0.0 0.0 copy-start
  0.0 1.6 %pack.1 = (f32[40,128]{1,0:T(8,128)}, f32[40,128]{1,0:T(8,128)}, f32[40,128]{1,0:T(8,128)}, f32[40,128]{1,0:T(8,128)}) custom-call(f32[4,3,8,128]{3,2,1,0:T(8,128)} %coords_ref.1, s32[4,8,1,32]{3,2,1,0:T(1,128)} %counts_ref.1), custom_call_target="tpu_custom_call" | custom-call | tf_op jit(solution)/shard_map/pack/pallas_call | solution.py:373
  1.6 3.0 %collective-permute-start = (f32[40,128]{1,0:T(8,128)}, f32[40,128]{1,0:T(8,128)S(1)}, u32[]{:S(2)}, u32[]{:S(2)}) collective-permute-start(f32[40,128]{1,0:T(8,128)} %get-tuple-element.17), channel_id=1, source_target_pairs={{0,8},{4,12},{8,16},{12,20},{16,24},{20,28},{24,0},{28,4},{1,9},{5... | collective-permute-start | bytes 61448 | tf_op jit(solution)/shard_map/ppermute | solution.py:386
  4.6 2.6 %collective-permute-start.1 = (f32[40,128]{1,0:T(8,128)}, f32[40,128]{1,0:T(8,128)S(1)}, u32[]{:S(2)}, u32[]{:S(2)}) collective-permute-start(f32[40,128]{1,0:T(8,128)} %get-tuple-element.18), channel_id=1, source_target_pairs={{0,16},{4,20},{8,24},{12,28},{16,0},{20,4},{24,8},{28,12},{1,17},{... | collective-permute-start | bytes 61448 | tf_op jit(solution)/shard_map/ppermute | solution.py:386
  7.2 1.3 %collective-permute-start.2 = (f32[40,128]{1,0:T(8,128)}, f32[40,128]{1,0:T(8,128)S(1)}, u32[]{:S(2)}, u32[]{:S(2)}) collective-permute-start(f32[40,128]{1,0:T(8,128)} %get-tuple-element.19), channel_id=1, source_target_pairs={{0,24},{4,28},{8,0},{12,4},{16,8},{20,12},{24,16},{28,20},{1,25},{... | collective-permute-start | bytes 61448 | tf_op jit(solution)/shard_map/ppermute | solution.py:386
  8.5 0.8 %select_reduce_fusion = s32[46]{0:T(128)S(1)} fusion(s32[46]{0:T(128)} %lengths_ref.1), kind=kLoop, calls=%fused_computation | loop fusion | flops 6302 | bytes 368 | tf_op jit(solution)/shard_map/reduce_sum | solution.py:419
  9.3 0.7 sub.43
  10.0 0.2 select_reduce_fusion.1
  10.2 0.2 select_reduce_fusion.2
  10.3 0.7 %fusion.6 = (s32[]{:T(128)}, s32[32]{0:T(128)S(1)}, s32[32]{0:T(128)S(1)}) fusion(s32[]{:T(128)S(6)} %add.89, s32[32]{0:T(128)S(1)} %select_reduce_fusion.2, s32[32]{0:T(128)S(1)} %select_reduce_fusion.1), kind=kLoop, calls=%fused_computation.31 | loop fusion | flops 2239 | bytes 520 | tf_op jit(solution)/shard_map/reduce_sum | solution.py:431
  11.1 0.0 copy-done
  11.8 0.0 collective-permute-done.refs_1_
  11.8 0.0 copy-start.8
  11.8 0.0 collective-permute-done.1.refs_2_
  11.8 0.0 copy-start.9
  11.8 0.0 collective-permute-done.2.refs_3_
  11.8 0.0 copy-start.10
  11.8 0.6 copy-done.8
  12.4 0.0 copy-done.9
  12.4 0.0 copy-done.10
  12.4 1.4 %merge.1.own_ref.refs_0_ = f32[136,128]{1,0:T(8,128)} custom-call(f32[40,128]{1,0:T(8,128)} %get-tuple-element.16.refs_0_, f32[40,128]{1,0:T(8,128)} %copy-done.8, f32[40,128]{1,0:T(8,128)} %copy-done.9, f32[40,128]{1,0:T(8,128)} %copy-done.10), custom_call_target="tpu_custom_call" | custom-call | tf_op jit(solution)/shard_map/merge/pallas_call | solution.py:387
  13.8 1.5 %collective-permute-start.3 = (f32[136,128]{1,0:T(8,128)}, f32[136,128]{1,0:T(8,128)S(1)}, u32[]{:S(2)}, u32[]{:S(2)}) collective-permute-start(f32[136,128]{1,0:T(8,128)} %merge.1.own_ref.refs_0_), channel_id=1, source_target_pairs={{0,2},{1,3},{2,4},{3,5},{4,6},{5,7},{6,0},{7,1},{8,10},{9,11},{10,... | collective-permute-start | bytes 208904 | tf_op jit(solution)/shard_map/ppermute | solution.py:407
  15.3 1.5 %collective-permute-start.4 = (f32[136,128]{1,0:T(8,128)}, f32[136,128]{1,0:T(8,128)S(1)}, u32[]{:S(2)}, u32[]{:S(2)}) collective-permute-start(f32[136,128]{1,0:T(8,128)} %merge.1.own_ref.refs_0_), channel_id=1, source_target_pairs={{0,4},{1,5},{2,6},{3,7},{4,0},{5,1},{6,2},{7,3},{8,12},{9,13},{10,... | collective-permute-start | bytes 208904 | tf_op jit(solution)/shard_map/ppermute | solution.py:407
  16.8 1.4 %collective-permute-start.5 = (f32[136,128]{1,0:T(8,128)}, f32[136,128]{1,0:T(8,128)S(1)}, u32[]{:S(2)}, u32[]{:S(2)}) collective-permute-start(f32[136,128]{1,0:T(8,128)} %merge.1.own_ref.refs_0_), channel_id=1, source_target_pairs={{0,6},{1,7},{2,0},{3,1},{4,2},{5,3},{6,4},{7,5},{8,14},{9,15},{10,... | collective-permute-start | bytes 208904 | tf_op jit(solution)/shard_map/ppermute | solution.py:407
  18.3 0.1 fusion.7
  18.3 1.3 %collective-permute-done.3.refs_1_ = f32[136,128]{1,0:T(8,128)S(1)} collective-permute-done((f32[136,128]{1,0:T(8,128)}, f32[136,128]{1,0:T(8,128)S(1)}, u32[]{:S(2)}, u32[]{:S(2)}) %collective-permute-start.3) | collective-permute-done | bytes 69664 | tf_op jit(solution)/shard_map/ppermute | solution.py:407
  19.6 0.0 copy-start.5
  19.6 0.6 collective-permute-done.4.refs_2_
  20.2 0.0 copy-start.6
  20.2 1.1 %collective-permute-done.5.refs_3_ = f32[136,128]{1,0:T(8,128)S(1)} collective-permute-done((f32[136,128]{1,0:T(8,128)}, f32[136,128]{1,0:T(8,128)S(1)}, u32[]{:S(2)}, u32[]{:S(2)}) %collective-permute-start.5) | collective-permute-done | bytes 69664 | tf_op jit(solution)/shard_map/ppermute | solution.py:407
  21.4 0.0 copy-done.5
  21.4 0.0 copy-done.6
  21.4 0.0 copy-start.7
  21.4 0.6 copy-done.7
  22.0 1.7 %join.1.same_ref = f32[544,128]{1,0:T(8,128)} custom-call(f32[136,128]{1,0:T(8,128)} %merge.1.own_ref.refs_0_, f32[136,128]{1,0:T(8,128)} %copy-done.5, f32[136,128]{1,0:T(8,128)} %copy-done.6, f32[136,128]{1,0:T(8,128)} %copy-done.7), custom_call_target="tpu_custom_call" | custom-call | tf_op jit(solution)/shard_map/join/pallas_call | solution.py:408
  23.7 0.0 copy-start.1
  23.7 0.0 collective-permute-start.6
  23.7 0.8 %constant_dynamic-slice_fusion = s32[1,1024]{1,0:T(1,128)S(1)} fusion(s32[4,1024]{1,0:T(4,128)} %param.9, s32[]{:T(128)S(6)} %select_n.76), kind=kLoop, calls=%fused_computation.34 | loop fusion | bytes 8196 | tf_op jit(solution)/shard_map/jit(dynamic_index_in_dim)/dynamic_slice | solution.py:462
  24.5 0.0 copy-start.2
  24.5 0.9 %copy-done.2 = f32[136,128]{1,0:T(8,128)S(1)} copy-done((f32[136,128]{1,0:T(8,128)S(1)}, f32[136,128]{1,0:T(8,128)}, u32[]{:S(2)}) %copy-start.2) | copy-done | bytes 69656
  25.4 0.0 copy-start.4
  25.4 0.7 copy-done.4
  26.0 3.9 %prepare.1 = (bf16[64,128,64]{2,1,0:T(8,128)(2,1)S(1)}, bf16[256,48,128]{2,1,0:T(8,128)(2,1)S(1)}, s32[42,128]{1,0:T(8,128)S(1)}) custom-call(s32[46]{0:T(128)S(1)} %copy-done.4, s32[16,128]{1,0:T(8,128)S(1)} %reshape.38.pairs_ref, f32[136,128]{1,0:T(8,128)S(1)} %copy-done.2), custom_call_target="tpu_custom_call" | custom-call | flops 1073741824 | bytes 8388608 | tf_op jit(solution)/shard_map/prepare/pallas_call | solution.py:443
  30.0 0.0 collective-permute-done.6.across_ref
  30.0 0.0 copy-done.1
  30.0 29.9 %tiles.1 = (f32[3,8,128]{2,1,0:T(8,128)S(1)}, f32[3,8,128]{2,1,0:T(8,128)S(1)}, f32[3,8,128]{2,1,0:T(8,128)S(1)}, f32[3,8,128]{2,1,0:T(8,128)S(1)}) custom-call(s32[2,34]{1,0:T(2,128)S(1)} %pad_add_fusion.reach_ref, s32[42,128]{1,0:T(8,128)S(1)} %get-tuple-element.20.list_ref, s32[8,128]{1,0:T(8,128)S(1)} %bitcast.10, ...), custom_call_target="tpu_custom_call" | custom-call | tf_op jit(solution)/shard_map/tiles/pallas_call | solution.py:464
  59.9 0.0 copy-start.3
  59.9 0.6 copy-done.3
  60.5 0.7 collective-permute-start.7
  61.2 1.8 %collective-permute-start.8 = (f32[3,8,128]{2,1,0:T(8,128)S(1)}, f32[3,8,128]{2,1,0:T(8,128)S(1)}, u32[]{:S(2)}, u32[]{:S(2)}) collective-permute-start(f32[3,8,128]{2,1,0:T(8,128)S(1)} %get-tuple-element.25), channel_id=1, source_target_pairs={{0,16},{4,20},{8,24},{12,28},{16,0},{20,4},{24,8},{28,12},{1,17},{... | collective-permute-start | bytes 36872 | tf_op jit(solution)/shard_map/ppermute | solution.py:484
  63.0 1.4 %collective-permute-start.9 = (f32[3,8,128]{2,1,0:T(8,128)S(1)}, f32[3,8,128]{2,1,0:T(8,128)S(1)}, u32[]{:S(2)}, u32[]{:S(2)}) collective-permute-start(f32[3,8,128]{2,1,0:T(8,128)S(1)} %get-tuple-element.26), channel_id=1, source_target_pairs={{0,24},{4,28},{8,0},{12,4},{16,8},{20,12},{24,16},{28,20},{1,25},{... | collective-permute-start | bytes 36872 | tf_op jit(solution)/shard_map/ppermute | solution.py:484
  64.4 1.7 %collective-permute-done.7.refs_1_ = f32[3,8,128]{2,1,0:T(8,128)S(1)} collective-permute-done((f32[3,8,128]{2,1,0:T(8,128)S(1)}, f32[3,8,128]{2,1,0:T(8,128)S(1)}, u32[]{:S(2)}, u32[]{:S(2)}) %collective-permute-start.7) | collective-permute-done | bytes 12320 | tf_op jit(solution)/shard_map/ppermute | solution.py:484
  66.0 0.0 copy-start.11
  66.0 0.0 collective-permute-done.8.refs_2_
  66.0 0.0 copy-start.12
  66.0 0.6 collective-permute-done.9.refs_3_
  66.7 0.0 copy-start.13
  66.7 0.0 copy-done.11
  66.7 0.0 copy-done.12
  66.7 0.6 copy-done.13
  67.3 1.4 %place.1 = f32[4,3,8,128]{3,2,1,0:T(8,128)} custom-call(f32[3,8,128]{2,1,0:T(8,128)} %copy-done.3, f32[3,8,128]{2,1,0:T(8,128)} %copy-done.11, f32[3,8,128]{2,1,0:T(8,128)} %copy-done.12, f32[3,8,128]{2,1,0:T(8,128)} %copy-done.13), custom_call_target="tpu_custom_call" | custom-call | tf_op jit(solution)/shard_map/place/pallas_call | solution.py:485
  (5 shorter events, 0.0 us)
Async XLA Ops:
  0.0 11.1 %copy-start = (s32[4,1024,2]{1,2,0:T(2,128)S(1)}, s32[4,1024,2]{1,2,0:T(2,128)}, u32[]{:S(2)}) copy-start(s32[4,1024,2]{1,2,0:T(2,128)} %param.8) | copy-start | bytes 98308
  1.6 10.2 %collective-permute-start = (f32[40,128]{1,0:T(8,128)}, f32[40,128]{1,0:T(8,128)S(1)}, u32[]{:S(2)}, u32[]{:S(2)}) collective-permute-start(f32[40,128]{1,0:T(8,128)} %get-tuple-element.17), channel_id=1, source_target_pairs={{0,8},{4,12},{8,16},{12,20},{16,24},{20,28},{24,0},{28,4},{1,9},{5... | collective-permute-start | bytes 61448 | tf_op jit(solution)/shard_map/ppermute | solution.py:386
  4.6 7.2 %collective-permute-start.1 = (f32[40,128]{1,0:T(8,128)}, f32[40,128]{1,0:T(8,128)S(1)}, u32[]{:S(2)}, u32[]{:S(2)}) collective-permute-start(f32[40,128]{1,0:T(8,128)} %get-tuple-element.18), channel_id=1, source_target_pairs={{0,16},{4,20},{8,24},{12,28},{16,0},{20,4},{24,8},{28,12},{1,17},{... | collective-permute-start | bytes 61448 | tf_op jit(solution)/shard_map/ppermute | solution.py:386
  7.2 4.6 %collective-permute-start.2 = (f32[40,128]{1,0:T(8,128)}, f32[40,128]{1,0:T(8,128)S(1)}, u32[]{:S(2)}, u32[]{:S(2)}) collective-permute-start(f32[40,128]{1,0:T(8,128)} %get-tuple-element.19), channel_id=1, source_target_pairs={{0,24},{4,28},{8,0},{12,4},{16,8},{20,12},{24,16},{28,20},{1,25},{... | collective-permute-start | bytes 61448 | tf_op jit(solution)/shard_map/ppermute | solution.py:386
  11.8 0.6 copy-start.8
  11.8 0.6 copy-start.9
  11.8 0.6 copy-start.10
  13.8 5.8 %collective-permute-start.3 = (f32[136,128]{1,0:T(8,128)}, f32[136,128]{1,0:T(8,128)S(1)}, u32[]{:S(2)}, u32[]{:S(2)}) collective-permute-start(f32[136,128]{1,0:T(8,128)} %merge.1.own_ref.refs_0_), channel_id=1, source_target_pairs={{0,2},{1,3},{2,4},{3,5},{4,6},{5,7},{6,0},{7,1},{8,10},{9,11},{10,... | collective-permute-start | bytes 208904 | tf_op jit(solution)/shard_map/ppermute | solution.py:407
  15.3 4.9 %collective-permute-start.4 = (f32[136,128]{1,0:T(8,128)}, f32[136,128]{1,0:T(8,128)S(1)}, u32[]{:S(2)}, u32[]{:S(2)}) collective-permute-start(f32[136,128]{1,0:T(8,128)} %merge.1.own_ref.refs_0_), channel_id=1, source_target_pairs={{0,4},{1,5},{2,6},{3,7},{4,0},{5,1},{6,2},{7,3},{8,12},{9,13},{10,... | collective-permute-start | bytes 208904 | tf_op jit(solution)/shard_map/ppermute | solution.py:407
  16.8 4.5 %collective-permute-start.5 = (f32[136,128]{1,0:T(8,128)}, f32[136,128]{1,0:T(8,128)S(1)}, u32[]{:S(2)}, u32[]{:S(2)}) collective-permute-start(f32[136,128]{1,0:T(8,128)} %merge.1.own_ref.refs_0_), channel_id=1, source_target_pairs={{0,6},{1,7},{2,0},{3,1},{4,2},{5,3},{6,4},{7,5},{8,14},{9,15},{10,... | collective-permute-start | bytes 208904 | tf_op jit(solution)/shard_map/ppermute | solution.py:407
  19.6 1.7 %copy-start.5 = (f32[136,128]{1,0:T(8,128)}, f32[136,128]{1,0:T(8,128)S(1)}, u32[]{:S(2)}) copy-start(f32[136,128]{1,0:T(8,128)S(1)} %collective-permute-done.3.refs_1_) | copy-start | bytes 208900
  20.2 1.1 %copy-start.6 = (f32[136,128]{1,0:T(8,128)}, f32[136,128]{1,0:T(8,128)S(1)}, u32[]{:S(2)}) copy-start(f32[136,128]{1,0:T(8,128)S(1)} %collective-permute-done.4.refs_2_) | copy-start | bytes 208900
  21.4 0.6 copy-start.7
  23.7 6.3 %copy-start.1 = (f32[544,128]{1,0:T(8,128)S(1)}, f32[544,128]{1,0:T(8,128)}, u32[]{:S(2)}) copy-start(f32[544,128]{1,0:T(8,128)} %join.1.same_ref) | copy-start | bytes 835588
  23.7 6.3 %collective-permute-start.6 = (f32[544,128]{1,0:T(8,128)}, f32[544,128]{1,0:T(8,128)S(1)}, u32[]{:S(2)}, u32[]{:S(2)}) collective-permute-start(f32[544,128]{1,0:T(8,128)} %join.1.same_ref), channel_id=1, source_target_pairs={{0,1},{1,0},{2,3},{3,2},{4,5},{5,4},{6,7},{7,6},{8,9},{9,8},{10,11... | collective-permute-start | bytes 835592 | tf_op jit(solution)/shard_map/ppermute | solution.py:415
  24.5 0.9 %copy-start.2 = (f32[136,128]{1,0:T(8,128)S(1)}, f32[136,128]{1,0:T(8,128)}, u32[]{:S(2)}) copy-start(f32[136,128]{1,0:T(8,128)} %merge.1.own_ref.refs_0_) | copy-start | bytes 208900
  25.4 0.7 copy-start.4
  59.9 0.6 copy-start.3
  60.5 5.5 %collective-permute-start.7 = (f32[3,8,128]{2,1,0:T(8,128)S(1)}, f32[3,8,128]{2,1,0:T(8,128)S(1)}, u32[]{:S(2)}, u32[]{:S(2)}) collective-permute-start(f32[3,8,128]{2,1,0:T(8,128)S(1)} %get-tuple-element.24), channel_id=1, source_target_pairs={{0,8},{4,12},{8,16},{12,20},{16,24},{20,28},{24,0},{28,4},{1,9},{5... | collective-permute-start | bytes 36872 | tf_op jit(solution)/shard_map/ppermute | solution.py:484
  61.2 4.8 %collective-permute-start.8 = (f32[3,8,128]{2,1,0:T(8,128)S(1)}, f32[3,8,128]{2,1,0:T(8,128)S(1)}, u32[]{:S(2)}, u32[]{:S(2)}) collective-permute-start(f32[3,8,128]{2,1,0:T(8,128)S(1)} %get-tuple-element.25), channel_id=1, source_target_pairs={{0,16},{4,20},{8,24},{12,28},{16,0},{20,4},{24,8},{28,12},{1,17},{... | collective-permute-start | bytes 36872 | tf_op jit(solution)/shard_map/ppermute | solution.py:484
  63.0 3.7 %collective-permute-start.9 = (f32[3,8,128]{2,1,0:T(8,128)S(1)}, f32[3,8,128]{2,1,0:T(8,128)S(1)}, u32[]{:S(2)}, u32[]{:S(2)}) collective-permute-start(f32[3,8,128]{2,1,0:T(8,128)S(1)} %get-tuple-element.26), channel_id=1, source_target_pairs={{0,24},{4,28},{8,0},{12,4},{16,8},{20,12},{24,16},{28,20},{1,25},{... | collective-permute-start | bytes 36872 | tf_op jit(solution)/shard_map/ppermute | solution.py:484
  66.0 0.7 copy-start.11
  66.0 0.7 copy-start.12
  66.7 0.6 copy-start.13
where the time goes:
time: 69.1 us; the launch traced here: 68.7 us
  Pallas kernels  39.9 us (58%)
  starting transfers between devices  15.2 us (22%)
  waiting for transfers between devices  5.33 us (8%)
  local copies, waits for them, and re-layouts  4.77 us (7%)
  other arithmetic  2.61 us (4%)
  between operations  0.79 us (1%)
    pallas_call x1, Pallas kernels, on_device(): pl.pallas_call(functools.partial(tile_kernel, sizes), out_shape=[jax.Shap...  29.9 us
    ppermute x3, starting transfers between devices, on_device(): received.append(lax.ppermute(messages[k], 'row', deal[k]))  6.96 us
    ppermute x3, starting transfers between devices, on_device(): pieces.append(lax.ppermute(own_row, AXES, moves))  4.44 us
    unnamed x28, local copies, waits for them, and re-layouts  3.98 us
    pallas_call x1, Pallas kernels, on_device(): pl.pallas_call(functools.partial(prepare_kernel, sizes), out_shape=[jax.S...  3.93 us
    ppermute x3, starting transfers between devices, on_device(): arrived.append(lax.ppermute(gains[k], 'row', deal[k]))  3.83 us
    ppermute x3, waiting for transfers between devices, on_device(): pieces.append(lax.ppermute(own_row, AXES, moves))  3 us
    ppermute x3, waiting for transfers between devices, on_device(): arrived.append(lax.ppermute(gains[k], 'row', deal[k]))  2.31 us
  transfers between devices with their start and end apart: 10, of which 5 were waited for; matrix products, arithmetic and copies ran while one was open for 5% of the time, Pallas kernels for 6%

commit v1 on v0

--- a/solution.py
+++ b/solution.py
@@ -11,7 +11,7 @@
 CONTACT_SLOPE = 0.5
 BACKGROUND = 0.5
 FAR = 32.0
-UNIT = 8
+UNIT = 16
 POINT_ROWS = 16
 AXES = ("row", "col")
 VMEM = pl.BlockSpec(memory_space=pltpu.VMEM)
@@ -92,11 +92,26 @@
 
     starts_ref[...] = jnp.zeros_like(starts_ref)
     ends_ref[...] = jnp.zeros_like(ends_ref)
+    slot_row = lax.broadcasted_iota(jnp.int32, (slots, 128), 0)
+    block = modulo(slot_row, sweeps) * groups + divide(slot_row, sweeps) * sizes.plane + here
+    first_bead = block * 128
+    low = jnp.zeros((slots, 128), jnp.int32)
+    high = jnp.full((slots, 128), sizes.blocks * 128)
     end = jnp.int32(0)
     for k in range(lengths_ref.shape[0]):
-        starts_ref[k : k + 1] = jnp.full((1, 128), end)
+        start = end
         end = end + lengths_ref[k]
+        starts_ref[k : k + 1] = jnp.full((1, 128), start)
         ends_ref[k : k + 1] = jnp.full((1, 128), end)
+        low = jnp.maximum(low, jnp.where(start <= first_bead, start, 0))
+        high = jnp.minimum(high, jnp.where(end > first_bead + 127, end, sizes.blocks * 128))
+
+    low = jnp.maximum(low >> 7, block - (sizes.width - 1))
+    high = jnp.minimum(jnp.minimum((high - 1) >> 7, block + (sizes.width - 1)), sizes.blocks - 1)
+    reach = []
+    for value in (low, high, (high - low + 2) >> 1):
+        reach.append(jnp.sum(jnp.where(slot_row == lane, value, 0), axis=0, keepdims=True))
+    steps = lax.div(jnp.sum(reach[2]) + (UNIT // 2 - 1), UNIT // 2)
 
     def mark(group, carry):
         for u in range(sweeps):
@@ -137,21 +152,25 @@
 
     lax.fori_loop(0, sizes.structures, fill, 0)
 
-    lines = pairs_ref.shape[0]
-    half = lines // 2
-    pairs = pairs_ref[...]
+    half = pairs_ref.shape[2] // 128
+    lines = 2 * half
+    pairs = pairs_ref[family]
     group = modulo(pairs, groups)
     mine = modulo(group, sizes.plane) == here
     slot = jnp.where(mine, divide(group, sizes.plane) * sweeps + divide(pairs, groups), -1)
     other = sizes.at(pairs)
-    slot_row = lax.broadcasted_iota(jnp.int32, (slots, 128), 0)
+
+    def cut(value, line):
+        side, at = line // half, line % half * 128
+        return value[side : side + 1, at : at + 128]
+
     before = lax.broadcasted_iota(jnp.int32, (128, 256), 0)
     after = lax.broadcasted_iota(jnp.int32, (128, 256), 1)
     count = (before <= after).astype(jnp.float32).astype(jnp.bfloat16)
     running = jnp.zeros((slots, 128), jnp.float32)
     picked = []
     for line in range(lines):
-        chosen = (slot[line : line + 1] == slot_row).astype(jnp.float32)
+        chosen = (cut(slot, line) == slot_row).astype(jnp.float32)
         counted = jnp.dot(chosen.astype(jnp.bfloat16), count, preferred_element_type=jnp.float32)
         inner = jnp.sum(chosen * (counted[:, :128] - 1.0 + running), axis=0, keepdims=True)
         picked.append((chosen, inner))
@@ -167,12 +186,12 @@
     for line in range(lines):
         chosen, inner = picked[line]
         rank = inner + jnp.sum(chosen * base, axis=0, keepdims=True)
-        ranks.append(jnp.where(slot[line : line + 1] >= 0, rank.astype(jnp.int32), -1))
+        ranks.append(jnp.where(cut(slot, line) >= 0, rank.astype(jnp.int32), -1))
         opposite = (line + half) % lines
-        partner = other[opposite : opposite + 1]
+        partner = cut(other, opposite)
         digits = jnp.zeros((POINT_ROWS, 128), jnp.int32)
         for place, digit in enumerate(
-            (partner & 31, partner >> 5, slot[line : line + 1], lane, line % half + 0 * lane, 1 + 0 * lane)
+            (partner & 31, partner >> 5, cut(slot, line), lane, line % half + 0 * lane, 1 + 0 * lane)
         ):
             digits = jnp.where(digit_row == place, digit, digits)
         digits_ref[line] = digits.astype(jnp.float32).astype(jnp.bfloat16)
@@ -202,10 +221,14 @@
         return carry
 
     lax.fori_loop(0, lax.div(number + 2 * UNIT - 1, 128) + 1, compact, 0)
-    list_ref[2 * chunks : 2 * chunks + 8] = jnp.full((8, 128), number)
-
-
-def tile_kernel(sizes, reach_ref, list_ref, listed_ref, first_ref, marks_ref, same_ref, across_ref, *refs):
+    end = 2 * chunks
+    list_ref[end : end + 1] = jnp.full((1, 128), number)
+    list_ref[end + 1 : end + 2] = reach[0]
+    list_ref[end + 2 : end + 3] = reach[1]
+    list_ref[end + 3 : end + 4] = jnp.full((1, 128), steps)
+
+
+def tile_kernel(sizes, list_ref, listed_ref, first_ref, marks_ref, same_ref, across_ref, *refs):
     structures, sweeps, slots = sizes.structures, sizes.sweeps, sizes.slots
     out_refs = refs[:structures]
     second_ref, counts_ref, held_ref, sums_ref, picks_ref, diag_ref, total_ref = refs[structures:]
@@ -246,7 +269,13 @@
                     second_ref[at + 2 * pair] = even.astype(jnp.bfloat16)
                     second_ref[at + 2 * pair + 1] = odd.astype(jnp.bfloat16)
     listed_base = sizes.plane * sweeps
-    counts_ref[listed_base : listed_base + listed_ref.shape[0]] = listed_ref[...].astype(jnp.float32)
+    chosen = lax.broadcasted_iota(jnp.int32, (structures, 128), 0) == family
+    for k in range(listed_ref.shape[1] // 128):
+        line = jnp.where(chosen, listed_ref[:, k * 128 : (k + 1) * 128], 0)
+        counts_ref[listed_base + k : listed_base + k + 1] = jnp.sum(line, axis=0, keepdims=True).astype(
+            jnp.float32
+        )
+    chunks = (list_ref.shape[0] - 8) // 2
 
     total_ref[...] = jnp.zeros_like(total_ref)
     spare = 1.0 / (1.0 + jnp.exp(jnp.float32(-CONTACT_SHIFT)))
@@ -302,7 +331,7 @@
         beginning = []
         for _ in range(UNIT // 2):
             block = modulo(slot, sweeps) * groups + divide(slot, sweeps) * sizes.plane + here
-            high = reach_ref[1, slot]
+            high = list_ref[2 * chunks + 2, slot]
             for i in range(2):
                 second = jnp.minimum(other + i, high)
                 first = jnp.minimum(block, second)
@@ -315,7 +344,7 @@
                 beginning.append((code, place, (apart == 0).astype(jnp.float32)))
             over = other + 2 > high
             slot = jnp.minimum(slot + over.astype(jnp.int32), slots)
-            other = jnp.where(over, reach_ref[0, slot], other + 2)
+            other = jnp.where(over, list_ref[2 * chunks + 1, slot], other + 2)
         return slot, other, step(ending, beginning)
 
     def listed_step(turn, ending):
@@ -327,11 +356,10 @@
             )
         return step(ending, beginning)
 
-    chunks = (list_ref.shape[0] - 8) // 2
     idle = (jnp.int32(slots << 19),) * UNIT
     sums_ref[...] = jnp.zeros_like(sums_ref)
-    carry = (jnp.int32(0), reach_ref[0, 0], idle)
-    ending = lax.fori_loop(0, reach_ref[0, slots + 1], band_step, carry)[2]
+    carry = (jnp.int32(0), list_ref[2 * chunks + 1, 0], idle)
+    ending = lax.fori_loop(0, list_ref[2 * chunks + 3, 0], band_step, carry)[2]
     listed_steps = lax.div(list_ref[2 * chunks, 0] + UNIT - 1, UNIT)
     lax.fori_loop(0, listed_steps + 1, listed_step, ending)
 
@@ -361,14 +389,9 @@
 def on_device(n_row, n_col, coords, chrom_lengths, band_counts, inter_pairs, inter_counts):
     structures, _, sweeps, block_size = coords.shape
     width = band_counts.shape[3]
-    band_reach = width - 1
     listed = inter_pairs.shape[1]
     sizes = Sizes(n_row, n_col, structures, sweeps, width)
-    share, groups, slots, blocks = sizes.share, sizes.groups, sizes.slots, sizes.blocks
-    row_here = lax.axis_index("row")
-    column_here = lax.axis_index("col")
-    member = row_here // share
-    here = row_here % share * n_col + column_here
+    share, slots, blocks = sizes.share, sizes.slots, sizes.blocks
 
     messages = pl.pallas_call(
         functools.partial(pack_kernel, sizes),
@@ -414,30 +437,7 @@
     )(*pieces)
     across = lax.ppermute(same, "col", [(i, i ^ 1) for i in range(n_col)])
 
-    chromosomes = chrom_lengths.shape[0]
-    numbers = jnp.arange(chromosomes)
-    ends = jnp.sum(jnp.where(numbers[None, :] <= numbers[:, None], chrom_lengths[None, :], 0), axis=1)
-    starts = ends - chrom_lengths
-    slot = jnp.arange(slots)
-    block = slot % sweeps * groups + slot // sweeps * sizes.plane + here
-    first_bead = block * block_size
-    last_bead = first_bead + block_size - 1
-    low = jnp.max(jnp.where(starts[None, :] <= first_bead[:, None], starts[None, :], 0), axis=1)
-    high = jnp.min(
-        jnp.where(ends[None, :] > last_bead[:, None], ends[None, :], blocks * block_size), axis=1
-    )
-    low = jnp.maximum(low // block_size, block - band_reach)
-    high = jnp.minimum(jnp.minimum((high - 1) // block_size, block + band_reach), blocks - 1)
-    steps = (jnp.sum((high - low + 2) // 2) + UNIT // 2 - 1) // (UNIT // 2)
-    reach = jnp.stack(
-        [
-            jnp.concatenate([low, jnp.stack([jnp.zeros_like(steps), steps])]),
-            jnp.concatenate([high, jnp.stack([jnp.zeros_like(steps), steps])]),
-        ]
-    ).astype(jnp.int32)
-    pairs = jnp.transpose(lax.dynamic_index_in_dim(inter_pairs, member, 0, keepdims=False))
-    pairs = pairs.reshape(2 * listed // block_size, block_size)
-    labels = -(-chromosomes // 16) * 16
+    labels = -(-chrom_lengths.shape[0] // 16) * 16
     depth = POINT_ROWS + labels
     chunks = -(-(2 * listed + slots + 2 * UNIT) // block_size)
     own, marks, tiles = pl.pallas_call(
@@ -457,14 +457,12 @@
         cost_estimate=pl.CostEstimate(flops=1 << 30, bytes_accessed=1 << 23, transcendentals=0),
         compiler_params=pltpu.CompilerParams(vmem_limit_bytes=24 * 1024 * 1024),
         name="prepare",
-    )(chrom_lengths, pairs, own_row)
-
-    counts = lax.dynamic_index_in_dim(inter_counts, member, 0, keepdims=False)
-    counts = counts.reshape(listed // block_size, block_size)
+    )(chrom_lengths, jnp.transpose(inter_pairs, (0, 2, 1)), own_row)
+
     gains = pl.pallas_call(
         functools.partial(tile_kernel, sizes),
         out_shape=[jax.ShapeDtypeStruct((3, sweeps, block_size), jnp.float32)] * structures,
-        in_specs=[SMEM] * 2 + [VMEM] * 5,
+        in_specs=[SMEM] + [VMEM] * 5,
         out_specs=[VMEM] * structures,
         scratch_shapes=[
             pltpu.VMEM((blocks, POINT_ROWS, block_size), jnp.bfloat16),
@@ -477,7 +475,7 @@
         ],
         compiler_params=pltpu.CompilerParams(vmem_limit_bytes=40 * 1024 * 1024),
         name="tiles",
-    )(reach, tiles, counts, own, marks, same, across)
+    )(tiles, inter_counts, own, marks, same, across)
 
     arrived = [gains[0]]
     for k in range(1, structures):

time: 69.1 us -> 64.7 us (0.936)
  Pallas kernels: 39.9 us -> 35.9 us
  waiting for transfers between devices: 5.33 us -> 7.95 us
  other arithmetic: 2.61 us -> 0 us
  between operations: 0.79 us -> 0.07 us
    pallas_call x1, Pallas kernels: 29.9 us -> 25.6 us  [on_device(): pl.pallas_call(functools.partial(tile_kernel, sizes), out_shape=[jax.Shap...]
    ppermute x3, waiting for transfers between devices: 0.01 us -> 2.64 us  [on_device(): received.append(lax.ppermute(messages[k], 'row', deal[k]))]
    reduce_sum x2 -> x0, other arithmetic: 1.48 us -> none  [the longest x1 0.76 us: on_device(): jnp.sum(jnp.where(numbers[None, :] <= numbers[:, None], chrom_lengths[Non...]
    unnamed x28 -> x30, local copies, waits for them, and re-layouts: 3.98 us -> 4.77 us
    dynamic_slice x1 -> x0, local copies, waits for them, and re-layouts: 0.77 us -> none  [on_device(): counts = lax.dynamic_index_in_dim(inter_counts, member, 0, keepdims=False)]
  transfers between devices with their start and end apart: 10 -> 10, of which waited for: 5 -> 8; matrix products, arithmetic and copies ran while one was open for 5% -> 0% of each run, Pallas kernels for 6% -> 7%
where the time goes in v1:
time: 64.7 us; the launch traced here: 63.9 us
  Pallas kernels  35.9 us (55%)
  starting transfers between devices  15.2 us (23%)
  waiting for transfers between devices  7.95 us (12%)
  local copies, waits for them, and re-layouts  4.77 us (7%)
    pallas_call x1, Pallas kernels, on_device(): pl.pallas_call(functools.partial(tile_kernel, sizes), out_shape=[jax.Shap...  25.6 us
    ppermute x3, starting transfers between devices, on_device(): received.append(lax.ppermute(messages[k], 'row', deal[k]))  6.96 us
    unnamed x30, local copies, waits for them, and re-layouts  4.77 us
    ppermute x3, starting transfers between devices, on_device(): pieces.append(lax.ppermute(own_row, AXES, moves))  4.44 us
    pallas_call x1, Pallas kernels, on_device(): pl.pallas_call(functools.partial(prepare_kernel, sizes), out_shape=[jax.S...  4.26 us
    ppermute x3, starting transfers between devices, on_device(): arrived.append(lax.ppermute(gains[k], 'row', deal[k]))  3.83 us
    ppermute x3, waiting for transfers between devices, on_device(): pieces.append(lax.ppermute(own_row, AXES, moves))  3.08 us
    ppermute x3, waiting for transfers between devices, on_device(): received.append(lax.ppermute(messages[k], 'row', deal[k]))  2.64 us
  transfers between devices with their start and end apart: 10, of which 8 were waited for; matrix products, arithmetic and copies ran while one was open for 0% of the time, Pallas kernels for 7%

profile of v1, /device:TPU:0, one launch (start us, length us, event | category | flops | bytes accessed | tf_op | source)
XLA Modules:
  0.0 63.9 jit_solution(11313034088580800655)
XLA Ops:
  0.0 0.0 copy-start.2
  0.0 1.6 %pack.1 = (f32[40,128]{1,0:T(8,128)}, f32[40,128]{1,0:T(8,128)}, f32[40,128]{1,0:T(8,128)}, f32[40,128]{1,0:T(8,128)}) custom-call(f32[4,3,8,128]{3,2,1,0:T(8,128)} %coords_ref.1, s32[4,8,1,32]{3,2,1,0:T(1,128)} %counts_ref.1), custom_call_target="tpu_custom_call" | custom-call | tf_op jit(solution)/shard_map/pack/pallas_call | solution.py:396
  1.6 3.0 %collective-permute-start = (f32[40,128]{1,0:T(8,128)}, f32[40,128]{1,0:T(8,128)S(1)}, u32[]{:S(2)}, u32[]{:S(2)}) collective-permute-start(f32[40,128]{1,0:T(8,128)} %get-tuple-element.17), channel_id=1, source_target_pairs={{0,8},{4,12},{8,16},{12,20},{16,24},{20,28},{24,0},{28,4},{1,9},{5... | collective-permute-start | bytes 61448 | tf_op jit(solution)/shard_map/ppermute | solution.py:409
  4.6 2.6 %collective-permute-start.1 = (f32[40,128]{1,0:T(8,128)}, f32[40,128]{1,0:T(8,128)S(1)}, u32[]{:S(2)}, u32[]{:S(2)}) collective-permute-start(f32[40,128]{1,0:T(8,128)} %get-tuple-element.18), channel_id=1, source_target_pairs={{0,16},{4,20},{8,24},{12,28},{16,0},{20,4},{24,8},{28,12},{1,17},{... | collective-permute-start | bytes 61448 | tf_op jit(solution)/shard_map/ppermute | solution.py:409
  7.2 1.3 %collective-permute-start.2 = (f32[40,128]{1,0:T(8,128)}, f32[40,128]{1,0:T(8,128)S(1)}, u32[]{:S(2)}, u32[]{:S(2)}) collective-permute-start(f32[40,128]{1,0:T(8,128)} %get-tuple-element.19), channel_id=1, source_target_pairs={{0,24},{4,28},{8,0},{12,4},{16,8},{20,12},{24,16},{28,20},{1,25},{... | collective-permute-start | bytes 61448 | tf_op jit(solution)/shard_map/ppermute | solution.py:409
  8.5 0.1 collective-permute-done.refs_1_
  8.6 0.0 copy-start.9
  8.6 1.0 %collective-permute-done.1.refs_2_ = f32[40,128]{1,0:T(8,128)S(1)} collective-permute-done((f32[40,128]{1,0:T(8,128)}, f32[40,128]{1,0:T(8,128)S(1)}, u32[]{:S(2)}, u32[]{:S(2)}) %collective-permute-start.1) | collective-permute-done | bytes 20512 | tf_op jit(solution)/shard_map/ppermute | solution.py:409
  9.6 0.0 copy-start.10
  9.6 1.5 %collective-permute-done.2.refs_3_ = f32[40,128]{1,0:T(8,128)S(1)} collective-permute-done((f32[40,128]{1,0:T(8,128)}, f32[40,128]{1,0:T(8,128)S(1)}, u32[]{:S(2)}, u32[]{:S(2)}) %collective-permute-start.2) | collective-permute-done | bytes 20512 | tf_op jit(solution)/shard_map/ppermute | solution.py:409
  11.2 0.0 copy-start.11
  11.2 0.0 copy-done.9
  11.2 0.0 copy-done.10
  11.2 0.6 copy-done.11
  11.8 1.4 %merge.1.own_ref.refs_0_ = f32[136,128]{1,0:T(8,128)} custom-call(f32[40,128]{1,0:T(8,128)} %get-tuple-element.16.refs_0_, f32[40,128]{1,0:T(8,128)} %copy-done.9, f32[40,128]{1,0:T(8,128)} %copy-done.10, f32[40,128]{1,0:T(8,128)} %copy-done.11), custom_call_target="tpu_custom_call" | custom-call | tf_op jit(solution)/shard_map/merge/pallas_call | solution.py:410
  13.2 1.5 %collective-permute-start.3 = (f32[136,128]{1,0:T(8,128)}, f32[136,128]{1,0:T(8,128)S(1)}, u32[]{:S(2)}, u32[]{:S(2)}) collective-permute-start(f32[136,128]{1,0:T(8,128)} %merge.1.own_ref.refs_0_), channel_id=1, source_target_pairs={{0,2},{1,3},{2,4},{3,5},{4,6},{5,7},{6,0},{7,1},{8,10},{9,11},{10,... | collective-permute-start | bytes 208904 | tf_op jit(solution)/shard_map/ppermute | solution.py:430
  14.7 1.5 %collective-permute-start.4 = (f32[136,128]{1,0:T(8,128)}, f32[136,128]{1,0:T(8,128)S(1)}, u32[]{:S(2)}, u32[]{:S(2)}) collective-permute-start(f32[136,128]{1,0:T(8,128)} %merge.1.own_ref.refs_0_), channel_id=1, source_target_pairs={{0,4},{1,5},{2,6},{3,7},{4,0},{5,1},{6,2},{7,3},{8,12},{9,13},{10,... | collective-permute-start | bytes 208904 | tf_op jit(solution)/shard_map/ppermute | solution.py:430
  16.2 1.4 %collective-permute-start.5 = (f32[136,128]{1,0:T(8,128)}, f32[136,128]{1,0:T(8,128)S(1)}, u32[]{:S(2)}, u32[]{:S(2)}) collective-permute-start(f32[136,128]{1,0:T(8,128)} %merge.1.own_ref.refs_0_), channel_id=1, source_target_pairs={{0,6},{1,7},{2,0},{3,1},{4,2},{5,3},{6,4},{7,5},{8,14},{9,15},{10,... | collective-permute-start | bytes 208904 | tf_op jit(solution)/shard_map/ppermute | solution.py:430
  17.6 1.0 %collective-permute-done.3.refs_1_ = f32[136,128]{1,0:T(8,128)S(1)} collective-permute-done((f32[136,128]{1,0:T(8,128)}, f32[136,128]{1,0:T(8,128)S(1)}, u32[]{:S(2)}, u32[]{:S(2)}) %collective-permute-start.3) | collective-permute-done | bytes 69664 | tf_op jit(solution)/shard_map/ppermute | solution.py:430
  18.6 0.0 copy-start.6
  18.6 0.7 %collective-permute-done.4.refs_2_ = f32[136,128]{1,0:T(8,128)S(1)} collective-permute-done((f32[136,128]{1,0:T(8,128)}, f32[136,128]{1,0:T(8,128)S(1)}, u32[]{:S(2)}, u32[]{:S(2)}) %collective-permute-start.4) | collective-permute-done | bytes 69664 | tf_op jit(solution)/shard_map/ppermute | solution.py:430
  19.3 0.0 copy-start.7
  19.3 1.4 %collective-permute-done.5.refs_3_ = f32[136,128]{1,0:T(8,128)S(1)} collective-permute-done((f32[136,128]{1,0:T(8,128)}, f32[136,128]{1,0:T(8,128)S(1)}, u32[]{:S(2)}, u32[]{:S(2)}) %collective-permute-start.5) | collective-permute-done | bytes 69664 | tf_op jit(solution)/shard_map/ppermute | solution.py:430
  20.7 0.0 copy-done.6
  20.7 0.0 copy-done.7
  20.7 0.0 copy-start.8
  20.7 0.6 copy-done.8
  21.3 1.7 %join.1.same_ref = f32[544,128]{1,0:T(8,128)} custom-call(f32[136,128]{1,0:T(8,128)} %merge.1.own_ref.refs_0_, f32[136,128]{1,0:T(8,128)} %copy-done.6, f32[136,128]{1,0:T(8,128)} %copy-done.7, f32[136,128]{1,0:T(8,128)} %copy-done.8), custom_call_target="tpu_custom_call" | custom-call | tf_op jit(solution)/shard_map/join/pallas_call | solution.py:431
  23.1 0.0 copy-start
  23.1 0.0 collective-permute-start.6
  23.1 0.0 copy-start.1
  23.1 0.9 %copy-done.1 = f32[136,128]{1,0:T(8,128)S(1)} copy-done((f32[136,128]{1,0:T(8,128)S(1)}, f32[136,128]{1,0:T(8,128)}, u32[]{:S(2)}) %copy-start.1) | copy-done | bytes 69656
  24.0 0.0 copy-start.4
  24.0 0.8 %copy-done.4 = s32[4,1024,2]{1,2,0:T(2,128)S(1)} copy-done((s32[4,1024,2]{1,2,0:T(2,128)S(1)}, s32[4,1024,2]{1,2,0:T(2,128)}, u32[]{:S(2)}) %copy-start.4) | copy-done | bytes 32792
  24.7 0.0 copy-start.5
  24.7 0.7 %copy-done.5 = s32[46]{0:T(128)S(1)} copy-done((s32[46]{0:T(128)S(1)}, s32[46]{0:T(128)}, u32[]{:S(2)}) %copy-start.5) | copy-done | bytes 208
  25.4 4.3 %prepare.1 = (bf16[64,128,64]{2,1,0:T(8,128)(2,1)S(1)}, bf16[256,48,128]{2,1,0:T(8,128)(2,1)S(1)}, s32[42,128]{1,0:T(8,128)S(1)}) custom-call(s32[46]{0:T(128)S(1)} %copy-done.5, s32[4,2,1024]{2,1,0:T(2,128)S(1)} %bitcast.1, f32[136,128]{1,0:T(8,128)S(1)} %copy-done.1), custom_call_target="tpu_custom_call" | custom-call | flops 1073741824 | bytes 8388608 | tf_op jit(solution)/shard_map/prepare/pallas_call | solution.py:443
  29.7 0.0 collective-permute-done.6.across_ref
  29.7 0.0 copy-done.2
  29.7 0.0 copy-done
  29.7 25.6 %tiles.1 = (f32[3,8,128]{2,1,0:T(8,128)S(1)}, f32[3,8,128]{2,1,0:T(8,128)S(1)}, f32[3,8,128]{2,1,0:T(8,128)S(1)}, f32[3,8,128]{2,1,0:T(8,128)S(1)}) custom-call(s32[42,128]{1,0:T(8,128)S(1)} %get-tuple-element.20.list_ref, s32[4,1024]{1,0:T(4,128)S(1)} %copy-done.2, bf16[64,128,64]{2,1,0:T(8,128)(2,1)S(1)} %get-tuple-element.21.first_ref, ...), custom_call_target="tpu_custom_call" | custom-call | tf_op jit(solution)/shard_map/tiles/pallas_call | solution.py:462
  55.3 0.0 copy-start.3
  55.3 0.6 copy-done.3
  55.9 0.2 collective-permute-start.7
  56.1 2.0 %collective-permute-start.8 = (f32[3,8,128]{2,1,0:T(8,128)S(1)}, f32[3,8,128]{2,1,0:T(8,128)S(1)}, u32[]{:S(2)}, u32[]{:S(2)}) collective-permute-start(f32[3,8,128]{2,1,0:T(8,128)S(1)} %get-tuple-element.25), channel_id=1, source_target_pairs={{0,16},{4,20},{8,24},{12,28},{16,0},{20,4},{24,8},{28,12},{1,17},{... | collective-permute-start | bytes 36872 | tf_op jit(solution)/shard_map/ppermute | solution.py:482
  58.1 1.6 %collective-permute-start.9 = (f32[3,8,128]{2,1,0:T(8,128)S(1)}, f32[3,8,128]{2,1,0:T(8,128)S(1)}, u32[]{:S(2)}, u32[]{:S(2)}) collective-permute-start(f32[3,8,128]{2,1,0:T(8,128)S(1)} %get-tuple-element.26), channel_id=1, source_target_pairs={{0,24},{4,28},{8,0},{12,4},{16,8},{20,12},{24,16},{28,20},{1,25},{... | collective-permute-start | bytes 36872 | tf_op jit(solution)/shard_map/ppermute | solution.py:482
  59.7 1.7 %collective-permute-done.7.refs_1_ = f32[3,8,128]{2,1,0:T(8,128)S(1)} collective-permute-done((f32[3,8,128]{2,1,0:T(8,128)S(1)}, f32[3,8,128]{2,1,0:T(8,128)S(1)}, u32[]{:S(2)}, u32[]{:S(2)}) %collective-permute-start.7) | collective-permute-done | bytes 12320 | tf_op jit(solution)/shard_map/ppermute | solution.py:482
  61.4 0.0 copy-start.12
  61.4 0.0 collective-permute-done.8.refs_2_
  61.4 0.0 copy-start.13
  61.4 0.6 collective-permute-done.9.refs_3_
  62.0 0.0 copy-start.14
  62.0 0.0 copy-done.12
  62.0 0.0 copy-done.13
  62.0 0.6 copy-done.14
  62.5 1.4 %place.1 = f32[4,3,8,128]{3,2,1,0:T(8,128)} custom-call(f32[3,8,128]{2,1,0:T(8,128)} %copy-done.3, f32[3,8,128]{2,1,0:T(8,128)} %copy-done.12, f32[3,8,128]{2,1,0:T(8,128)} %copy-done.13, f32[3,8,128]{2,1,0:T(8,128)} %copy-done.14), custom_call_target="tpu_custom_call" | custom-call | tf_op jit(solution)/shard_map/place/pallas_call | solution.py:483
Async XLA Ops:
  0.0 29.7 %copy-start.2 = (s32[4,1024]{1,0:T(4,128)S(1)}, s32[4,1024]{1,0:T(4,128)}, u32[]{:S(2)}) copy-start(s32[4,1024]{1,0:T(4,128)} %listed_ref.1) | copy-start | bytes 49156
  1.6 7.0 %collective-permute-start = (f32[40,128]{1,0:T(8,128)}, f32[40,128]{1,0:T(8,128)S(1)}, u32[]{:S(2)}, u32[]{:S(2)}) collective-permute-start(f32[40,128]{1,0:T(8,128)} %get-tuple-element.17), channel_id=1, source_target_pairs={{0,8},{4,12},{8,16},{12,20},{16,24},{20,28},{24,0},{28,4},{1,9},{5... | collective-permute-start | bytes 61448 | tf_op jit(solution)/shard_map/ppermute | solution.py:409
  4.6 5.0 %collective-permute-start.1 = (f32[40,128]{1,0:T(8,128)}, f32[40,128]{1,0:T(8,128)S(1)}, u32[]{:S(2)}, u32[]{:S(2)}) collective-permute-start(f32[40,128]{1,0:T(8,128)} %get-tuple-element.18), channel_id=1, source_target_pairs={{0,16},{4,20},{8,24},{12,28},{16,0},{20,4},{24,8},{28,12},{1,17},{... | collective-permute-start | bytes 61448 | tf_op jit(solution)/shard_map/ppermute | solution.py:409
  7.2 4.0 %collective-permute-start.2 = (f32[40,128]{1,0:T(8,128)}, f32[40,128]{1,0:T(8,128)S(1)}, u32[]{:S(2)}, u32[]{:S(2)}) collective-permute-start(f32[40,128]{1,0:T(8,128)} %get-tuple-element.19), channel_id=1, source_target_pairs={{0,24},{4,28},{8,0},{12,4},{16,8},{20,12},{24,16},{28,20},{1,25},{... | collective-permute-start | bytes 61448 | tf_op jit(solution)/shard_map/ppermute | solution.py:409
  8.6 2.6 %copy-start.9 = (f32[40,128]{1,0:T(8,128)}, f32[40,128]{1,0:T(8,128)S(1)}, u32[]{:S(2)}) copy-start(f32[40,128]{1,0:T(8,128)S(1)} %collective-permute-done.refs_1_) | copy-start | bytes 61444
  9.6 1.6 %copy-start.10 = (f32[40,128]{1,0:T(8,128)}, f32[40,128]{1,0:T(8,128)S(1)}, u32[]{:S(2)}) copy-start(f32[40,128]{1,0:T(8,128)S(1)} %collective-permute-done.1.refs_2_) | copy-start | bytes 61444
  11.2 0.6 copy-start.11
  13.2 5.4 %collective-permute-start.3 = (f32[136,128]{1,0:T(8,128)}, f32[136,128]{1,0:T(8,128)S(1)}, u32[]{:S(2)}, u32[]{:S(2)}) collective-permute-start(f32[136,128]{1,0:T(8,128)} %merge.1.own_ref.refs_0_), channel_id=1, source_target_pairs={{0,2},{1,3},{2,4},{3,5},{4,6},{5,7},{6,0},{7,1},{8,10},{9,11},{10,... | collective-permute-start | bytes 208904 | tf_op jit(solution)/shard_map/ppermute | solution.py:430
  14.7 4.7 %collective-permute-start.4 = (f32[136,128]{1,0:T(8,128)}, f32[136,128]{1,0:T(8,128)S(1)}, u32[]{:S(2)}, u32[]{:S(2)}) collective-permute-start(f32[136,128]{1,0:T(8,128)} %merge.1.own_ref.refs_0_), channel_id=1, source_target_pairs={{0,4},{1,5},{2,6},{3,7},{4,0},{5,1},{6,2},{7,3},{8,12},{9,13},{10,... | collective-permute-start | bytes 208904 | tf_op jit(solution)/shard_map/ppermute | solution.py:430
  16.2 4.5 %collective-permute-start.5 = (f32[136,128]{1,0:T(8,128)}, f32[136,128]{1,0:T(8,128)S(1)}, u32[]{:S(2)}, u32[]{:S(2)}) collective-permute-start(f32[136,128]{1,0:T(8,128)} %merge.1.own_ref.refs_0_), channel_id=1, source_target_pairs={{0,6},{1,7},{2,0},{3,1},{4,2},{5,3},{6,4},{7,5},{8,14},{9,15},{10,... | collective-permute-start | bytes 208904 | tf_op jit(solution)/shard_map/ppermute | solution.py:430
  18.6 2.1 %copy-start.6 = (f32[136,128]{1,0:T(8,128)}, f32[136,128]{1,0:T(8,128)S(1)}, u32[]{:S(2)}) copy-start(f32[136,128]{1,0:T(8,128)S(1)} %collective-permute-done.3.refs_1_) | copy-start | bytes 208900
  19.3 1.4 %copy-start.7 = (f32[136,128]{1,0:T(8,128)}, f32[136,128]{1,0:T(8,128)S(1)}, u32[]{:S(2)}) copy-start(f32[136,128]{1,0:T(8,128)S(1)} %collective-permute-done.4.refs_2_) | copy-start | bytes 208900
  20.7 0.6 copy-start.8
  23.1 6.6 %copy-start = (f32[544,128]{1,0:T(8,128)S(1)}, f32[544,128]{1,0:T(8,128)}, u32[]{:S(2)}) copy-start(f32[544,128]{1,0:T(8,128)} %join.1.same_ref) | copy-start | bytes 835588
  23.1 6.6 %collective-permute-start.6 = (f32[544,128]{1,0:T(8,128)}, f32[544,128]{1,0:T(8,128)S(1)}, u32[]{:S(2)}, u32[]{:S(2)}) collective-permute-start(f32[544,128]{1,0:T(8,128)} %join.1.same_ref), channel_id=1, source_target_pairs={{0,1},{1,0},{2,3},{3,2},{4,5},{5,4},{6,7},{7,6},{8,9},{9,8},{10,11... | collective-permute-start | bytes 835592 | tf_op jit(solution)/shard_map/ppermute | solution.py:438
  23.1 0.9 %copy-start.1 = (f32[136,128]{1,0:T(8,128)S(1)}, f32[136,128]{1,0:T(8,128)}, u32[]{:S(2)}) copy-start(f32[136,128]{1,0:T(8,128)} %merge.1.own_ref.refs_0_) | copy-start | bytes 208900
  24.0 0.8 %copy-start.4 = (s32[4,1024,2]{1,2,0:T(2,128)S(1)}, s32[4,1024,2]{1,2,0:T(2,128)}, u32[]{:S(2)}) copy-start(s32[4,1024,2]{1,2,0:T(2,128)} %param.8) | copy-start | bytes 98308
  24.7 0.7 %copy-start.5 = (s32[46]{0:T(128)S(1)}, s32[46]{0:T(128)}, u32[]{:S(2)}) copy-start(s32[46]{0:T(128)} %lengths_ref.1) | copy-start | bytes 556
  55.3 0.6 copy-start.3
  55.9 5.5 %collective-permute-start.7 = (f32[3,8,128]{2,1,0:T(8,128)S(1)}, f32[3,8,128]{2,1,0:T(8,128)S(1)}, u32[]{:S(2)}, u32[]{:S(2)}) collective-permute-start(f32[3,8,128]{2,1,0:T(8,128)S(1)} %get-tuple-element.24), channel_id=1, source_target_pairs={{0,8},{4,12},{8,16},{12,20},{16,24},{20,28},{24,0},{28,4},{1,9},{5... | collective-permute-start | bytes 36872 | tf_op jit(solution)/shard_map/ppermute | solution.py:482
  56.1 5.3 %collective-permute-start.8 = (f32[3,8,128]{2,1,0:T(8,128)S(1)}, f32[3,8,128]{2,1,0:T(8,128)S(1)}, u32[]{:S(2)}, u32[]{:S(2)}) collective-permute-start(f32[3,8,128]{2,1,0:T(8,128)S(1)} %get-tuple-element.25), channel_id=1, source_target_pairs={{0,16},{4,20},{8,24},{12,28},{16,0},{20,4},{24,8},{28,12},{1,17},{... | collective-permute-start | bytes 36872 | tf_op jit(solution)/shard_map/ppermute | solution.py:482
  58.1 3.9 %collective-permute-start.9 = (f32[3,8,128]{2,1,0:T(8,128)S(1)}, f32[3,8,128]{2,1,0:T(8,128)S(1)}, u32[]{:S(2)}, u32[]{:S(2)}) collective-permute-start(f32[3,8,128]{2,1,0:T(8,128)S(1)} %get-tuple-element.26), channel_id=1, source_target_pairs={{0,24},{4,28},{8,0},{12,4},{16,8},{20,12},{24,16},{28,20},{1,25},{... | collective-permute-start | bytes 36872 | tf_op jit(solution)/shard_map/ppermute | solution.py:482
  61.4 0.6 copy-start.12
  61.4 0.6 copy-start.13
  62.0 0.6 copy-start.14

commit v2 on v1

--- a/solution.py
+++ b/solution.py
@@ -11,11 +11,13 @@
 CONTACT_SLOPE = 0.5
 BACKGROUND = 0.5
 FAR = 32.0
-UNIT = 16
+UNIT = 32
 POINT_ROWS = 16
 AXES = ("row", "col")
 VMEM = pl.BlockSpec(memory_space=pltpu.VMEM)
 SMEM = pl.BlockSpec(memory_space=pltpu.SMEM)
+ANY = pl.BlockSpec(memory_space=pl.ANY)
+SMALL = pltpu.CompilerParams(vmem_limit_bytes=8 * 1024 * 1024)
 
 
 def rounded(value):
@@ -67,7 +69,7 @@
         out_ref[4 * sweeps : 5 * sweeps] = jnp.dot(counts, spread, preferred_element_type=jnp.float32)
 
 
-def merge_kernel(points, *refs):
+def merge_kernel(points, after_ref, *refs):
     counts = refs[0][points:]
     for k, ref in enumerate(refs[:-1]):
         refs[-1][k * points : (k + 1) * points] = ref[:points]
@@ -81,17 +83,12 @@
         refs[-1][k * rows : (k + 1) * rows] = ref[...]
 
 
-def prepare_kernel(sizes, lengths_ref, pairs_ref, own_ref, first_ref, marks_ref, list_ref, starts_ref, ends_ref, digits_ref):
+def list_kernel(sizes, lengths_ref, pairs_ref, list_ref, digits_ref):
     slots, sweeps, groups = sizes.slots, sizes.sweeps, sizes.groups
     family = lax.div(lax.axis_index("row"), sizes.share)
     here = lax.rem(lax.axis_index("row"), sizes.share) * sizes.n_col + lax.axis_index("col")
     lane = lax.broadcasted_iota(jnp.int32, (1, 128), 1)
-    row = lax.broadcasted_iota(jnp.int32, (8, 128), 0)
-    labels = starts_ref.shape[0]
-    depth = POINT_ROWS + labels
-
-    starts_ref[...] = jnp.zeros_like(starts_ref)
-    ends_ref[...] = jnp.zeros_like(ends_ref)
+
     slot_row = lax.broadcasted_iota(jnp.int32, (slots, 128), 0)
     block = modulo(slot_row, sweeps) * groups + divide(slot_row, sweeps) * sizes.plane + here
     first_bead = block * 128
@@ -101,56 +98,14 @@
     for k in range(lengths_ref.shape[0]):
         start = end
         end = end + lengths_ref[k]
-        starts_ref[k : k + 1] = jnp.full((1, 128), start)
-        ends_ref[k : k + 1] = jnp.full((1, 128), end)
         low = jnp.maximum(low, jnp.where(start <= first_bead, start, 0))
         high = jnp.minimum(high, jnp.where(end > first_bead + 127, end, sizes.blocks * 128))
-
     low = jnp.maximum(low >> 7, block - (sizes.width - 1))
     high = jnp.minimum(jnp.minimum((high - 1) >> 7, block + (sizes.width - 1)), sizes.blocks - 1)
     reach = []
     for value in (low, high, (high - low + 2) >> 1):
         reach.append(jnp.sum(jnp.where(slot_row == lane, value, 0), axis=0, keepdims=True))
     steps = lax.div(jnp.sum(reach[2]) + (UNIT // 2 - 1), UNIT // 2)
-
-    def mark(group, carry):
-        for u in range(sweeps):
-            bead = (u * groups + group) * 128 + lane
-            inside = (bead >= starts_ref[...]) & (bead < ends_ref[...])
-            marks_ref[group * sweeps + u] = inside.astype(jnp.float32).astype(jnp.bfloat16)
-        return carry
-
-    lax.fori_loop(0, groups, mark, 0)
-
-    def fill(turn, carry):
-        origin = lax.rem(family + (sizes.structures - turn), sizes.structures)
-        for pair in range(sweeps // 2):
-            value = own_ref[pl.ds(pl.multiple_of(turn * sweeps * 4 + pair * 8, 8), 8), :]
-            for odd in range(2):
-                value = pltpu.roll(value, 4, 0) if odd else value
-                high = rounded(value)
-                low = rounded(value - high)
-                shifted = value + 0.5 * CONTACT_SHIFT
-                shifted_high = rounded(shifted)
-                shifted_low = rounded(shifted - shifted_high)
-                both = jnp.where(row < 4, high, pltpu.roll(high, 4, 0))
-                near = jnp.where((row & 3) == 3, 1.0, CONTACT_SLOPE * both)
-                rest = jnp.where(row == 4, pltpu.roll(shifted_low, 1, 0), 0.0)
-                rest = jnp.where(row == 3, shifted_high, rest)
-                rest = jnp.where(row < 3, CONTACT_SLOPE * low, rest)
-                u = 2 * pair + odd
-                bead = (u * groups + origin * sizes.plane + here) * 128 + lane
-                inside = (bead >= starts_ref[...]) & (bead < ends_ref[...])
-                apart = jnp.where(inside, 0.0, -FAR)
-                blank = jnp.zeros((128 - depth, 128), jnp.float32)
-                turned = jnp.transpose(jnp.concatenate([near, rest, apart, blank], axis=0))
-                slot = origin * sweeps + u
-                first_ref[slot] = turned[:, :depth].astype(jnp.bfloat16)
-                other = jnp.where(lane < POINT_ROWS, turned, -FAR - turned)
-                first_ref[slots + slot] = other[:, :depth].astype(jnp.bfloat16)
-        return carry
-
-    lax.fori_loop(0, sizes.structures, fill, 0)
 
     half = pairs_ref.shape[2] // 128
     lines = 2 * half
@@ -226,6 +181,63 @@
     list_ref[end + 1 : end + 2] = reach[0]
     list_ref[end + 2 : end + 3] = reach[1]
     list_ref[end + 3 : end + 4] = jnp.full((1, 128), steps)
+
+
+def own_kernel(sizes, lengths_ref, own_ref, first_ref, marks_ref, starts_ref, ends_ref):
+    slots, sweeps, groups = sizes.slots, sizes.sweeps, sizes.groups
+    family = lax.div(lax.axis_index("row"), sizes.share)
+    here = lax.rem(lax.axis_index("row"), sizes.share) * sizes.n_col + lax.axis_index("col")
+    lane = lax.broadcasted_iota(jnp.int32, (1, 128), 1)
+    row = lax.broadcasted_iota(jnp.int32, (8, 128), 0)
+    labels = starts_ref.shape[0]
+    depth = POINT_ROWS + labels
+
+    starts_ref[...] = jnp.zeros_like(starts_ref)
+    ends_ref[...] = jnp.zeros_like(ends_ref)
+    end = jnp.int32(0)
+    for k in range(lengths_ref.shape[0]):
+        starts_ref[k : k + 1] = jnp.full((1, 128), end)
+        end = end + lengths_ref[k]
+        ends_ref[k : k + 1] = jnp.full((1, 128), end)
+
+    def mark(group, carry):
+        for u in range(sweeps):
+            bead = (u * groups + group) * 128 + lane
+            inside = (bead >= starts_ref[...]) & (bead < ends_ref[...])
+            marks_ref[group * sweeps + u] = inside.astype(jnp.float32).astype(jnp.bfloat16)
+        return carry
+
+    lax.fori_loop(0, groups, mark, 0)
+
+    def fill(turn, carry):
+        origin = lax.rem(family + (sizes.structures - turn), sizes.structures)
+        for pair in range(sweeps // 2):
+            value = own_ref[pl.ds(pl.multiple_of(turn * sweeps * 4 + pair * 8, 8), 8), :]
+            for odd in range(2):
+                value = pltpu.roll(value, 4, 0) if odd else value
+                high = rounded(value)
+                low = rounded(value - high)
+                shifted = value + 0.5 * CONTACT_SHIFT
+                shifted_high = rounded(shifted)
+                shifted_low = rounded(shifted - shifted_high)
+                both = jnp.where(row < 4, high, pltpu.roll(high, 4, 0))
+                near = jnp.where((row & 3) == 3, 1.0, CONTACT_SLOPE * both)
+                rest = jnp.where(row == 4, pltpu.roll(shifted_low, 1, 0), 0.0)
+                rest = jnp.where(row == 3, shifted_high, rest)
+                rest = jnp.where(row < 3, CONTACT_SLOPE * low, rest)
+                u = 2 * pair + odd
+                bead = (u * groups + origin * sizes.plane + here) * 128 + lane
+                inside = (bead >= starts_ref[...]) & (bead < ends_ref[...])
+                apart = jnp.where(inside, 0.0, -FAR)
+                blank = jnp.zeros((128 - depth, 128), jnp.float32)
+                turned = jnp.transpose(jnp.concatenate([near, rest, apart, blank], axis=0))
+                slot = origin * sweeps + u
+                first_ref[slot] = turned[:, :depth].astype(jnp.bfloat16)
+                other = jnp.where(lane < POINT_ROWS, turned, -FAR - turned)
+                first_ref[slots + slot] = other[:, :depth].astype(jnp.bfloat16)
+        return carry
+
+    lax.fori_loop(0, sizes.structures, fill, 0)
 
 
 def tile_kernel(sizes, list_ref, listed_ref, first_ref, marks_ref, same_ref, across_ref, *refs):
@@ -398,6 +410,7 @@
         out_shape=[jax.ShapeDtypeStruct((5 * sweeps, block_size), jnp.float32)] * structures,
         in_specs=[VMEM, VMEM],
         out_specs=[VMEM] * structures,
+        compiler_params=SMALL,
         name="pack",
     )(coords, band_counts)
     deal = [
@@ -407,13 +420,25 @@
     received = [messages[0]]
     for k in range(1, structures):
         received.append(lax.ppermute(messages[k], "row", deal[k]))
+    chunks = -(-(2 * listed + slots + 2 * UNIT) // block_size)
+    tiles = pl.pallas_call(
+        functools.partial(list_kernel, sizes),
+        out_shape=jax.ShapeDtypeStruct((2 * chunks + 8, block_size), jnp.int32),
+        in_specs=[SMEM, VMEM],
+        out_specs=VMEM,
+        scratch_shapes=[pltpu.VMEM((2 * listed // block_size, POINT_ROWS, block_size), jnp.bfloat16)],
+        compiler_params=SMALL,
+        name="list_tiles",
+    )(chrom_lengths, jnp.transpose(inter_pairs, (0, 2, 1)))
+
     own_row = pl.pallas_call(
         functools.partial(merge_kernel, 4 * sweeps),
         out_shape=jax.ShapeDtypeStruct((sizes.rows, block_size), jnp.float32),
-        in_specs=[VMEM] * structures,
+        in_specs=[ANY] + [VMEM] * structures,
         out_specs=VMEM,
+        compiler_params=SMALL,
         name="merge",
-    )(*received)
+    )(tiles, *received)
 
     def device(family, chip, core):
         row = family * share + chip // sizes.half
@@ -433,31 +458,29 @@
         out_shape=jax.ShapeDtypeStruct((sizes.chips * sizes.rows, block_size), jnp.float32),
         in_specs=[VMEM] * sizes.chips,
         out_specs=VMEM,
+        compiler_params=SMALL,
         name="join",
     )(*pieces)
     across = lax.ppermute(same, "col", [(i, i ^ 1) for i in range(n_col)])
 
     labels = -(-chrom_lengths.shape[0] // 16) * 16
     depth = POINT_ROWS + labels
-    chunks = -(-(2 * listed + slots + 2 * UNIT) // block_size)
-    own, marks, tiles = pl.pallas_call(
-        functools.partial(prepare_kernel, sizes),
+    own, marks = pl.pallas_call(
+        functools.partial(own_kernel, sizes),
         out_shape=[
             jax.ShapeDtypeStruct((2 * slots, block_size, depth), jnp.bfloat16),
             jax.ShapeDtypeStruct((blocks, labels, block_size), jnp.bfloat16),
-            jax.ShapeDtypeStruct((2 * chunks + 8, block_size), jnp.int32),
         ],
-        in_specs=[SMEM, VMEM, VMEM],
-        out_specs=[VMEM] * 3,
+        in_specs=[SMEM, VMEM],
+        out_specs=[VMEM] * 2,
         scratch_shapes=[
             pltpu.VMEM((labels, block_size), jnp.int32),
             pltpu.VMEM((labels, block_size), jnp.int32),
-            pltpu.VMEM((2 * listed // block_size, POINT_ROWS, block_size), jnp.bfloat16),
         ],
         cost_estimate=pl.CostEstimate(flops=1 << 30, bytes_accessed=1 << 23, transcendentals=0),
         compiler_params=pltpu.CompilerParams(vmem_limit_bytes=24 * 1024 * 1024),
-        name="prepare",
-    )(chrom_lengths, jnp.transpose(inter_pairs, (0, 2, 1)), own_row)
+        name="own_features",
+    )(chrom_lengths, own_row)
 
     gains = pl.pallas_call(
         functools.partial(tile_kernel, sizes),
@@ -485,6 +508,7 @@
         out_shape=jax.ShapeDtypeStruct(coords.shape, jnp.float32),
         in_specs=[VMEM] * structures,
         out_specs=VMEM,
+        compiler_params=SMALL,
         name="place",
     )(*arrived)
 

time: 64.7 us -> 54.6 us (0.84); the launches traced: 63.9 us -> 55.1 us
  Pallas kernels: 35.9 us -> 30.9 us
  waiting for transfers between devices: 7.95 us -> 5.12 us
  local copies, waits for them, and re-layouts: 4.77 us -> 3.58 us
    ppermute x3, waiting for transfers between devices: 2.64 us -> 0.01 us  [on_device(): received.append(lax.ppermute(messages[k], 'row', deal[k]))]
    pallas_call x1, Pallas kernels: 1.71 us -> 0.02 us  [on_device(): pl.pallas_call(join_kernel, out_shape=jax.ShapeDtypeStruct((sizes.chips *...]
    pallas_call x1, Pallas kernels: 1.56 us -> 0.14 us  [on_device(): pl.pallas_call(functools.partial(pack_kernel, sizes), out_shape=[jax.Shap...]
    pallas_call x1, Pallas kernels: 1.41 us -> 0.01 us  [on_device(): pl.pallas_call(functools.partial(merge_kernel, 4 * sweeps), out_shape=jax...]
    unnamed x30 -> x12, local copies, waits for them, and re-layouts: 4.77 us -> 3.58 us
    pallas_call x1, Pallas kernels: 1.38 us -> 0.63 us  [on_device(): pl.pallas_call(functools.partial(place_kernel, sizes), out_shape=jax.Shap...]
    pallas_call x1 -> x2, Pallas kernels: 4.26 us -> 4.6 us  [the longest x1 2.54 us: on_device(): pl.pallas_call(functools.partial(own_kernel, sizes), out_shape=[jax.Shape...]
  transfers between devices with their start and end apart: 10 -> 10, of which waited for: 8 -> 5; matrix products, arithmetic and copies ran while one was open for 0% -> 0% of each run, Pallas kernels for 7% -> 8%
where the time goes in v2:
time: 54.6 us; the launch traced here: 55.1 us
  Pallas kernels  30.9 us (57%)
  starting transfers between devices  15.4 us (28%)
  waiting for transfers between devices  5.12 us (9%)
  local copies, waits for them, and re-layouts  3.58 us (7%)
    pallas_call x1, Pallas kernels, on_device(): pl.pallas_call(functools.partial(tile_kernel, sizes), out_shape=[jax.Shap...  25.5 us
    ppermute x3, starting transfers between devices, on_device(): received.append(lax.ppermute(messages[k], 'row', deal[k]))  6.96 us
    ppermute x3, starting transfers between devices, on_device(): pieces.append(lax.ppermute(own_row, AXES, moves))  4.5 us
    ppermute x3, starting transfers between devices, on_device(): arrived.append(lax.ppermute(gains[k], 'row', deal[k]))  3.87 us
    unnamed x12, local copies, waits for them, and re-layouts  3.58 us
    ppermute x3, waiting for transfers between devices, on_device(): pieces.append(lax.ppermute(own_row, AXES, moves))  2.87 us
    pallas_call x1, Pallas kernels, on_device(): pl.pallas_call(functools.partial(own_kernel, sizes), out_shape=[jax.Shape...  2.54 us
    ppermute x3, waiting for transfers between devices, on_device(): arrived.append(lax.ppermute(gains[k], 'row', deal[k]))  2.23 us
  transfers between devices with their start and end apart: 10, of which 5 were waited for; matrix products, arithmetic and copies ran while one was open for 0% of the time, Pallas kernels for 8%

profile of v2, /device:TPU:0, one launch (start us, length us, event | category | flops | bytes accessed | tf_op | source)
XLA Modules:
  0.0 55.1 jit_solution(7326707330073882785)
XLA Ops:
  0.0 0.0 copy-start
  0.0 0.8 %copy-done = f32[4,3,8,128]{3,2,1,0:T(8,128)S(1)} copy-done((f32[4,3,8,128]{3,2,1,0:T(8,128)S(1)}, f32[4,3,8,128]{3,2,1,0:T(8,128)}, u32[]{:S(2)}) %copy-start) | copy-done | bytes 49176
  0.8 0.0 copy-start.3
  0.8 0.7 %copy-done.3 = s32[4,8,1,32]{3,2,1,0:T(1,128)S(1)} copy-done((s32[4,8,1,32]{3,2,1,0:T(1,128)S(1)}, s32[4,8,1,32]{3,2,1,0:T(1,128)}, u32[]{:S(2)}) %copy-start.3) | copy-done | bytes 4120
  1.5 0.0 copy-start.2
  1.5 0.1 pack.1
  1.7 3.0 %collective-permute-start = (f32[40,128]{1,0:T(8,128)S(1)}, f32[40,128]{1,0:T(8,128)S(1)}, u32[]{:S(2)}, u32[]{:S(2)}) collective-permute-start(f32[40,128]{1,0:T(8,128)S(1)} %get-tuple-element.16), channel_id=1, source_target_pairs={{0,8},{4,12},{8,16},{12,20},{16,24},{20,28},{24,0},{28,4},{1,9},{5... | collective-permute-start | bytes 61448 | tf_op jit(solution)/shard_map/ppermute | solution.py:422
  4.7 2.6 %collective-permute-start.1 = (f32[40,128]{1,0:T(8,128)S(1)}, f32[40,128]{1,0:T(8,128)S(1)}, u32[]{:S(2)}, u32[]{:S(2)}) collective-permute-start(f32[40,128]{1,0:T(8,128)S(1)} %get-tuple-element.17), channel_id=1, source_target_pairs={{0,16},{4,20},{8,24},{12,28},{16,0},{20,4},{24,8},{28,12},{1,17},{... | collective-permute-start | bytes 61448 | tf_op jit(solution)/shard_map/ppermute | solution.py:422
  7.3 1.3 %collective-permute-start.2 = (f32[40,128]{1,0:T(8,128)S(1)}, f32[40,128]{1,0:T(8,128)S(1)}, u32[]{:S(2)}, u32[]{:S(2)}) collective-permute-start(f32[40,128]{1,0:T(8,128)S(1)} %get-tuple-element.18), channel_id=1, source_target_pairs={{0,24},{4,28},{8,0},{12,4},{16,8},{20,12},{24,16},{28,20},{1,25},{... | collective-permute-start | bytes 61448 | tf_op jit(solution)/shard_map/ppermute | solution.py:422
  8.6 0.0 copy-start.1
  8.6 0.8 %copy-done.1 = s32[4,1024,2]{1,2,0:T(2,128)S(1)} copy-done((s32[4,1024,2]{1,2,0:T(2,128)S(1)}, s32[4,1024,2]{1,2,0:T(2,128)}, u32[]{:S(2)}) %copy-start.1) | copy-done | bytes 32792
  9.4 0.0 copy-start.4
  9.4 0.7 %copy-done.4 = s32[46]{0:T(128)S(1)} copy-done((s32[46]{0:T(128)S(1)}, s32[46]{0:T(128)}, u32[]{:S(2)}) %copy-start.4) | copy-done | bytes 208
  10.0 2.1 %list_tiles.1.after_ref.list_ref = s32[42,128]{1,0:T(8,128)S(1)} custom-call(s32[46]{0:T(128)S(1)} %copy-done.4, s32[4,2,1024]{2,1,0:T(2,128)S(1)} %bitcast.1), custom_call_target="tpu_custom_call" | custom-call | tf_op jit(solution)/shard_map/list_tiles/pallas_call | solution.py:424
  12.1 0.0 collective-permute-done.refs_1_
  12.1 0.0 collective-permute-done.1.refs_2_
  12.1 0.0 collective-permute-done.2.refs_3_
  12.2 1.5 %collective-permute-start.3 = (f32[136,128]{1,0:T(8,128)S(1)}, f32[136,128]{1,0:T(8,128)S(1)}, u32[]{:S(2)}, u32[]{:S(2)}) collective-permute-start(f32[136,128]{1,0:T(8,128)S(1)} %merge.1.own_ref.refs_0_), channel_id=1, source_target_pairs={{0,2},{1,3},{2,4},{3,5},{4,6},{5,7},{6,0},{7,1},{8,10},{9,11},{10,... | collective-permute-start | bytes 208904 | tf_op jit(solution)/shard_map/ppermute | solution.py:455
  13.7 1.5 %collective-permute-start.4 = (f32[136,128]{1,0:T(8,128)S(1)}, f32[136,128]{1,0:T(8,128)S(1)}, u32[]{:S(2)}, u32[]{:S(2)}) collective-permute-start(f32[136,128]{1,0:T(8,128)S(1)} %merge.1.own_ref.refs_0_), channel_id=1, source_target_pairs={{0,4},{1,5},{2,6},{3,7},{4,0},{5,1},{6,2},{7,3},{8,12},{9,13},{10,... | collective-permute-start | bytes 208904 | tf_op jit(solution)/shard_map/ppermute | solution.py:455
  15.2 1.4 %collective-permute-start.5 = (f32[136,128]{1,0:T(8,128)S(1)}, f32[136,128]{1,0:T(8,128)S(1)}, u32[]{:S(2)}, u32[]{:S(2)}) collective-permute-start(f32[136,128]{1,0:T(8,128)S(1)} %merge.1.own_ref.refs_0_), channel_id=1, source_target_pairs={{0,6},{1,7},{2,0},{3,1},{4,2},{5,3},{6,4},{7,5},{8,14},{9,15},{10,... | collective-permute-start | bytes 208904 | tf_op jit(solution)/shard_map/ppermute | solution.py:455
  16.7 1.1 %collective-permute-done.3.refs_1_ = f32[136,128]{1,0:T(8,128)S(1)} collective-permute-done((f32[136,128]{1,0:T(8,128)S(1)}, f32[136,128]{1,0:T(8,128)S(1)}, u32[]{:S(2)}, u32[]{:S(2)}) %collective-permute-start.3) | collective-permute-done | bytes 69664 | tf_op jit(solution)/shard_map/ppermute | solution.py:455
  17.8 0.6 %collective-permute-done.4.refs_2_ = f32[136,128]{1,0:T(8,128)S(1)} collective-permute-done((f32[136,128]{1,0:T(8,128)S(1)}, f32[136,128]{1,0:T(8,128)S(1)}, u32[]{:S(2)}, u32[]{:S(2)}) %collective-permute-start.4) | collective-permute-done | bytes 69664 | tf_op jit(solution)/shard_map/ppermute | solution.py:455
  18.4 1.1 %collective-permute-done.5.refs_3_ = f32[136,128]{1,0:T(8,128)S(1)} collective-permute-done((f32[136,128]{1,0:T(8,128)S(1)}, f32[136,128]{1,0:T(8,128)S(1)}, u32[]{:S(2)}, u32[]{:S(2)}) %collective-permute-start.5) | collective-permute-done | bytes 69664 | tf_op jit(solution)/shard_map/ppermute | solution.py:455
  19.6 0.1 collective-permute-start.6
  19.6 0.0 copy-start.5
  19.6 0.6 %copy-done.5 = s32[46]{0:T(128)S(1)} copy-done((s32[46]{0:T(128)S(1)}, s32[46]{0:T(128)}, u32[]{:S(2)}) %copy-start.5) | copy-done | bytes 208
  20.3 2.5 %own_features.1 = (bf16[64,128,64]{2,1,0:T(8,128)(2,1)S(1)}, bf16[256,48,128]{2,1,0:T(8,128)(2,1)S(1)}) custom-call(s32[46]{0:T(128)S(1)} %copy-done.5, f32[136,128]{1,0:T(8,128)S(1)} %merge.1.own_ref.refs_0_), custom_call_target="tpu_custom_call" | custom-call | flops 1073741824 | bytes 8388608 | tf_op jit(solution)/shard_map/own_features/pallas_call | solution.py:468
  22.8 0.0 collective-permute-done.6.across_ref
  22.8 0.0 copy-done.2
  22.9 25.5 %tiles.1 = (f32[3,8,128]{2,1,0:T(8,128)S(1)}, f32[3,8,128]{2,1,0:T(8,128)S(1)}, f32[3,8,128]{2,1,0:T(8,128)S(1)}, f32[3,8,128]{2,1,0:T(8,128)S(1)}) custom-call(s32[42,128]{1,0:T(8,128)S(1)} %list_tiles.1.after_ref.list_ref, s32[4,1024]{1,0:T(4,128)S(1)} %copy-done.2, bf16[64,128,64]{2,1,0:T(8,128)(2,1)S(1)} %get-tuple-element.19.first_ref, ...), custom_call_target="tpu_custom_call" | custom-call | tf_op jit(solution)/shard_map/tiles/pallas_call | solution.py:485
  48.4 0.1 collective-permute-start.7
  48.4 1.8 %collective-permute-start.8 = (f32[3,8,128]{2,1,0:T(8,128)S(1)}, f32[3,8,128]{2,1,0:T(8,128)S(1)}, u32[]{:S(2)}, u32[]{:S(2)}) collective-permute-start(f32[3,8,128]{2,1,0:T(8,128)S(1)} %get-tuple-element.23), channel_id=1, source_target_pairs={{0,16},{4,20},{8,24},{12,28},{16,0},{20,4},{24,8},{28,12},{1,17},{... | collective-permute-start | bytes 36872 | tf_op jit(solution)/shard_map/ppermute | solution.py:505
  50.2 2.1 %collective-permute-start.9 = (f32[3,8,128]{2,1,0:T(8,128)S(1)}, f32[3,8,128]{2,1,0:T(8,128)S(1)}, u32[]{:S(2)}, u32[]{:S(2)}) collective-permute-start(f32[3,8,128]{2,1,0:T(8,128)S(1)} %get-tuple-element.24), channel_id=1, source_target_pairs={{0,24},{4,28},{8,0},{12,4},{16,8},{20,12},{24,16},{28,20},{1,25},{... | collective-permute-start | bytes 36872 | tf_op jit(solution)/shard_map/ppermute | solution.py:505
  52.3 1.7 %collective-permute-done.7.refs_1_ = f32[3,8,128]{2,1,0:T(8,128)S(1)} collective-permute-done((f32[3,8,128]{2,1,0:T(8,128)S(1)}, f32[3,8,128]{2,1,0:T(8,128)S(1)}, u32[]{:S(2)}, u32[]{:S(2)}) %collective-permute-start.7) | collective-permute-done | bytes 12320 | tf_op jit(solution)/shard_map/ppermute | solution.py:505
  53.9 0.0 collective-permute-done.8.refs_2_
  53.9 0.6 %collective-permute-done.9.refs_3_ = f32[3,8,128]{2,1,0:T(8,128)S(1)} collective-permute-done((f32[3,8,128]{2,1,0:T(8,128)S(1)}, f32[3,8,128]{2,1,0:T(8,128)S(1)}, u32[]{:S(2)}, u32[]{:S(2)}) %collective-permute-start.9) | collective-permute-done | bytes 12320 | tf_op jit(solution)/shard_map/ppermute | solution.py:505
  54.5 0.6 %place.1 = f32[4,3,8,128]{3,2,1,0:T(8,128)} custom-call(f32[3,8,128]{2,1,0:T(8,128)S(1)} %get-tuple-element.21.refs_0_, f32[3,8,128]{2,1,0:T(8,128)S(1)} %collective-permute-done.7.refs_1_, f32[3,8,128]{2,1,0:T(8,128)S(1)} %collective-permute-done.8.refs_2_, f32[3,8,128]{2,1,0:T(8,128)S(1)} %collective-permute-done.9.refs_3_), custom_call_target="tpu_custom_call" | custom-call | tf_op jit(solution)/shard_map/place/pallas_call | solution.py:506
  (2 shorter events, 0.0 us)
Async XLA Ops:
  0.0 0.8 %copy-start = (f32[4,3,8,128]{3,2,1,0:T(8,128)S(1)}, f32[4,3,8,128]{3,2,1,0:T(8,128)}, u32[]{:S(2)}) copy-start(f32[4,3,8,128]{3,2,1,0:T(8,128)} %coords_ref.1) | copy-start | bytes 147460
  0.8 0.7 %copy-start.3 = (s32[4,8,1,32]{3,2,1,0:T(1,128)S(1)}, s32[4,8,1,32]{3,2,1,0:T(1,128)}, u32[]{:S(2)}) copy-start(s32[4,8,1,32]{3,2,1,0:T(1,128)} %counts_ref.1) | copy-start | bytes 12292
  1.5 21.3 %copy-start.2 = (s32[4,1024]{1,0:T(4,128)S(1)}, s32[4,1024]{1,0:T(4,128)}, u32[]{:S(2)}) copy-start(s32[4,1024]{1,0:T(4,128)} %listed_ref.1) | copy-start | bytes 49156
  1.7 10.5 %collective-permute-start = (f32[40,128]{1,0:T(8,128)S(1)}, f32[40,128]{1,0:T(8,128)S(1)}, u32[]{:S(2)}, u32[]{:S(2)}) collective-permute-start(f32[40,128]{1,0:T(8,128)S(1)} %get-tuple-element.16), channel_id=1, source_target_pairs={{0,8},{4,12},{8,16},{12,20},{16,24},{20,28},{24,0},{28,4},{1,9},{5... | collective-permute-start | bytes 61448 | tf_op jit(solution)/shard_map/ppermute | solution.py:422
  4.7 7.4 %collective-permute-start.1 = (f32[40,128]{1,0:T(8,128)S(1)}, f32[40,128]{1,0:T(8,128)S(1)}, u32[]{:S(2)}, u32[]{:S(2)}) collective-permute-start(f32[40,128]{1,0:T(8,128)S(1)} %get-tuple-element.17), channel_id=1, source_target_pairs={{0,16},{4,20},{8,24},{12,28},{16,0},{20,4},{24,8},{28,12},{1,17},{... | collective-permute-start | bytes 61448 | tf_op jit(solution)/shard_map/ppermute | solution.py:422
  7.3 4.9 %collective-permute-start.2 = (f32[40,128]{1,0:T(8,128)S(1)}, f32[40,128]{1,0:T(8,128)S(1)}, u32[]{:S(2)}, u32[]{:S(2)}) collective-permute-start(f32[40,128]{1,0:T(8,128)S(1)} %get-tuple-element.18), channel_id=1, source_target_pairs={{0,24},{4,28},{8,0},{12,4},{16,8},{20,12},{24,16},{28,20},{1,25},{... | collective-permute-start | bytes 61448 | tf_op jit(solution)/shard_map/ppermute | solution.py:422
  8.6 0.8 %copy-start.1 = (s32[4,1024,2]{1,2,0:T(2,128)S(1)}, s32[4,1024,2]{1,2,0:T(2,128)}, u32[]{:S(2)}) copy-start(s32[4,1024,2]{1,2,0:T(2,128)} %param.8) | copy-start | bytes 98308
  9.4 0.7 %copy-start.4 = (s32[46]{0:T(128)S(1)}, s32[46]{0:T(128)}, u32[]{:S(2)}) copy-start(s32[46]{0:T(128)} %lengths_ref.3) | copy-start | bytes 556
  12.2 5.6 %collective-permute-start.3 = (f32[136,128]{1,0:T(8,128)S(1)}, f32[136,128]{1,0:T(8,128)S(1)}, u32[]{:S(2)}, u32[]{:S(2)}) collective-permute-start(f32[136,128]{1,0:T(8,128)S(1)} %merge.1.own_ref.refs_0_), channel_id=1, source_target_pairs={{0,2},{1,3},{2,4},{3,5},{4,6},{5,7},{6,0},{7,1},{8,10},{9,11},{10,... | collective-permute-start | bytes 208904 | tf_op jit(solution)/shard_map/ppermute | solution.py:455
  13.7 4.7 %collective-permute-start.4 = (f32[136,128]{1,0:T(8,128)S(1)}, f32[136,128]{1,0:T(8,128)S(1)}, u32[]{:S(2)}, u32[]{:S(2)}) collective-permute-start(f32[136,128]{1,0:T(8,128)S(1)} %merge.1.own_ref.refs_0_), channel_id=1, source_target_pairs={{0,4},{1,5},{2,6},{3,7},{4,0},{5,1},{6,2},{7,3},{8,12},{9,13},{10,... | collective-permute-start | bytes 208904 | tf_op jit(solution)/shard_map/ppermute | solution.py:455
  15.2 4.3 %collective-permute-start.5 = (f32[136,128]{1,0:T(8,128)S(1)}, f32[136,128]{1,0:T(8,128)S(1)}, u32[]{:S(2)}, u32[]{:S(2)}) collective-permute-start(f32[136,128]{1,0:T(8,128)S(1)} %merge.1.own_ref.refs_0_), channel_id=1, source_target_pairs={{0,6},{1,7},{2,0},{3,1},{4,2},{5,3},{6,4},{7,5},{8,14},{9,15},{10,... | collective-permute-start | bytes 208904 | tf_op jit(solution)/shard_map/ppermute | solution.py:455
  19.6 3.3 %collective-permute-start.6 = (f32[544,128]{1,0:T(8,128)S(1)}, f32[544,128]{1,0:T(8,128)S(1)}, u32[]{:S(2)}, u32[]{:S(2)}) collective-permute-start(f32[544,128]{1,0:T(8,128)S(1)} %join.1.same_ref), channel_id=1, source_target_pairs={{0,1},{1,0},{2,3},{3,2},{4,5},{5,4},{6,7},{7,6},{8,9},{9,8},{10,11... | collective-permute-start | bytes 835592 | tf_op jit(solution)/shard_map/ppermute | solution.py:464
  19.6 0.7 %copy-start.5 = (s32[46]{0:T(128)S(1)}, s32[46]{0:T(128)}, u32[]{:S(2)}) copy-start(s32[46]{0:T(128)} %lengths_ref.3) | copy-start | bytes 556
  48.4 5.5 %collective-permute-start.7 = (f32[3,8,128]{2,1,0:T(8,128)S(1)}, f32[3,8,128]{2,1,0:T(8,128)S(1)}, u32[]{:S(2)}, u32[]{:S(2)}) collective-permute-start(f32[3,8,128]{2,1,0:T(8,128)S(1)} %get-tuple-element.22), channel_id=1, source_target_pairs={{0,8},{4,12},{8,16},{12,20},{16,24},{20,28},{24,0},{28,4},{1,9},{5... | collective-permute-start | bytes 36872 | tf_op jit(solution)/shard_map/ppermute | solution.py:505
  48.4 5.5 %collective-permute-start.8 = (f32[3,8,128]{2,1,0:T(8,128)S(1)}, f32[3,8,128]{2,1,0:T(8,128)S(1)}, u32[]{:S(2)}, u32[]{:S(2)}) collective-permute-start(f32[3,8,128]{2,1,0:T(8,128)S(1)} %get-tuple-element.23), channel_id=1, source_target_pairs={{0,16},{4,20},{8,24},{12,28},{16,0},{20,4},{24,8},{28,12},{1,17},{... | collective-permute-start | bytes 36872 | tf_op jit(solution)/shard_map/ppermute | solution.py:505
  50.2 4.3 %collective-permute-start.9 = (f32[3,8,128]{2,1,0:T(8,128)S(1)}, f32[3,8,128]{2,1,0:T(8,128)S(1)}, u32[]{:S(2)}, u32[]{:S(2)}) collective-permute-start(f32[3,8,128]{2,1,0:T(8,128)S(1)} %get-tuple-element.24), channel_id=1, source_target_pairs={{0,24},{4,28},{8,0},{12,4},{16,8},{20,12},{24,16},{28,20},{1,25},{... | collective-permute-start | bytes 36872 | tf_op jit(solution)/shard_map/ppermute | solution.py:505

commit v3 on v2

--- a/solution.py
+++ b/solution.py
@@ -77,13 +77,13 @@
     refs[-1][(len(refs) - 1) * points :] = counts
 
 
-def join_kernel(*refs):
+def join_kernel(after_ref, *refs):
     rows = refs[0].shape[0]
     for k, ref in enumerate(refs[:-1]):
         refs[-1][k * rows : (k + 1) * rows] = ref[...]
 
 
-def list_kernel(sizes, lengths_ref, pairs_ref, list_ref, digits_ref):
+def list_kernel(sizes, lengths_ref, pairs_ref, list_ref, edges_ref, digits_ref):
     slots, sweeps, groups = sizes.slots, sizes.sweeps, sizes.groups
     family = lax.div(lax.axis_index("row"), sizes.share)
     here = lax.rem(lax.axis_index("row"), sizes.share) * sizes.n_col + lax.axis_index("col")
@@ -94,10 +94,13 @@
     first_bead = block * 128
     low = jnp.zeros((slots, 128), jnp.int32)
     high = jnp.full((slots, 128), sizes.blocks * 128)
+    edges_ref[...] = jnp.zeros_like(edges_ref)
     end = jnp.int32(0)
     for k in range(lengths_ref.shape[0]):
         start = end
         end = end + lengths_ref[k]
+        edges_ref[0, k : k + 1] = jnp.full((1, 128), start)
+        edges_ref[1, k : k + 1] = jnp.full((1, 128), end)
         low = jnp.maximum(low, jnp.where(start <= first_bead, start, 0))
         high = jnp.minimum(high, jnp.where(end > first_bead + 127, end, sizes.blocks * 128))
     low = jnp.maximum(low >> 7, block - (sizes.width - 1))
@@ -183,27 +186,19 @@
     list_ref[end + 3 : end + 4] = jnp.full((1, 128), steps)
 
 
-def own_kernel(sizes, lengths_ref, own_ref, first_ref, marks_ref, starts_ref, ends_ref):
+def own_kernel(sizes, edges_ref, own_ref, first_ref, marks_ref):
     slots, sweeps, groups = sizes.slots, sizes.sweeps, sizes.groups
     family = lax.div(lax.axis_index("row"), sizes.share)
     here = lax.rem(lax.axis_index("row"), sizes.share) * sizes.n_col + lax.axis_index("col")
     lane = lax.broadcasted_iota(jnp.int32, (1, 128), 1)
     row = lax.broadcasted_iota(jnp.int32, (8, 128), 0)
-    labels = starts_ref.shape[0]
+    labels = edges_ref.shape[1]
     depth = POINT_ROWS + labels
-
-    starts_ref[...] = jnp.zeros_like(starts_ref)
-    ends_ref[...] = jnp.zeros_like(ends_ref)
-    end = jnp.int32(0)
-    for k in range(lengths_ref.shape[0]):
-        starts_ref[k : k + 1] = jnp.full((1, 128), end)
-        end = end + lengths_ref[k]
-        ends_ref[k : k + 1] = jnp.full((1, 128), end)
 
     def mark(group, carry):
         for u in range(sweeps):
             bead = (u * groups + group) * 128 + lane
-            inside = (bead >= starts_ref[...]) & (bead < ends_ref[...])
+            inside = (bead >= edges_ref[0]) & (bead < edges_ref[1])
             marks_ref[group * sweeps + u] = inside.astype(jnp.float32).astype(jnp.bfloat16)
         return carry
 
@@ -227,7 +222,7 @@
                 rest = jnp.where(row < 3, CONTACT_SLOPE * low, rest)
                 u = 2 * pair + odd
                 bead = (u * groups + origin * sizes.plane + here) * 128 + lane
-                inside = (bead >= starts_ref[...]) & (bead < ends_ref[...])
+                inside = (bead >= edges_ref[0]) & (bead < edges_ref[1])
                 apart = jnp.where(inside, 0.0, -FAR)
                 blank = jnp.zeros((128 - depth, 128), jnp.float32)
                 turned = jnp.transpose(jnp.concatenate([near, rest, apart, blank], axis=0))
@@ -243,7 +238,9 @@
 def tile_kernel(sizes, list_ref, listed_ref, first_ref, marks_ref, same_ref, across_ref, *refs):
     structures, sweeps, slots = sizes.structures, sizes.sweeps, sizes.slots
     out_refs = refs[:structures]
-    second_ref, counts_ref, held_ref, sums_ref, picks_ref, diag_ref, total_ref = refs[structures:]
+    second_ref, turned_ref, mask_ref, counts_ref, held_ref, sums_ref, picks_ref, state_ref, total_ref, gain_ref = refs[
+        structures:
+    ]
     row_here = lax.axis_index("row")
     column_here = lax.axis_index("col")
     family = lax.div(row_here, sizes.share)
@@ -252,6 +249,9 @@
     lane = lax.broadcasted_iota(jnp.int32, (1, 128), 1)
     row = lax.broadcasted_iota(jnp.int32, (8, 128), 0)
     ones = jnp.where((row == 3) | (row == 4), 1.0, 0.0)
+    unit = jnp.where(row == 3, 1.0, 0.0)
+    for k in range(2 * sweeps):
+        mask_ref[k] = jnp.broadcast_to(lane >> 3 == k, (16, 128)).astype(jnp.float32).astype(jnp.bfloat16)
 
     for core, piece_ref in ((core_here, same_ref), (1 - core_here, across_ref)):
         for k in range(sizes.chips):
@@ -263,23 +263,22 @@
             ]
             for turn in range(structures):
                 origin = lax.rem(family + (structures - turn), structures)
-                at = (origin * sizes.plane + device) * sweeps
+                group = origin * sizes.plane + device
+                columns = []
                 for pair in range(sweeps // 2):
                     start = base + turn * sweeps * 4 + pair * 8
                     value = piece_ref[start : start + 8]
                     high = rounded(value)
                     low = value - high
                     high_turned = pltpu.roll(high, 4, 0)
-                    even = jnp.concatenate(
-                        [jnp.where(row < 4, high, pltpu.roll(low, 4, 0)), jnp.where(row < 3, high, ones)],
-                        axis=0,
-                    )
-                    odd = jnp.concatenate(
-                        [jnp.where(row < 4, high_turned, low), jnp.where(row < 3, high_turned, ones)],
-                        axis=0,
-                    )
-                    second_ref[at + 2 * pair] = even.astype(jnp.bfloat16)
-                    second_ref[at + 2 * pair + 1] = odd.astype(jnp.bfloat16)
+                    for odd, (top, bottom) in enumerate(
+                        ((high, pltpu.roll(low, 4, 0)), (high_turned, low))
+                    ):
+                        points = jnp.where(row < 4, top, bottom)
+                        features = jnp.concatenate([points, jnp.where(row < 3, top, ones)], axis=0)
+                        second_ref[group * sweeps + 2 * pair + odd] = features.astype(jnp.bfloat16)
+                        columns.append(jnp.where((row & 3) == 3, unit, points))
+                turned_ref[group] = jnp.transpose(jnp.concatenate(columns * 2, axis=0)).astype(jnp.bfloat16)
     listed_base = sizes.plane * sweeps
     chosen = lax.broadcasted_iota(jnp.int32, (structures, 128), 0) == family
     for k in range(listed_ref.shape[1] // 128):
@@ -301,20 +300,21 @@
             sums = sums + sums_ref[pl.ds(k, UNIT, stride=8), :]
         chance = 64.0 * 128.0 + 0.5 * jnp.sum(sums, axis=1, keepdims=True)
         count = jnp.sum(picks_ref[...], axis=1, keepdims=True)
-        chance = jnp.where(diag_ref[...] > 0.5, 0.5 * (chance - 128.0 * spare), chance)
-        weight = 1.0 - count / (BACKGROUND + chance / 128.0)
+        state = state_ref[...]
+        chance = jnp.where(state == 1.0, 0.5 * (chance - 128.0 * spare), chance)
+        weight = jnp.where(state == 2.0, 0.0, 1.0 - count / (BACKGROUND + chance / 128.0))
         for t in range(0, UNIT, 2):
-            left, right = (second_ref[ending[t + i] & 4095] for i in range(2))
-            product = lax.dot_general(
-                jnp.concatenate([left, right], axis=0),
-                held_ref[t * 128 : (t + 2) * 128],
-                (((1,), (1,)), ((), ())),
-                preferred_element_type=jnp.float32,
+            columns = []
+            for i in range(2):
+                at = ending[t + i] & 4095
+                mask = mask_ref[modulo(at, sweeps) + i * sweeps]
+                column = turned_ref[divide(at, sweeps)].reshape(8, 16, 128) * mask[None]
+                columns.append(column.reshape(128, 128))
+            product = jnp.dot(
+                held_ref[t // 2], jnp.concatenate(columns, axis=0), preferred_element_type=jnp.float32
             )
-            for i in range(2):
-                gain = product[i * POINT_ROWS : (i + 1) * POINT_ROWS, i * 128 : (i + 1) * 128]
-                at = pl.multiple_of((ending[t + i] >> 19) * POINT_ROWS, POINT_ROWS)
-                total_ref[pl.ds(at, POINT_ROWS), :] += weight[t + i : t + i + 1] * gain
+            scale = jnp.where(lane < 64, weight[t : t + 1], weight[t + 1 : t + 2])
+            total_ref[ending[t] >> 19] += scale * product
         for t in range(0, UNIT, 2):
             seconds = [beginning[t + i][0] & 4095 for i in range(2)]
             logit = jnp.dot(
@@ -325,17 +325,14 @@
                 preferred_element_type=jnp.float32,
             )
             bend = jnp.tanh(logit)
-            rest = 1.0 - bend * bend
+            held_ref[t // 2] = (1.0 - bend * bend).astype(jnp.bfloat16)
             for i in range(2):
                 part = bend[:, i * 128 : (i + 1) * 128]
                 sums_ref[(t + i) * 8 : (t + i + 1) * 8] = jnp.sum(part.reshape(16, 8, 128), axis=0)
-                held_ref[(t + i) * 128 : (t + i + 1) * 128] = rest[:, i * 128 : (i + 1) * 128].astype(
-                    jnp.bfloat16
-                )
-                code, place, diagonal = beginning[t + i]
+                code, place, state = beginning[t + i]
                 picked = counts_ref[pl.ds(place >> 7, 1), :]
                 picks_ref[t + i : t + i + 1] = jnp.where(lane == (place & 127), picked, 0.0)
-                diag_ref[t + i : t + i + 1] = jnp.full((1, 128), diagonal)
+                state_ref[t + i : t + i + 1] = jnp.full((1, 128), state)
         return tuple(code for code, _, _ in beginning)
 
     def band_step(turn, carry):
@@ -351,9 +348,10 @@
                 line = modulo(group, sizes.plane) * sweeps + divide(first, groups)
                 apart = jnp.abs(block - second)
                 place = line * 128 + divide(group, sizes.plane) * sizes.width + apart
-                total = jnp.where(other + i <= high, slot, slots)
-                code = sizes.at(second) + (jnp.minimum(slot, slots - 1) << 12) + (total << 19)
-                beginning.append((code, place, (apart == 0).astype(jnp.float32)))
+                live = (other + i <= high) & (slot < slots)
+                code = sizes.at(second) + (jnp.minimum(slot, slots - 1) << 12) + (slot << 19)
+                state = jnp.where(live, (apart == 0).astype(jnp.float32), 2.0)
+                beginning.append((code, place, state))
             over = other + 2 > high
             slot = jnp.minimum(slot + over.astype(jnp.int32), slots)
             other = jnp.where(over, list_ref[2 * chunks + 1, slot], other + 2)
@@ -363,9 +361,9 @@
         beginning = []
         for t in range(UNIT):
             at = turn * UNIT + t
-            beginning.append(
-                (list_ref[at >> 7, at & 127], list_ref[chunks + (at >> 7), at & 127], jnp.float32(0.0))
-            )
+            code = list_ref[at >> 7, at & 127]
+            state = jnp.where(code >> 19 < slots, 0.0, 2.0)
+            beginning.append((code, list_ref[chunks + (at >> 7), at & 127], state))
         return step(ending, beginning)
 
     idle = (jnp.int32(slots << 19),) * UNIT
@@ -375,19 +373,25 @@
     listed_steps = lax.div(list_ref[2 * chunks, 0] + UNIT - 1, UNIT)
     lax.fori_loop(0, listed_steps + 1, listed_step, ending)
 
+    def collect(slot, carry):
+        turned = jnp.transpose(total_ref[slot])
+        gain_ref[pl.ds(pl.multiple_of(slot * 8, 8), 8), :] = jnp.sum(turned.reshape(16, 8, 128), axis=0)
+        return carry
+
+    lax.fori_loop(0, slots, collect, 0, unroll=4)
     scale = -2.0 * CONTACT_SLOPE / 128.0 / 4.0
     for k in range(structures):
         origin = lax.rem(family + k, structures)
         turn = (structures - k) % structures
-        first = origin * sweeps * POINT_ROWS
-        mass = total_ref[pl.ds(first + 11, sweeps, stride=POINT_ROWS), :]
+        first = origin * sweeps * 8
+        mass = gain_ref[pl.ds(first + 3, sweeps, stride=8), :]
         for place in range(3):
             point = same_ref[pl.ds(turn * sweeps * 4 + place, sweeps, stride=4), :]
             high = rounded(point)
             near = high + rounded(point - high)
             pull = (
-                total_ref[pl.ds(first + place, sweeps, stride=POINT_ROWS), :]
-                + total_ref[pl.ds(first + place + 4, sweeps, stride=POINT_ROWS), :]
+                gain_ref[pl.ds(first + place, sweeps, stride=8), :]
+                + gain_ref[pl.ds(first + place + 4, sweeps, stride=8), :]
             )
             out_refs[k][place] = scale * (near * mass - pull)
 
@@ -421,11 +425,15 @@
     for k in range(1, structures):
         received.append(lax.ppermute(messages[k], "row", deal[k]))
     chunks = -(-(2 * listed + slots + 2 * UNIT) // block_size)
-    tiles = pl.pallas_call(
+    labels = -(-chrom_lengths.shape[0] // 16) * 16
+    tiles, edges = pl.pallas_call(
         functools.partial(list_kernel, sizes),
-        out_shape=jax.ShapeDtypeStruct((2 * chunks + 8, block_size), jnp.int32),
+        out_shape=[
+            jax.ShapeDtypeStruct((2 * chunks + 8, block_size), jnp.int32),
+            jax.ShapeDtypeStruct((2, labels, block_size), jnp.int32),
+        ],
         in_specs=[SMEM, VMEM],
-        out_specs=VMEM,
+        out_specs=[VMEM] * 2,
         scratch_shapes=[pltpu.VMEM((2 * listed // block_size, POINT_ROWS, block_size), jnp.bfloat16)],
         compiler_params=SMALL,
         name="list_tiles",
@@ -453,17 +461,6 @@
             for core in range(2)
         ]
         pieces.append(lax.ppermute(own_row, AXES, moves))
-    same = pl.pallas_call(
-        join_kernel,
-        out_shape=jax.ShapeDtypeStruct((sizes.chips * sizes.rows, block_size), jnp.float32),
-        in_specs=[VMEM] * sizes.chips,
-        out_specs=VMEM,
-        compiler_params=SMALL,
-        name="join",
-    )(*pieces)
-    across = lax.ppermute(same, "col", [(i, i ^ 1) for i in range(n_col)])
-
-    labels = -(-chrom_lengths.shape[0] // 16) * 16
     depth = POINT_ROWS + labels
     own, marks = pl.pallas_call(
         functools.partial(own_kernel, sizes),
@@ -471,16 +468,21 @@
             jax.ShapeDtypeStruct((2 * slots, block_size, depth), jnp.bfloat16),
             jax.ShapeDtypeStruct((blocks, labels, block_size), jnp.bfloat16),
         ],
-        in_specs=[SMEM, VMEM],
+        in_specs=[VMEM, VMEM],
         out_specs=[VMEM] * 2,
-        scratch_shapes=[
-            pltpu.VMEM((labels, block_size), jnp.int32),
-            pltpu.VMEM((labels, block_size), jnp.int32),
-        ],
-        cost_estimate=pl.CostEstimate(flops=1 << 30, bytes_accessed=1 << 23, transcendentals=0),
         compiler_params=pltpu.CompilerParams(vmem_limit_bytes=24 * 1024 * 1024),
         name="own_features",
-    )(chrom_lengths, own_row)
+    )(edges, own_row)
+
+    same = pl.pallas_call(
+        join_kernel,
+        out_shape=jax.ShapeDtypeStruct((sizes.chips * sizes.rows, block_size), jnp.float32),
+        in_specs=[ANY] + [VMEM] * sizes.chips,
+        out_specs=VMEM,
+        compiler_params=SMALL,
+        name="join",
+    )(marks, *pieces)
+    across = lax.ppermute(same, "col", [(i, i ^ 1) for i in range(n_col)])
 
     gains = pl.pallas_call(
         functools.partial(tile_kernel, sizes),
@@ -489,12 +491,15 @@
         out_specs=[VMEM] * structures,
         scratch_shapes=[
             pltpu.VMEM((blocks, POINT_ROWS, block_size), jnp.bfloat16),
+            pltpu.VMEM((sizes.groups, block_size, block_size), jnp.bfloat16),
+            pltpu.VMEM((2 * sweeps, POINT_ROWS, block_size), jnp.bfloat16),
             pltpu.VMEM((sizes.plane * sweeps + listed // block_size, block_size), jnp.float32),
-            pltpu.VMEM((UNIT * block_size, block_size), jnp.bfloat16),
+            pltpu.VMEM((UNIT // 2, block_size, 2 * block_size), jnp.bfloat16),
             pltpu.VMEM((UNIT * 8, block_size), jnp.float32),
             pltpu.VMEM((UNIT, block_size), jnp.float32),
             pltpu.VMEM((UNIT, block_size), jnp.float32),
-            pltpu.VMEM(((slots + 1) * POINT_ROWS, block_size), jnp.float32),
+            pltpu.VMEM((slots + 1, block_size, block_size), jnp.float32),
+            pltpu.VMEM((slots * 8, block_size), jnp.float32),
         ],
         compiler_params=pltpu.CompilerParams(vmem_limit_bytes=40 * 1024 * 1024),
         name="tiles",

time: 54.6 us -> 54.8 us (level)
  waiting for transfers between devices: 5.12 us -> 7.26 us
  Pallas kernels: 30.9 us -> 29.9 us
  local copies, waits for them, and re-layouts: 3.58 us -> 2.93 us
  starting transfers between devices: 15.4 us -> 14.8 us
    ppermute x1, waiting for transfers between devices: 0.01 us -> 1.55 us  [on_device(): across = lax.ppermute(same, 'col', [(i, i ^ 1) for i in range(n_col)])]
    ppermute x3, starting transfers between devices: 4.5 us -> 3.6 us  [on_device(): pieces.append(lax.ppermute(own_row, AXES, moves))]
    ppermute x3, waiting for transfers between devices: 2.23 us -> 3.06 us  [on_device(): arrived.append(lax.ppermute(gains[k], 'row', deal[k]))]
    unnamed x12 -> x10, local copies, waits for them, and re-layouts: 3.58 us -> 2.93 us
    pallas_call x1, Pallas kernels: 2.54 us -> 1.96 us  [on_device(): pl.pallas_call(functools.partial(own_kernel, sizes), out_shape=[jax.Shape...]
  transfers between devices with their start and end apart: 10 -> 10, of which waited for: 5 -> 6; matrix products, arithmetic and copies ran while one was open for 0% -> 0% of each run, Pallas kernels for 8% -> 7%
where the time goes in v3:
time: 54.8 us; the launch traced here: 54.9 us
  Pallas kernels  29.9 us (55%)
  starting transfers between devices  14.8 us (27%)
  waiting for transfers between devices  7.26 us (13%)
  local copies, waits for them, and re-layouts  2.93 us (5%)
    pallas_call x1, Pallas kernels, on_device(): pl.pallas_call(functools.partial(tile_kernel, sizes), out_shape=[jax.Shap...  25 us
    ppermute x3, starting transfers between devices, on_device(): received.append(lax.ppermute(messages[k], 'row', deal[k]))  6.96 us
    ppermute x3, starting transfers between devices, on_device(): arrived.append(lax.ppermute(gains[k], 'row', deal[k]))  4.15 us
    ppermute x3, starting transfers between devices, on_device(): pieces.append(lax.ppermute(own_row, AXES, moves))  3.6 us
    ppermute x3, waiting for transfers between devices, on_device(): arrived.append(lax.ppermute(gains[k], 'row', deal[k]))  3.06 us
    unnamed x10, local copies, waits for them, and re-layouts  2.93 us
    ppermute x3, waiting for transfers between devices, on_device(): pieces.append(lax.ppermute(own_row, AXES, moves))  2.64 us
    pallas_call x1, Pallas kernels, on_device(): pl.pallas_call(functools.partial(list_kernel, sizes), out_shape=[jax.Shap...  2.06 us
  transfers between devices with their start and end apart: 10, of which 6 were waited for; matrix products, arithmetic and copies ran while one was open for 0% of the time, Pallas kernels for 7%

profile of v3, /device:TPU:0, one launch (start us, length us, event | category | flops | bytes accessed | tf_op | source)
XLA Modules:
  0.0 54.9 jit_solution(2742407669092371096)
XLA Ops:
  0.0 0.0 copy-start
  0.0 0.8 %copy-done = f32[4,3,8,128]{3,2,1,0:T(8,128)S(1)} copy-done((f32[4,3,8,128]{3,2,1,0:T(8,128)S(1)}, f32[4,3,8,128]{3,2,1,0:T(8,128)}, u32[]{:S(2)}) %copy-start) | copy-done | bytes 49176
  0.8 0.0 copy-start.3
  0.8 0.7 %copy-done.3 = s32[4,8,1,32]{3,2,1,0:T(1,128)S(1)} copy-done((s32[4,8,1,32]{3,2,1,0:T(1,128)S(1)}, s32[4,8,1,32]{3,2,1,0:T(1,128)}, u32[]{:S(2)}) %copy-start.3) | copy-done | bytes 4120
  1.5 0.0 copy-start.2
  1.5 0.1 pack.1
  1.7 3.0 %collective-permute-start = (f32[40,128]{1,0:T(8,128)S(1)}, f32[40,128]{1,0:T(8,128)S(1)}, u32[]{:S(2)}, u32[]{:S(2)}) collective-permute-start(f32[40,128]{1,0:T(8,128)S(1)} %get-tuple-element.20), channel_id=1, source_target_pairs={{0,8},{4,12},{8,16},{12,20},{16,24},{20,28},{24,0},{28,4},{1,9},{5... | collective-permute-start | bytes 61448 | tf_op jit(solution)/shard_map/ppermute | solution.py:426
  4.7 2.6 %collective-permute-start.1 = (f32[40,128]{1,0:T(8,128)S(1)}, f32[40,128]{1,0:T(8,128)S(1)}, u32[]{:S(2)}, u32[]{:S(2)}) collective-permute-start(f32[40,128]{1,0:T(8,128)S(1)} %get-tuple-element.21), channel_id=1, source_target_pairs={{0,16},{4,20},{8,24},{12,28},{16,0},{20,4},{24,8},{28,12},{1,17},{... | collective-permute-start | bytes 61448 | tf_op jit(solution)/shard_map/ppermute | solution.py:426
  7.3 1.3 %collective-permute-start.2 = (f32[40,128]{1,0:T(8,128)S(1)}, f32[40,128]{1,0:T(8,128)S(1)}, u32[]{:S(2)}, u32[]{:S(2)}) collective-permute-start(f32[40,128]{1,0:T(8,128)S(1)} %get-tuple-element.22), channel_id=1, source_target_pairs={{0,24},{4,28},{8,0},{12,4},{16,8},{20,12},{24,16},{28,20},{1,25},{... | collective-permute-start | bytes 61448 | tf_op jit(solution)/shard_map/ppermute | solution.py:426
  8.6 0.0 copy-start.1
  8.6 0.8 %copy-done.1 = s32[4,1024,2]{1,2,0:T(2,128)S(1)} copy-done((s32[4,1024,2]{1,2,0:T(2,128)S(1)}, s32[4,1024,2]{1,2,0:T(2,128)}, u32[]{:S(2)}) %copy-start.1) | copy-done | bytes 32792
  9.4 0.0 copy-start.4
  9.4 0.7 %copy-done.4 = s32[46]{0:T(128)S(1)} copy-done((s32[46]{0:T(128)S(1)}, s32[46]{0:T(128)}, u32[]{:S(2)}) %copy-start.4) | copy-done | bytes 208
  10.0 2.1 %list_tiles.1 = (s32[42,128]{1,0:T(8,128)S(1)}, s32[2,48,128]{2,1,0:T(8,128)S(1)}) custom-call(s32[46]{0:T(128)S(1)} %copy-done.4, s32[4,2,1024]{2,1,0:T(2,128)S(1)} %bitcast.1), custom_call_target="tpu_custom_call" | custom-call | tf_op jit(solution)/shard_map/list_tiles/pallas_call | solution.py:429
  12.1 0.0 collective-permute-done.refs_1_
  12.1 0.0 collective-permute-done.1.refs_2_
  12.1 0.0 collective-permute-done.2.refs_3_
  12.2 2.5 %collective-permute-start.5 = (f32[136,128]{1,0:T(8,128)S(1)}, f32[136,128]{1,0:T(8,128)S(1)}, u32[]{:S(2)}, u32[]{:S(2)}) collective-permute-start(f32[136,128]{1,0:T(8,128)S(1)} %merge.1.own_ref.refs_0_), channel_id=1, source_target_pairs={{0,6},{1,7},{2,0},{3,1},{4,2},{5,3},{6,4},{7,5},{8,14},{9,15},{10,... | collective-permute-start | bytes 208904 | tf_op jit(solution)/shard_map/ppermute | solution.py:463
  14.7 0.5 collective-permute-start.4
  15.2 0.6 %collective-permute-start.3 = (f32[136,128]{1,0:T(8,128)S(1)}, f32[136,128]{1,0:T(8,128)S(1)}, u32[]{:S(2)}, u32[]{:S(2)}) collective-permute-start(f32[136,128]{1,0:T(8,128)S(1)} %merge.1.own_ref.refs_0_), channel_id=1, source_target_pairs={{0,2},{1,3},{2,4},{3,5},{4,6},{5,7},{6,0},{7,1},{8,10},{9,11},{10,... | collective-permute-start | bytes 208904 | tf_op jit(solution)/shard_map/ppermute | solution.py:463
  15.8 2.0 %own_features.1 = (bf16[64,128,64]{2,1,0:T(8,128)(2,1)S(1)}, bf16[256,48,128]{2,1,0:T(8,128)(2,1)S(1)}) custom-call(s32[2,48,128]{2,1,0:T(8,128)S(1)} %get-tuple-element.18.edges_ref, f32[136,128]{1,0:T(8,128)S(1)} %merge.1.own_ref.refs_0_), custom_call_target="tpu_custom_call" | custom-call | tf_op jit(solution)/shard_map/own_features/pallas_call | solution.py:465
  17.7 0.0 collective-permute-done.5.refs_3_
  17.7 1.2 %collective-permute-done.4.refs_2_ = f32[136,128]{1,0:T(8,128)S(1)} collective-permute-done((f32[136,128]{1,0:T(8,128)S(1)}, f32[136,128]{1,0:T(8,128)S(1)}, u32[]{:S(2)}, u32[]{:S(2)}) %collective-permute-start.4) | collective-permute-done | bytes 69664 | tf_op jit(solution)/shard_map/ppermute | solution.py:463
  19.0 1.4 %collective-permute-done.3.refs_1_ = f32[136,128]{1,0:T(8,128)S(1)} collective-permute-done((f32[136,128]{1,0:T(8,128)S(1)}, f32[136,128]{1,0:T(8,128)S(1)}, u32[]{:S(2)}, u32[]{:S(2)}) %collective-permute-start.3) | collective-permute-done | bytes 69664 | tf_op jit(solution)/shard_map/ppermute | solution.py:463
  20.4 0.1 collective-permute-start.6
  20.5 1.5 %collective-permute-done.6.across_ref = f32[544,128]{1,0:T(8,128)S(1)} collective-permute-done((f32[544,128]{1,0:T(8,128)S(1)}, f32[544,128]{1,0:T(8,128)S(1)}, u32[]{:S(2)}, u32[]{:S(2)}) %collective-permute-start.6) | collective-permute-done | bytes 278560 | tf_op jit(solution)/shard_map/ppermute | solution.py:485
  22.0 0.0 copy-done.2
  22.0 25.0 %tiles.1 = (f32[3,8,128]{2,1,0:T(8,128)S(1)}, f32[3,8,128]{2,1,0:T(8,128)S(1)}, f32[3,8,128]{2,1,0:T(8,128)S(1)}, f32[3,8,128]{2,1,0:T(8,128)S(1)}) custom-call(s32[42,128]{1,0:T(8,128)S(1)} %get-tuple-element.17.after_ref.list_ref, s32[4,1024]{1,0:T(4,128)S(1)} %copy-done.2, bf16[64,128,64]{2,1,0:T(8,128)(2,1)S(1)} %get-tuple-element.23.first_ref, ...), custom_call_target="tpu_custom_call" | custom-call | tf_op jit(solution)/shard_map/tiles/pallas_call | solution.py:487
  47.1 1.6 %collective-permute-start.7 = (f32[3,8,128]{2,1,0:T(8,128)S(1)}, f32[3,8,128]{2,1,0:T(8,128)S(1)}, u32[]{:S(2)}, u32[]{:S(2)}) collective-permute-start(f32[3,8,128]{2,1,0:T(8,128)S(1)} %get-tuple-element.26), channel_id=1, source_target_pairs={{0,8},{4,12},{8,16},{12,20},{16,24},{20,28},{24,0},{28,4},{1,9},{5... | collective-permute-start | bytes 36872 | tf_op jit(solution)/shard_map/ppermute | solution.py:510
  48.6 1.9 %collective-permute-start.8 = (f32[3,8,128]{2,1,0:T(8,128)S(1)}, f32[3,8,128]{2,1,0:T(8,128)S(1)}, u32[]{:S(2)}, u32[]{:S(2)}) collective-permute-start(f32[3,8,128]{2,1,0:T(8,128)S(1)} %get-tuple-element.27), channel_id=1, source_target_pairs={{0,16},{4,20},{8,24},{12,28},{16,0},{20,4},{24,8},{28,12},{1,17},{... | collective-permute-start | bytes 36872 | tf_op jit(solution)/shard_map/ppermute | solution.py:510
  50.6 0.6 %collective-permute-start.9 = (f32[3,8,128]{2,1,0:T(8,128)S(1)}, f32[3,8,128]{2,1,0:T(8,128)S(1)}, u32[]{:S(2)}, u32[]{:S(2)}) collective-permute-start(f32[3,8,128]{2,1,0:T(8,128)S(1)} %get-tuple-element.28), channel_id=1, source_target_pairs={{0,24},{4,28},{8,0},{12,4},{16,8},{20,12},{24,16},{28,20},{1,25},{... | collective-permute-start | bytes 36872 | tf_op jit(solution)/shard_map/ppermute | solution.py:510
  51.2 1.4 %collective-permute-done.7.refs_1_ = f32[3,8,128]{2,1,0:T(8,128)S(1)} collective-permute-done((f32[3,8,128]{2,1,0:T(8,128)S(1)}, f32[3,8,128]{2,1,0:T(8,128)S(1)}, u32[]{:S(2)}, u32[]{:S(2)}) %collective-permute-start.7) | collective-permute-done | bytes 12320 | tf_op jit(solution)/shard_map/ppermute | solution.py:510
  52.6 0.6 %collective-permute-done.8.refs_2_ = f32[3,8,128]{2,1,0:T(8,128)S(1)} collective-permute-done((f32[3,8,128]{2,1,0:T(8,128)S(1)}, f32[3,8,128]{2,1,0:T(8,128)S(1)}, u32[]{:S(2)}, u32[]{:S(2)}) %collective-permute-start.8) | collective-permute-done | bytes 12320 | tf_op jit(solution)/shard_map/ppermute | solution.py:510
  53.2 1.0 %collective-permute-done.9.refs_3_ = f32[3,8,128]{2,1,0:T(8,128)S(1)} collective-permute-done((f32[3,8,128]{2,1,0:T(8,128)S(1)}, f32[3,8,128]{2,1,0:T(8,128)S(1)}, u32[]{:S(2)}, u32[]{:S(2)}) %collective-permute-start.9) | collective-permute-done | bytes 12320 | tf_op jit(solution)/shard_map/ppermute | solution.py:510
  54.3 0.6 %place.1 = f32[4,3,8,128]{3,2,1,0:T(8,128)} custom-call(f32[3,8,128]{2,1,0:T(8,128)S(1)} %get-tuple-element.25.refs_0_, f32[3,8,128]{2,1,0:T(8,128)S(1)} %collective-permute-done.7.refs_1_, f32[3,8,128]{2,1,0:T(8,128)S(1)} %collective-permute-done.8.refs_2_, f32[3,8,128]{2,1,0:T(8,128)S(1)} %collective-permute-done.9.refs_3_), custom_call_target="tpu_custom_call" | custom-call | tf_op jit(solution)/shard_map/place/pallas_call | solution.py:511
  (2 shorter events, 0.0 us)
Async XLA Ops:
  0.0 0.8 %copy-start = (f32[4,3,8,128]{3,2,1,0:T(8,128)S(1)}, f32[4,3,8,128]{3,2,1,0:T(8,128)}, u32[]{:S(2)}) copy-start(f32[4,3,8,128]{3,2,1,0:T(8,128)} %coords_ref.1) | copy-start | bytes 147460
  0.8 0.7 %copy-start.3 = (s32[4,8,1,32]{3,2,1,0:T(1,128)S(1)}, s32[4,8,1,32]{3,2,1,0:T(1,128)}, u32[]{:S(2)}) copy-start(s32[4,8,1,32]{3,2,1,0:T(1,128)} %counts_ref.1) | copy-start | bytes 12292
  1.5 20.5 %copy-start.2 = (s32[4,1024]{1,0:T(4,128)S(1)}, s32[4,1024]{1,0:T(4,128)}, u32[]{:S(2)}) copy-start(s32[4,1024]{1,0:T(4,128)} %listed_ref.1) | copy-start | bytes 49156
  1.7 10.5 %collective-permute-start = (f32[40,128]{1,0:T(8,128)S(1)}, f32[40,128]{1,0:T(8,128)S(1)}, u32[]{:S(2)}, u32[]{:S(2)}) collective-permute-start(f32[40,128]{1,0:T(8,128)S(1)} %get-tuple-element.20), channel_id=1, source_target_pairs={{0,8},{4,12},{8,16},{12,20},{16,24},{20,28},{24,0},{28,4},{1,9},{5... | collective-permute-start | bytes 61448 | tf_op jit(solution)/shard_map/ppermute | solution.py:426
  4.7 7.4 %collective-permute-start.1 = (f32[40,128]{1,0:T(8,128)S(1)}, f32[40,128]{1,0:T(8,128)S(1)}, u32[]{:S(2)}, u32[]{:S(2)}) collective-permute-start(f32[40,128]{1,0:T(8,128)S(1)} %get-tuple-element.21), channel_id=1, source_target_pairs={{0,16},{4,20},{8,24},{12,28},{16,0},{20,4},{24,8},{28,12},{1,17},{... | collective-permute-start | bytes 61448 | tf_op jit(solution)/shard_map/ppermute | solution.py:426
  7.3 4.9 %collective-permute-start.2 = (f32[40,128]{1,0:T(8,128)S(1)}, f32[40,128]{1,0:T(8,128)S(1)}, u32[]{:S(2)}, u32[]{:S(2)}) collective-permute-start(f32[40,128]{1,0:T(8,128)S(1)} %get-tuple-element.22), channel_id=1, source_target_pairs={{0,24},{4,28},{8,0},{12,4},{16,8},{20,12},{24,16},{28,20},{1,25},{... | collective-permute-start | bytes 61448 | tf_op jit(solution)/shard_map/ppermute | solution.py:426
  8.6 0.8 %copy-start.1 = (s32[4,1024,2]{1,2,0:T(2,128)S(1)}, s32[4,1024,2]{1,2,0:T(2,128)}, u32[]{:S(2)}) copy-start(s32[4,1024,2]{1,2,0:T(2,128)} %param.8) | copy-start | bytes 98308
  9.4 0.7 %copy-start.4 = (s32[46]{0:T(128)S(1)}, s32[46]{0:T(128)}, u32[]{:S(2)}) copy-start(s32[46]{0:T(128)} %lengths_ref.1) | copy-start | bytes 556
  12.2 5.6 %collective-permute-start.5 = (f32[136,128]{1,0:T(8,128)S(1)}, f32[136,128]{1,0:T(8,128)S(1)}, u32[]{:S(2)}, u32[]{:S(2)}) collective-permute-start(f32[136,128]{1,0:T(8,128)S(1)} %merge.1.own_ref.refs_0_), channel_id=1, source_target_pairs={{0,6},{1,7},{2,0},{3,1},{4,2},{5,3},{6,4},{7,5},{8,14},{9,15},{10,... | collective-permute-start | bytes 208904 | tf_op jit(solution)/shard_map/ppermute | solution.py:463
  14.7 4.3 %collective-permute-start.4 = (f32[136,128]{1,0:T(8,128)S(1)}, f32[136,128]{1,0:T(8,128)S(1)}, u32[]{:S(2)}, u32[]{:S(2)}) collective-permute-start(f32[136,128]{1,0:T(8,128)S(1)} %merge.1.own_ref.refs_0_), channel_id=1, source_target_pairs={{0,4},{1,5},{2,6},{3,7},{4,0},{5,1},{6,2},{7,3},{8,12},{9,13},{10,... | collective-permute-start | bytes 208904 | tf_op jit(solution)/shard_map/ppermute | solution.py:463
  15.2 5.2 %collective-permute-start.3 = (f32[136,128]{1,0:T(8,128)S(1)}, f32[136,128]{1,0:T(8,128)S(1)}, u32[]{:S(2)}, u32[]{:S(2)}) collective-permute-start(f32[136,128]{1,0:T(8,128)S(1)} %merge.1.own_ref.refs_0_), channel_id=1, source_target_pairs={{0,2},{1,3},{2,4},{3,5},{4,6},{5,7},{6,0},{7,1},{8,10},{9,11},{10,... | collective-permute-start | bytes 208904 | tf_op jit(solution)/shard_map/ppermute | solution.py:463
  20.4 1.6 %collective-permute-start.6 = (f32[544,128]{1,0:T(8,128)S(1)}, f32[544,128]{1,0:T(8,128)S(1)}, u32[]{:S(2)}, u32[]{:S(2)}) collective-permute-start(f32[544,128]{1,0:T(8,128)S(1)} %join.1.same_ref), channel_id=1, source_target_pairs={{0,1},{1,0},{2,3},{3,2},{4,5},{5,4},{6,7},{7,6},{8,9},{9,8},{10,11... | collective-permute-start | bytes 835592 | tf_op jit(solution)/shard_map/ppermute | solution.py:485
  47.1 5.5 %collective-permute-start.7 = (f32[3,8,128]{2,1,0:T(8,128)S(1)}, f32[3,8,128]{2,1,0:T(8,128)S(1)}, u32[]{:S(2)}, u32[]{:S(2)}) collective-permute-start(f32[3,8,128]{2,1,0:T(8,128)S(1)} %get-tuple-element.26), channel_id=1, source_target_pairs={{0,8},{4,12},{8,16},{12,20},{16,24},{20,28},{24,0},{28,4},{1,9},{5... | collective-permute-start | bytes 36872 | tf_op jit(solution)/shard_map/ppermute | solution.py:510
  48.6 4.6 %collective-permute-start.8 = (f32[3,8,128]{2,1,0:T(8,128)S(1)}, f32[3,8,128]{2,1,0:T(8,128)S(1)}, u32[]{:S(2)}, u32[]{:S(2)}) collective-permute-start(f32[3,8,128]{2,1,0:T(8,128)S(1)} %get-tuple-element.27), channel_id=1, source_target_pairs={{0,16},{4,20},{8,24},{12,28},{16,0},{20,4},{24,8},{28,12},{1,17},{... | collective-permute-start | bytes 36872 | tf_op jit(solution)/shard_map/ppermute | solution.py:510
  50.6 3.7 %collective-permute-start.9 = (f32[3,8,128]{2,1,0:T(8,128)S(1)}, f32[3,8,128]{2,1,0:T(8,128)S(1)}, u32[]{:S(2)}, u32[]{:S(2)}) collective-permute-start(f32[3,8,128]{2,1,0:T(8,128)S(1)} %get-tuple-element.28), channel_id=1, source_target_pairs={{0,24},{4,28},{8,0},{12,4},{16,8},{20,12},{24,16},{28,20},{1,25},{... | collective-permute-start | bytes 36872 | tf_op jit(solution)/shard_map/ppermute | solution.py:510

commit v4 on v3

--- a/solution.py
+++ b/solution.py
@@ -10,7 +10,8 @@
 CONTACT_SHIFT = 3.0
 CONTACT_SLOPE = 0.5
 BACKGROUND = 0.5
-FAR = 32.0
+LOG2E = 1.4426950408889634
+FAR = 256.0
 UNIT = 32
 POINT_ROWS = 16
 AXES = ("row", "col")
@@ -63,7 +64,7 @@
             out_ref[pl.ds(place, sweeps, stride=4), :] = point
             high = rounded(point)
             near = high + rounded(point - high)
-            norm = norm - 0.5 * CONTACT_SLOPE * near * near
+            norm = norm + LOG2E * CONTACT_SLOPE * near * near
         out_ref[pl.ds(3, sweeps, stride=4), :] = norm
         counts = counts_ref[member][:, 0, :].astype(jnp.float32)
         out_ref[4 * sweeps : 5 * sweeps] = jnp.dot(counts, spread, preferred_element_type=jnp.float32)
@@ -212,23 +213,26 @@
                 value = pltpu.roll(value, 4, 0) if odd else value
                 high = rounded(value)
                 low = rounded(value - high)
-                shifted = value + 0.5 * CONTACT_SHIFT
+                scaled = -2.0 * LOG2E * CONTACT_SLOPE * (high + low)
+                scaled_high = rounded(scaled)
+                scaled_low = rounded(scaled - scaled_high)
+                shifted = value - LOG2E * CONTACT_SHIFT
                 shifted_high = rounded(shifted)
                 shifted_low = rounded(shifted - shifted_high)
-                both = jnp.where(row < 4, high, pltpu.roll(high, 4, 0))
-                near = jnp.where((row & 3) == 3, 1.0, CONTACT_SLOPE * both)
+                both = jnp.where(row < 4, scaled_high, pltpu.roll(scaled_high, 4, 0))
+                near = jnp.where((row & 3) == 3, 1.0, both)
                 rest = jnp.where(row == 4, pltpu.roll(shifted_low, 1, 0), 0.0)
                 rest = jnp.where(row == 3, shifted_high, rest)
-                rest = jnp.where(row < 3, CONTACT_SLOPE * low, rest)
+                rest = jnp.where(row < 3, scaled_low, rest)
                 u = 2 * pair + odd
                 bead = (u * groups + origin * sizes.plane + here) * 128 + lane
                 inside = (bead >= edges_ref[0]) & (bead < edges_ref[1])
-                apart = jnp.where(inside, 0.0, -FAR)
+                apart = jnp.where(inside, 0.0, FAR)
                 blank = jnp.zeros((128 - depth, 128), jnp.float32)
                 turned = jnp.transpose(jnp.concatenate([near, rest, apart, blank], axis=0))
                 slot = origin * sweeps + u
                 first_ref[slot] = turned[:, :depth].astype(jnp.bfloat16)
-                other = jnp.where(lane < POINT_ROWS, turned, -FAR - turned)
+                other = jnp.where(lane < POINT_ROWS, turned, FAR - turned)
                 first_ref[slots + slot] = other[:, :depth].astype(jnp.bfloat16)
         return carry
 
@@ -298,7 +302,7 @@
         sums = sums_ref[pl.ds(0, UNIT, stride=8), :]
         for k in range(1, 8):
             sums = sums + sums_ref[pl.ds(k, UNIT, stride=8), :]
-        chance = 64.0 * 128.0 + 0.5 * jnp.sum(sums, axis=1, keepdims=True)
+        chance = jnp.sum(sums, axis=1, keepdims=True)
         count = jnp.sum(picks_ref[...], axis=1, keepdims=True)
         state = state_ref[...]
         chance = jnp.where(state == 1.0, 0.5 * (chance - 128.0 * spare), chance)
@@ -317,17 +321,17 @@
             total_ref[ending[t] >> 19] += scale * product
         for t in range(0, UNIT, 2):
             seconds = [beginning[t + i][0] & 4095 for i in range(2)]
-            logit = jnp.dot(
+            power = jnp.dot(
                 first_ref[(beginning[t][0] >> 12) & 127],
                 jnp.concatenate(
                     [jnp.concatenate([second_ref[at], marks_ref[at]], axis=0) for at in seconds], axis=1
                 ),
                 preferred_element_type=jnp.float32,
             )
-            bend = jnp.tanh(logit)
-            held_ref[t // 2] = (1.0 - bend * bend).astype(jnp.bfloat16)
+            chance = pl.reciprocal(1.0 + jnp.exp2(power), approx=True)
+            held_ref[t // 2] = (chance - chance * chance).astype(jnp.bfloat16)
             for i in range(2):
-                part = bend[:, i * 128 : (i + 1) * 128]
+                part = chance[:, i * 128 : (i + 1) * 128]
                 sums_ref[(t + i) * 8 : (t + i + 1) * 8] = jnp.sum(part.reshape(16, 8, 128), axis=0)
                 code, place, state = beginning[t + i]
                 picked = counts_ref[pl.ds(place >> 7, 1), :]
@@ -379,7 +383,7 @@
         return carry
 
     lax.fori_loop(0, slots, collect, 0, unroll=4)
-    scale = -2.0 * CONTACT_SLOPE / 128.0 / 4.0
+    scale = -2.0 * CONTACT_SLOPE / 128.0
     for k in range(structures):
         origin = lax.rem(family + k, structures)
         turn = (structures - k) % structures

time: 54.8 us -> 57.9 us (1.057)
  Pallas kernels: 29.9 us -> 33.7 us
  waiting for transfers between devices: 7.26 us -> 6.61 us
  starting transfers between devices: 14.8 us -> 14.2 us
    pallas_call x1, Pallas kernels: 25 us -> 28.8 us  [on_device(): pl.pallas_call(functools.partial(tile_kernel, sizes), out_shape=[jax.Shap...]
    ppermute x3, waiting for transfers between devices: 3.06 us -> 2.23 us  [on_device(): arrived.append(lax.ppermute(gains[k], 'row', deal[k]))]
  transfers between devices with their start and end apart: 10 -> 10, of which waited for: 6 -> 5; matrix products, arithmetic and copies ran while one was open for 0% -> 0% of each run, Pallas kernels for 7% -> 7%
where the time goes in v4:
time: 57.9 us; the launch traced here: 57.6 us
  Pallas kernels  33.7 us (58%)
  starting transfers between devices  14.2 us (25%)
  waiting for transfers between devices  6.61 us (11%)
  local copies, waits for them, and re-layouts  2.93 us (5%)
    pallas_call x1, Pallas kernels, on_device(): pl.pallas_call(functools.partial(tile_kernel, sizes), out_shape=[jax.Shap...  28.8 us
    ppermute x3, starting transfers between devices, on_device(): received.append(lax.ppermute(messages[k], 'row', deal[k]))  6.96 us
    ppermute x3, starting transfers between devices, on_device(): arrived.append(lax.ppermute(gains[k], 'row', deal[k]))  3.86 us
    ppermute x3, starting transfers between devices, on_device(): pieces.append(lax.ppermute(own_row, AXES, moves))  3.33 us
    unnamed x10, local copies, waits for them, and re-layouts  2.93 us
    ppermute x3, waiting for transfers between devices, on_device(): pieces.append(lax.ppermute(own_row, AXES, moves))  2.82 us
    pallas_call x1, Pallas kernels, on_device(): pl.pallas_call(functools.partial(list_kernel, sizes), out_shape=[jax.Shap...  2.33 us
    ppermute x3, waiting for transfers between devices, on_device(): arrived.append(lax.ppermute(gains[k], 'row', deal[k]))  2.23 us
  transfers between devices with their start and end apart: 10, of which 5 were waited for; matrix products, arithmetic and copies ran while one was open for 0% of the time, Pallas kernels for 7%

profile of v4, /device:TPU:0, one launch (start us, length us, event | category | flops | bytes accessed | tf_op | source)
XLA Modules:
  0.0 57.6 jit_solution(7911402608897421887)
XLA Ops:
  0.0 0.0 copy-start
  0.0 0.8 %copy-done = f32[4,3,8,128]{3,2,1,0:T(8,128)S(1)} copy-done((f32[4,3,8,128]{3,2,1,0:T(8,128)S(1)}, f32[4,3,8,128]{3,2,1,0:T(8,128)}, u32[]{:S(2)}) %copy-start) | copy-done | bytes 49176
  0.8 0.0 copy-start.3
  0.8 0.7 %copy-done.3 = s32[4,8,1,32]{3,2,1,0:T(1,128)S(1)} copy-done((s32[4,8,1,32]{3,2,1,0:T(1,128)S(1)}, s32[4,8,1,32]{3,2,1,0:T(1,128)}, u32[]{:S(2)}) %copy-start.3) | copy-done | bytes 4120
  1.5 0.0 copy-start.2
  1.5 0.1 pack.1
  1.7 3.0 %collective-permute-start = (f32[40,128]{1,0:T(8,128)S(1)}, f32[40,128]{1,0:T(8,128)S(1)}, u32[]{:S(2)}, u32[]{:S(2)}) collective-permute-start(f32[40,128]{1,0:T(8,128)S(1)} %get-tuple-element.20), channel_id=1, source_target_pairs={{0,8},{4,12},{8,16},{12,20},{16,24},{20,28},{24,0},{28,4},{1,9},{5... | collective-permute-start | bytes 61448 | tf_op jit(solution)/shard_map/ppermute | solution.py:430
  4.7 2.6 %collective-permute-start.1 = (f32[40,128]{1,0:T(8,128)S(1)}, f32[40,128]{1,0:T(8,128)S(1)}, u32[]{:S(2)}, u32[]{:S(2)}) collective-permute-start(f32[40,128]{1,0:T(8,128)S(1)} %get-tuple-element.21), channel_id=1, source_target_pairs={{0,16},{4,20},{8,24},{12,28},{16,0},{20,4},{24,8},{28,12},{1,17},{... | collective-permute-start | bytes 61448 | tf_op jit(solution)/shard_map/ppermute | solution.py:430
  7.3 1.3 %collective-permute-start.2 = (f32[40,128]{1,0:T(8,128)S(1)}, f32[40,128]{1,0:T(8,128)S(1)}, u32[]{:S(2)}, u32[]{:S(2)}) collective-permute-start(f32[40,128]{1,0:T(8,128)S(1)} %get-tuple-element.22), channel_id=1, source_target_pairs={{0,24},{4,28},{8,0},{12,4},{16,8},{20,12},{24,16},{28,20},{1,25},{... | collective-permute-start | bytes 61448 | tf_op jit(solution)/shard_map/ppermute | solution.py:430
  8.6 0.0 copy-start.1
  8.6 0.8 %copy-done.1 = s32[4,1024,2]{1,2,0:T(2,128)S(1)} copy-done((s32[4,1024,2]{1,2,0:T(2,128)S(1)}, s32[4,1024,2]{1,2,0:T(2,128)}, u32[]{:S(2)}) %copy-start.1) | copy-done | bytes 32792
  9.4 0.0 copy-start.4
  9.4 0.7 %copy-done.4 = s32[46]{0:T(128)S(1)} copy-done((s32[46]{0:T(128)S(1)}, s32[46]{0:T(128)}, u32[]{:S(2)}) %copy-start.4) | copy-done | bytes 208
  10.0 2.3 %list_tiles.1 = (s32[42,128]{1,0:T(8,128)S(1)}, s32[2,48,128]{2,1,0:T(8,128)S(1)}) custom-call(s32[46]{0:T(128)S(1)} %copy-done.4, s32[4,2,1024]{2,1,0:T(2,128)S(1)} %bitcast.1), custom_call_target="tpu_custom_call" | custom-call | tf_op jit(solution)/shard_map/list_tiles/pallas_call | solution.py:433
  12.4 0.0 collective-permute-done.refs_1_
  12.4 0.0 collective-permute-done.1.refs_2_
  12.4 0.0 collective-permute-done.2.refs_3_
  12.4 2.2 %collective-permute-start.5 = (f32[136,128]{1,0:T(8,128)S(1)}, f32[136,128]{1,0:T(8,128)S(1)}, u32[]{:S(2)}, u32[]{:S(2)}) collective-permute-start(f32[136,128]{1,0:T(8,128)S(1)} %merge.1.own_ref.refs_0_), channel_id=1, source_target_pairs={{0,6},{1,7},{2,0},{3,1},{4,2},{5,3},{6,4},{7,5},{8,14},{9,15},{10,... | collective-permute-start | bytes 208904 | tf_op jit(solution)/shard_map/ppermute | solution.py:467
  14.7 0.5 collective-permute-start.4
  15.2 0.6 %collective-permute-start.3 = (f32[136,128]{1,0:T(8,128)S(1)}, f32[136,128]{1,0:T(8,128)S(1)}, u32[]{:S(2)}, u32[]{:S(2)}) collective-permute-start(f32[136,128]{1,0:T(8,128)S(1)} %merge.1.own_ref.refs_0_), channel_id=1, source_target_pairs={{0,2},{1,3},{2,4},{3,5},{4,6},{5,7},{6,0},{7,1},{8,10},{9,11},{10,... | collective-permute-start | bytes 208904 | tf_op jit(solution)/shard_map/ppermute | solution.py:467
  15.8 1.8 %own_features.1 = (bf16[64,128,64]{2,1,0:T(8,128)(2,1)S(1)}, bf16[256,48,128]{2,1,0:T(8,128)(2,1)S(1)}) custom-call(s32[2,48,128]{2,1,0:T(8,128)S(1)} %get-tuple-element.18.edges_ref, f32[136,128]{1,0:T(8,128)S(1)} %merge.1.own_ref.refs_0_), custom_call_target="tpu_custom_call" | custom-call | tf_op jit(solution)/shard_map/own_features/pallas_call | solution.py:469
  17.5 0.0 collective-permute-done.5.refs_3_
  17.6 1.4 %collective-permute-done.4.refs_2_ = f32[136,128]{1,0:T(8,128)S(1)} collective-permute-done((f32[136,128]{1,0:T(8,128)S(1)}, f32[136,128]{1,0:T(8,128)S(1)}, u32[]{:S(2)}, u32[]{:S(2)}) %collective-permute-start.4) | collective-permute-done | bytes 69664 | tf_op jit(solution)/shard_map/ppermute | solution.py:467
  19.0 1.4 %collective-permute-done.3.refs_1_ = f32[136,128]{1,0:T(8,128)S(1)} collective-permute-done((f32[136,128]{1,0:T(8,128)S(1)}, f32[136,128]{1,0:T(8,128)S(1)}, u32[]{:S(2)}, u32[]{:S(2)}) %collective-permute-start.3) | collective-permute-done | bytes 69664 | tf_op jit(solution)/shard_map/ppermute | solution.py:467
  20.4 0.1 collective-permute-start.6
  20.5 1.5 %collective-permute-done.6.across_ref = f32[544,128]{1,0:T(8,128)S(1)} collective-permute-done((f32[544,128]{1,0:T(8,128)S(1)}, f32[544,128]{1,0:T(8,128)S(1)}, u32[]{:S(2)}, u32[]{:S(2)}) %collective-permute-start.6) | collective-permute-done | bytes 278560 | tf_op jit(solution)/shard_map/ppermute | solution.py:489
  22.0 0.0 copy-done.2
  22.0 28.8 %tiles.1 = (f32[3,8,128]{2,1,0:T(8,128)S(1)}, f32[3,8,128]{2,1,0:T(8,128)S(1)}, f32[3,8,128]{2,1,0:T(8,128)S(1)}, f32[3,8,128]{2,1,0:T(8,128)S(1)}) custom-call(s32[42,128]{1,0:T(8,128)S(1)} %get-tuple-element.17.after_ref.list_ref, s32[4,1024]{1,0:T(4,128)S(1)} %copy-done.2, bf16[64,128,64]{2,1,0:T(8,128)(2,1)S(1)} %get-tuple-element.23.first_ref, ...), custom_call_target="tpu_custom_call" | custom-call | tf_op jit(solution)/shard_map/tiles/pallas_call | solution.py:491
  50.8 0.1 collective-permute-start.7
  50.9 0.1 collective-permute-start.8
  51.0 3.7 %collective-permute-start.9 = (f32[3,8,128]{2,1,0:T(8,128)S(1)}, f32[3,8,128]{2,1,0:T(8,128)S(1)}, u32[]{:S(2)}, u32[]{:S(2)}) collective-permute-start(f32[3,8,128]{2,1,0:T(8,128)S(1)} %get-tuple-element.28), channel_id=1, source_target_pairs={{0,24},{4,28},{8,0},{12,4},{16,8},{20,12},{24,16},{28,20},{1,25},{... | collective-permute-start | bytes 36872 | tf_op jit(solution)/shard_map/ppermute | solution.py:514
  54.7 1.7 %collective-permute-done.7.refs_1_ = f32[3,8,128]{2,1,0:T(8,128)S(1)} collective-permute-done((f32[3,8,128]{2,1,0:T(8,128)S(1)}, f32[3,8,128]{2,1,0:T(8,128)S(1)}, u32[]{:S(2)}, u32[]{:S(2)}) %collective-permute-start.7) | collective-permute-done | bytes 12320 | tf_op jit(solution)/shard_map/ppermute | solution.py:514
  56.4 0.0 collective-permute-done.8.refs_2_
  56.4 0.6 collective-permute-done.9.refs_3_
  57.0 0.6 %place.1 = f32[4,3,8,128]{3,2,1,0:T(8,128)} custom-call(f32[3,8,128]{2,1,0:T(8,128)S(1)} %get-tuple-element.25.refs_0_, f32[3,8,128]{2,1,0:T(8,128)S(1)} %collective-permute-done.7.refs_1_, f32[3,8,128]{2,1,0:T(8,128)S(1)} %collective-permute-done.8.refs_2_, f32[3,8,128]{2,1,0:T(8,128)S(1)} %collective-permute-done.9.refs_3_), custom_call_target="tpu_custom_call" | custom-call | tf_op jit(solution)/shard_map/place/pallas_call | solution.py:515
  (2 shorter events, 0.0 us)
Async XLA Ops:
  0.0 0.8 %copy-start = (f32[4,3,8,128]{3,2,1,0:T(8,128)S(1)}, f32[4,3,8,128]{3,2,1,0:T(8,128)}, u32[]{:S(2)}) copy-start(f32[4,3,8,128]{3,2,1,0:T(8,128)} %coords_ref.1) | copy-start | bytes 147460
  0.8 0.7 %copy-start.3 = (s32[4,8,1,32]{3,2,1,0:T(1,128)S(1)}, s32[4,8,1,32]{3,2,1,0:T(1,128)}, u32[]{:S(2)}) copy-start(s32[4,8,1,32]{3,2,1,0:T(1,128)} %counts_ref.1) | copy-start | bytes 12292
  1.5 20.5 %copy-start.2 = (s32[4,1024]{1,0:T(4,128)S(1)}, s32[4,1024]{1,0:T(4,128)}, u32[]{:S(2)}) copy-start(s32[4,1024]{1,0:T(4,128)} %listed_ref.1) | copy-start | bytes 49156
  1.7 10.7 %collective-permute-start = (f32[40,128]{1,0:T(8,128)S(1)}, f32[40,128]{1,0:T(8,128)S(1)}, u32[]{:S(2)}, u32[]{:S(2)}) collective-permute-start(f32[40,128]{1,0:T(8,128)S(1)} %get-tuple-element.20), channel_id=1, source_target_pairs={{0,8},{4,12},{8,16},{12,20},{16,24},{20,28},{24,0},{28,4},{1,9},{5... | collective-permute-start | bytes 61448 | tf_op jit(solution)/shard_map/ppermute | solution.py:430
  4.7 7.7 %collective-permute-start.1 = (f32[40,128]{1,0:T(8,128)S(1)}, f32[40,128]{1,0:T(8,128)S(1)}, u32[]{:S(2)}, u32[]{:S(2)}) collective-permute-start(f32[40,128]{1,0:T(8,128)S(1)} %get-tuple-element.21), channel_id=1, source_target_pairs={{0,16},{4,20},{8,24},{12,28},{16,0},{20,4},{24,8},{28,12},{1,17},{... | collective-permute-start | bytes 61448 | tf_op jit(solution)/shard_map/ppermute | solution.py:430
  7.3 5.1 %collective-permute-start.2 = (f32[40,128]{1,0:T(8,128)S(1)}, f32[40,128]{1,0:T(8,128)S(1)}, u32[]{:S(2)}, u32[]{:S(2)}) collective-permute-start(f32[40,128]{1,0:T(8,128)S(1)} %get-tuple-element.22), channel_id=1, source_target_pairs={{0,24},{4,28},{8,0},{12,4},{16,8},{20,12},{24,16},{28,20},{1,25},{... | collective-permute-start | bytes 61448 | tf_op jit(solution)/shard_map/ppermute | solution.py:430
  8.6 0.8 %copy-start.1 = (s32[4,1024,2]{1,2,0:T(2,128)S(1)}, s32[4,1024,2]{1,2,0:T(2,128)}, u32[]{:S(2)}) copy-start(s32[4,1024,2]{1,2,0:T(2,128)} %param.8) | copy-start | bytes 98308
  9.4 0.7 %copy-start.4 = (s32[46]{0:T(128)S(1)}, s32[46]{0:T(128)}, u32[]{:S(2)}) copy-start(s32[46]{0:T(128)} %lengths_ref.1) | copy-start | bytes 556
  12.4 5.1 %collective-permute-start.5 = (f32[136,128]{1,0:T(8,128)S(1)}, f32[136,128]{1,0:T(8,128)S(1)}, u32[]{:S(2)}, u32[]{:S(2)}) collective-permute-start(f32[136,128]{1,0:T(8,128)S(1)} %merge.1.own_ref.refs_0_), channel_id=1, source_target_pairs={{0,6},{1,7},{2,0},{3,1},{4,2},{5,3},{6,4},{7,5},{8,14},{9,15},{10,... | collective-permute-start | bytes 208904 | tf_op jit(solution)/shard_map/ppermute | solution.py:467
  14.7 4.3 %collective-permute-start.4 = (f32[136,128]{1,0:T(8,128)S(1)}, f32[136,128]{1,0:T(8,128)S(1)}, u32[]{:S(2)}, u32[]{:S(2)}) collective-permute-start(f32[136,128]{1,0:T(8,128)S(1)} %merge.1.own_ref.refs_0_), channel_id=1, source_target_pairs={{0,4},{1,5},{2,6},{3,7},{4,0},{5,1},{6,2},{7,3},{8,12},{9,13},{10,... | collective-permute-start | bytes 208904 | tf_op jit(solution)/shard_map/ppermute | solution.py:467
  15.2 5.2 %collective-permute-start.3 = (f32[136,128]{1,0:T(8,128)S(1)}, f32[136,128]{1,0:T(8,128)S(1)}, u32[]{:S(2)}, u32[]{:S(2)}) collective-permute-start(f32[136,128]{1,0:T(8,128)S(1)} %merge.1.own_ref.refs_0_), channel_id=1, source_target_pairs={{0,2},{1,3},{2,4},{3,5},{4,6},{5,7},{6,0},{7,1},{8,10},{9,11},{10,... | collective-permute-start | bytes 208904 | tf_op jit(solution)/shard_map/ppermute | solution.py:467
  20.4 1.6 %collective-permute-start.6 = (f32[544,128]{1,0:T(8,128)S(1)}, f32[544,128]{1,0:T(8,128)S(1)}, u32[]{:S(2)}, u32[]{:S(2)}) collective-permute-start(f32[544,128]{1,0:T(8,128)S(1)} %join.1.same_ref), channel_id=1, source_target_pairs={{0,1},{1,0},{2,3},{3,2},{4,5},{5,4},{6,7},{7,6},{8,9},{9,8},{10,11... | collective-permute-start | bytes 835592 | tf_op jit(solution)/shard_map/ppermute | solution.py:489
  50.8 5.5 %collective-permute-start.7 = (f32[3,8,128]{2,1,0:T(8,128)S(1)}, f32[3,8,128]{2,1,0:T(8,128)S(1)}, u32[]{:S(2)}, u32[]{:S(2)}) collective-permute-start(f32[3,8,128]{2,1,0:T(8,128)S(1)} %get-tuple-element.26), channel_id=1, source_target_pairs={{0,8},{4,12},{8,16},{12,20},{16,24},{20,28},{24,0},{28,4},{1,9},{5... | collective-permute-start | bytes 36872 | tf_op jit(solution)/shard_map/ppermute | solution.py:514
  50.9 5.5 %collective-permute-start.8 = (f32[3,8,128]{2,1,0:T(8,128)S(1)}, f32[3,8,128]{2,1,0:T(8,128)S(1)}, u32[]{:S(2)}, u32[]{:S(2)}) collective-permute-start(f32[3,8,128]{2,1,0:T(8,128)S(1)} %get-tuple-element.27), channel_id=1, source_target_pairs={{0,16},{4,20},{8,24},{12,28},{16,0},{20,4},{24,8},{28,12},{1,17},{... | collective-permute-start | bytes 36872 | tf_op jit(solution)/shard_map/ppermute | solution.py:514
  51.0 6.0 %collective-permute-start.9 = (f32[3,8,128]{2,1,0:T(8,128)S(1)}, f32[3,8,128]{2,1,0:T(8,128)S(1)}, u32[]{:S(2)}, u32[]{:S(2)}) collective-permute-start(f32[3,8,128]{2,1,0:T(8,128)S(1)} %get-tuple-element.28), channel_id=1, source_target_pairs={{0,24},{4,28},{8,0},{12,4},{16,8},{20,12},{24,16},{28,20},{1,25},{... | collective-permute-start | bytes 36872 | tf_op jit(solution)/shard_map/ppermute | solution.py:514

commit v5 on v3

--- a/solution.py
+++ b/solution.py
@@ -238,9 +238,7 @@
 def tile_kernel(sizes, list_ref, listed_ref, first_ref, marks_ref, same_ref, across_ref, *refs):
     structures, sweeps, slots = sizes.structures, sizes.sweeps, sizes.slots
     out_refs = refs[:structures]
-    second_ref, turned_ref, mask_ref, counts_ref, held_ref, sums_ref, picks_ref, state_ref, total_ref, gain_ref = refs[
-        structures:
-    ]
+    second_ref, counts_ref, held_ref, sums_ref, picks_ref, state_ref, total_ref, gain_ref = refs[structures:]
     row_here = lax.axis_index("row")
     column_here = lax.axis_index("col")
     family = lax.div(row_here, sizes.share)
@@ -249,9 +247,7 @@
     lane = lax.broadcasted_iota(jnp.int32, (1, 128), 1)
     row = lax.broadcasted_iota(jnp.int32, (8, 128), 0)
     ones = jnp.where((row == 3) | (row == 4), 1.0, 0.0)
-    unit = jnp.where(row == 3, 1.0, 0.0)
-    for k in range(2 * sweeps):
-        mask_ref[k] = jnp.broadcast_to(lane >> 3 == k, (16, 128)).astype(jnp.float32).astype(jnp.bfloat16)
+    narrow = lax.broadcasted_iota(jnp.int32, (1, 2 * POINT_ROWS), 1)
 
     for core, piece_ref in ((core_here, same_ref), (1 - core_here, across_ref)):
         for k in range(sizes.chips):
@@ -264,7 +260,6 @@
             for turn in range(structures):
                 origin = lax.rem(family + (structures - turn), structures)
                 group = origin * sizes.plane + device
-                columns = []
                 for pair in range(sweeps // 2):
                     start = base + turn * sweeps * 4 + pair * 8
                     value = piece_ref[start : start + 8]
@@ -277,8 +272,6 @@
                         points = jnp.where(row < 4, top, bottom)
                         features = jnp.concatenate([points, jnp.where(row < 3, top, ones)], axis=0)
                         second_ref[group * sweeps + 2 * pair + odd] = features.astype(jnp.bfloat16)
-                        columns.append(jnp.where((row & 3) == 3, unit, points))
-                turned_ref[group] = jnp.transpose(jnp.concatenate(columns * 2, axis=0)).astype(jnp.bfloat16)
     listed_base = sizes.plane * sweeps
     chosen = lax.broadcasted_iota(jnp.int32, (structures, 128), 0) == family
     for k in range(listed_ref.shape[1] // 128):
@@ -304,16 +297,19 @@
         chance = jnp.where(state == 1.0, 0.5 * (chance - 128.0 * spare), chance)
         weight = jnp.where(state == 2.0, 0.0, 1.0 - count / (BACKGROUND + chance / 128.0))
         for t in range(0, UNIT, 2):
-            columns = []
-            for i in range(2):
-                at = ending[t + i] & 4095
-                mask = mask_ref[modulo(at, sweeps) + i * sweeps]
-                column = turned_ref[divide(at, sweeps)].reshape(8, 16, 128) * mask[None]
-                columns.append(column.reshape(128, 128))
-            product = jnp.dot(
-                held_ref[t // 2], jnp.concatenate(columns, axis=0), preferred_element_type=jnp.float32
-            )
-            scale = jnp.where(lane < 64, weight[t : t + 1], weight[t + 1 : t + 2])
+            left, right = (second_ref[ending[t + i] & 4095] for i in range(2))
+            blank = jnp.zeros_like(left)
+            both = jnp.concatenate(
+                [jnp.concatenate([left, blank], axis=1), jnp.concatenate([blank, right], axis=1)], axis=0
+            )
+            product = lax.dot_general(
+                held_ref[t // 2], both, (((1,), (1,)), ((), ())), preferred_element_type=jnp.float32
+            )
+            scale = jnp.where(
+                narrow < POINT_ROWS,
+                weight[t : t + 1, : 2 * POINT_ROWS],
+                weight[t + 1 : t + 2, : 2 * POINT_ROWS],
+            )
             total_ref[ending[t] >> 19] += scale * product
         for t in range(0, UNIT, 2):
             seconds = [beginning[t + i][0] & 4095 for i in range(2)]
@@ -375,7 +371,9 @@
 
     def collect(slot, carry):
         turned = jnp.transpose(total_ref[slot])
-        gain_ref[pl.ds(pl.multiple_of(slot * 8, 8), 8), :] = jnp.sum(turned.reshape(16, 8, 128), axis=0)
+        gain_ref[pl.ds(pl.multiple_of(slot * POINT_ROWS, POINT_ROWS), POINT_ROWS), :] = (
+            turned[:POINT_ROWS] + turned[POINT_ROWS:]
+        )
         return carry
 
     lax.fori_loop(0, slots, collect, 0, unroll=4)
@@ -383,15 +381,15 @@
     for k in range(structures):
         origin = lax.rem(family + k, structures)
         turn = (structures - k) % structures
-        first = origin * sweeps * 8
-        mass = gain_ref[pl.ds(first + 3, sweeps, stride=8), :]
+        first = origin * sweeps * POINT_ROWS
+        mass = gain_ref[pl.ds(first + 11, sweeps, stride=POINT_ROWS), :]
         for place in range(3):
             point = same_ref[pl.ds(turn * sweeps * 4 + place, sweeps, stride=4), :]
             high = rounded(point)
             near = high + rounded(point - high)
             pull = (
-                gain_ref[pl.ds(first + place, sweeps, stride=8), :]
-                + gain_ref[pl.ds(first + place + 4, sweeps, stride=8), :]
+                gain_ref[pl.ds(first + place, sweeps, stride=POINT_ROWS), :]
+                + gain_ref[pl.ds(first + place + 4, sweeps, stride=POINT_ROWS), :]
             )
             out_refs[k][place] = scale * (near * mass - pull)
 
@@ -491,15 +489,13 @@
         out_specs=[VMEM] * structures,
         scratch_shapes=[
             pltpu.VMEM((blocks, POINT_ROWS, block_size), jnp.bfloat16),
-            pltpu.VMEM((sizes.groups, block_size, block_size), jnp.bfloat16),
-            pltpu.VMEM((2 * sweeps, POINT_ROWS, block_size), jnp.bfloat16),
             pltpu.VMEM((sizes.plane * sweeps + listed // block_size, block_size), jnp.float32),
             pltpu.VMEM((UNIT // 2, block_size, 2 * block_size), jnp.bfloat16),
             pltpu.VMEM((UNIT * 8, block_size), jnp.float32),
             pltpu.VMEM((UNIT, block_size), jnp.float32),
             pltpu.VMEM((UNIT, block_size), jnp.float32),
-            pltpu.VMEM((slots + 1, block_size, block_size), jnp.float32),
-            pltpu.VMEM((slots * 8, block_size), jnp.float32),
+            pltpu.VMEM((slots + 1, block_size, 2 * POINT_ROWS), jnp.float32),
+            pltpu.VMEM((slots * POINT_ROWS, block_size), jnp.float32),
         ],
         compiler_params=pltpu.CompilerParams(vmem_limit_bytes=40 * 1024 * 1024),
         name="tiles",

time: 54.8 us -> 52.1 us (0.951); the launches traced: 54.9 us -> 51.5 us
  Pallas kernels: 29.9 us -> 27.3 us
  waiting for transfers between devices: 7.26 us -> 6.69 us
    pallas_call x1, Pallas kernels: 25 us -> 22.5 us  [on_device(): pl.pallas_call(functools.partial(tile_kernel, sizes), out_shape=[jax.Shap...]
    ppermute x3, waiting for transfers between devices: 3.06 us -> 2.5 us  [on_device(): arrived.append(lax.ppermute(gains[k], 'row', deal[k]))]
  transfers between devices with their start and end apart: 10 -> 10, of which waited for: 6 -> 5; matrix products, arithmetic and copies ran while one was open for 0% -> 0% of each run, Pallas kernels for 7% -> 8%
where the time goes in v5:
time: 52.1 us; the launch traced here: 51.5 us
  Pallas kernels  27.3 us (52%)
  starting transfers between devices  14.5 us (28%)
  waiting for transfers between devices  6.69 us (13%)
  local copies, waits for them, and re-layouts  2.93 us (6%)
    pallas_call x1, Pallas kernels, on_device(): pl.pallas_call(functools.partial(tile_kernel, sizes), out_shape=[jax.Shap...  22.5 us
    ppermute x3, starting transfers between devices, on_device(): received.append(lax.ppermute(messages[k], 'row', deal[k]))  6.96 us
    ppermute x3, starting transfers between devices, on_device(): arrived.append(lax.ppermute(gains[k], 'row', deal[k]))  3.88 us
    ppermute x3, starting transfers between devices, on_device(): pieces.append(lax.ppermute(own_row, AXES, moves))  3.6 us
    unnamed x10, local copies, waits for them, and re-layouts  2.93 us
    ppermute x3, waiting for transfers between devices, on_device(): pieces.append(lax.ppermute(own_row, AXES, moves))  2.64 us
    ppermute x3, waiting for transfers between devices, on_device(): arrived.append(lax.ppermute(gains[k], 'row', deal[k]))  2.5 us
    pallas_call x1, Pallas kernels, on_device(): pl.pallas_call(functools.partial(list_kernel, sizes), out_shape=[jax.Shap...  2.06 us
  transfers between devices with their start and end apart: 10, of which 5 were waited for; matrix products, arithmetic and copies ran while one was open for 0% of the time, Pallas kernels for 8%

profile of v5, /device:TPU:0, one launch (start us, length us, event | category | flops | bytes accessed | tf_op | source)
XLA Modules:
  0.0 51.5 jit_solution(3250318747049672933)
XLA Ops:
  0.0 0.0 copy-start
  0.0 0.8 %copy-done = f32[4,3,8,128]{3,2,1,0:T(8,128)S(1)} copy-done((f32[4,3,8,128]{3,2,1,0:T(8,128)S(1)}, f32[4,3,8,128]{3,2,1,0:T(8,128)}, u32[]{:S(2)}) %copy-start) | copy-done | bytes 49176
  0.8 0.0 copy-start.3
  0.8 0.7 %copy-done.3 = s32[4,8,1,32]{3,2,1,0:T(1,128)S(1)} copy-done((s32[4,8,1,32]{3,2,1,0:T(1,128)S(1)}, s32[4,8,1,32]{3,2,1,0:T(1,128)}, u32[]{:S(2)}) %copy-start.3) | copy-done | bytes 4120
  1.5 0.0 copy-start.2
  1.5 0.1 pack.1
  1.7 3.0 %collective-permute-start = (f32[40,128]{1,0:T(8,128)S(1)}, f32[40,128]{1,0:T(8,128)S(1)}, u32[]{:S(2)}, u32[]{:S(2)}) collective-permute-start(f32[40,128]{1,0:T(8,128)S(1)} %get-tuple-element.20), channel_id=1, source_target_pairs={{0,8},{4,12},{8,16},{12,20},{16,24},{20,28},{24,0},{28,4},{1,9},{5... | collective-permute-start | bytes 61448 | tf_op jit(solution)/shard_map/ppermute | solution.py:424
  4.7 2.6 %collective-permute-start.1 = (f32[40,128]{1,0:T(8,128)S(1)}, f32[40,128]{1,0:T(8,128)S(1)}, u32[]{:S(2)}, u32[]{:S(2)}) collective-permute-start(f32[40,128]{1,0:T(8,128)S(1)} %get-tuple-element.21), channel_id=1, source_target_pairs={{0,16},{4,20},{8,24},{12,28},{16,0},{20,4},{24,8},{28,12},{1,17},{... | collective-permute-start | bytes 61448 | tf_op jit(solution)/shard_map/ppermute | solution.py:424
  7.3 1.3 %collective-permute-start.2 = (f32[40,128]{1,0:T(8,128)S(1)}, f32[40,128]{1,0:T(8,128)S(1)}, u32[]{:S(2)}, u32[]{:S(2)}) collective-permute-start(f32[40,128]{1,0:T(8,128)S(1)} %get-tuple-element.22), channel_id=1, source_target_pairs={{0,24},{4,28},{8,0},{12,4},{16,8},{20,12},{24,16},{28,20},{1,25},{... | collective-permute-start | bytes 61448 | tf_op jit(solution)/shard_map/ppermute | solution.py:424
  8.6 0.0 copy-start.1
  8.6 0.8 %copy-done.1 = s32[4,1024,2]{1,2,0:T(2,128)S(1)} copy-done((s32[4,1024,2]{1,2,0:T(2,128)S(1)}, s32[4,1024,2]{1,2,0:T(2,128)}, u32[]{:S(2)}) %copy-start.1) | copy-done | bytes 32792
  9.4 0.0 copy-start.4
  9.4 0.7 %copy-done.4 = s32[46]{0:T(128)S(1)} copy-done((s32[46]{0:T(128)S(1)}, s32[46]{0:T(128)}, u32[]{:S(2)}) %copy-start.4) | copy-done | bytes 208
  10.0 2.1 %list_tiles.1 = (s32[42,128]{1,0:T(8,128)S(1)}, s32[2,48,128]{2,1,0:T(8,128)S(1)}) custom-call(s32[46]{0:T(128)S(1)} %copy-done.4, s32[4,2,1024]{2,1,0:T(2,128)S(1)} %bitcast.1), custom_call_target="tpu_custom_call" | custom-call | tf_op jit(solution)/shard_map/list_tiles/pallas_call | solution.py:427
  12.1 0.0 collective-permute-done.refs_1_
  12.1 0.0 collective-permute-done.1.refs_2_
  12.1 0.0 collective-permute-done.2.refs_3_
  12.2 2.5 %collective-permute-start.5 = (f32[136,128]{1,0:T(8,128)S(1)}, f32[136,128]{1,0:T(8,128)S(1)}, u32[]{:S(2)}, u32[]{:S(2)}) collective-permute-start(f32[136,128]{1,0:T(8,128)S(1)} %merge.1.own_ref.refs_0_), channel_id=1, source_target_pairs={{0,6},{1,7},{2,0},{3,1},{4,2},{5,3},{6,4},{7,5},{8,14},{9,15},{10,... | collective-permute-start | bytes 208904 | tf_op jit(solution)/shard_map/ppermute | solution.py:461
  14.7 0.5 collective-permute-start.4
  15.2 0.6 %collective-permute-start.3 = (f32[136,128]{1,0:T(8,128)S(1)}, f32[136,128]{1,0:T(8,128)S(1)}, u32[]{:S(2)}, u32[]{:S(2)}) collective-permute-start(f32[136,128]{1,0:T(8,128)S(1)} %merge.1.own_ref.refs_0_), channel_id=1, source_target_pairs={{0,2},{1,3},{2,4},{3,5},{4,6},{5,7},{6,0},{7,1},{8,10},{9,11},{10,... | collective-permute-start | bytes 208904 | tf_op jit(solution)/shard_map/ppermute | solution.py:461
  15.8 2.0 %own_features.1 = (bf16[64,128,64]{2,1,0:T(8,128)(2,1)S(1)}, bf16[256,48,128]{2,1,0:T(8,128)(2,1)S(1)}) custom-call(s32[2,48,128]{2,1,0:T(8,128)S(1)} %get-tuple-element.18.edges_ref, f32[136,128]{1,0:T(8,128)S(1)} %merge.1.own_ref.refs_0_), custom_call_target="tpu_custom_call" | custom-call | tf_op jit(solution)/shard_map/own_features/pallas_call | solution.py:463
  17.7 0.0 collective-permute-done.5.refs_3_
  17.7 1.2 %collective-permute-done.4.refs_2_ = f32[136,128]{1,0:T(8,128)S(1)} collective-permute-done((f32[136,128]{1,0:T(8,128)S(1)}, f32[136,128]{1,0:T(8,128)S(1)}, u32[]{:S(2)}, u32[]{:S(2)}) %collective-permute-start.4) | collective-permute-done | bytes 69664 | tf_op jit(solution)/shard_map/ppermute | solution.py:461
  19.0 1.4 %collective-permute-done.3.refs_1_ = f32[136,128]{1,0:T(8,128)S(1)} collective-permute-done((f32[136,128]{1,0:T(8,128)S(1)}, f32[136,128]{1,0:T(8,128)S(1)}, u32[]{:S(2)}, u32[]{:S(2)}) %collective-permute-start.3) | collective-permute-done | bytes 69664 | tf_op jit(solution)/shard_map/ppermute | solution.py:461
  20.4 0.1 collective-permute-start.6
  20.5 1.5 %collective-permute-done.6.across_ref = f32[544,128]{1,0:T(8,128)S(1)} collective-permute-done((f32[544,128]{1,0:T(8,128)S(1)}, f32[544,128]{1,0:T(8,128)S(1)}, u32[]{:S(2)}, u32[]{:S(2)}) %collective-permute-start.6) | collective-permute-done | bytes 278560 | tf_op jit(solution)/shard_map/ppermute | solution.py:483
  22.0 0.0 copy-done.2
  22.0 22.5 %tiles.1 = (f32[3,8,128]{2,1,0:T(8,128)S(1)}, f32[3,8,128]{2,1,0:T(8,128)S(1)}, f32[3,8,128]{2,1,0:T(8,128)S(1)}, f32[3,8,128]{2,1,0:T(8,128)S(1)}) custom-call(s32[42,128]{1,0:T(8,128)S(1)} %get-tuple-element.17.after_ref.list_ref, s32[4,1024]{1,0:T(4,128)S(1)} %copy-done.2, bf16[64,128,64]{2,1,0:T(8,128)(2,1)S(1)} %get-tuple-element.23.first_ref, ...), custom_call_target="tpu_custom_call" | custom-call | tf_op jit(solution)/shard_map/tiles/pallas_call | solution.py:485
  44.5 0.8 %collective-permute-start.7 = (f32[3,8,128]{2,1,0:T(8,128)S(1)}, f32[3,8,128]{2,1,0:T(8,128)S(1)}, u32[]{:S(2)}, u32[]{:S(2)}) collective-permute-start(f32[3,8,128]{2,1,0:T(8,128)S(1)} %get-tuple-element.26), channel_id=1, source_target_pairs={{0,8},{4,12},{8,16},{12,20},{16,24},{20,28},{24,0},{28,4},{1,9},{5... | collective-permute-start | bytes 36872 | tf_op jit(solution)/shard_map/ppermute | solution.py:506
  45.3 1.9 %collective-permute-start.8 = (f32[3,8,128]{2,1,0:T(8,128)S(1)}, f32[3,8,128]{2,1,0:T(8,128)S(1)}, u32[]{:S(2)}, u32[]{:S(2)}) collective-permute-start(f32[3,8,128]{2,1,0:T(8,128)S(1)} %get-tuple-element.27), channel_id=1, source_target_pairs={{0,16},{4,20},{8,24},{12,28},{16,0},{20,4},{24,8},{28,12},{1,17},{... | collective-permute-start | bytes 36872 | tf_op jit(solution)/shard_map/ppermute | solution.py:506
  47.2 1.2 %collective-permute-start.9 = (f32[3,8,128]{2,1,0:T(8,128)S(1)}, f32[3,8,128]{2,1,0:T(8,128)S(1)}, u32[]{:S(2)}, u32[]{:S(2)}) collective-permute-start(f32[3,8,128]{2,1,0:T(8,128)S(1)} %get-tuple-element.28), channel_id=1, source_target_pairs={{0,24},{4,28},{8,0},{12,4},{16,8},{20,12},{24,16},{28,20},{1,25},{... | collective-permute-start | bytes 36872 | tf_op jit(solution)/shard_map/ppermute | solution.py:506
  48.4 1.7 %collective-permute-done.7.refs_1_ = f32[3,8,128]{2,1,0:T(8,128)S(1)} collective-permute-done((f32[3,8,128]{2,1,0:T(8,128)S(1)}, f32[3,8,128]{2,1,0:T(8,128)S(1)}, u32[]{:S(2)}, u32[]{:S(2)}) %collective-permute-start.7) | collective-permute-done | bytes 12320 | tf_op jit(solution)/shard_map/ppermute | solution.py:506
  50.1 0.0 collective-permute-done.8.refs_2_
  50.1 0.8 %collective-permute-done.9.refs_3_ = f32[3,8,128]{2,1,0:T(8,128)S(1)} collective-permute-done((f32[3,8,128]{2,1,0:T(8,128)S(1)}, f32[3,8,128]{2,1,0:T(8,128)S(1)}, u32[]{:S(2)}, u32[]{:S(2)}) %collective-permute-start.9) | collective-permute-done | bytes 12320 | tf_op jit(solution)/shard_map/ppermute | solution.py:506
  50.9 0.6 %place.1 = f32[4,3,8,128]{3,2,1,0:T(8,128)} custom-call(f32[3,8,128]{2,1,0:T(8,128)S(1)} %get-tuple-element.25.refs_0_, f32[3,8,128]{2,1,0:T(8,128)S(1)} %collective-permute-done.7.refs_1_, f32[3,8,128]{2,1,0:T(8,128)S(1)} %collective-permute-done.8.refs_2_, f32[3,8,128]{2,1,0:T(8,128)S(1)} %collective-permute-done.9.refs_3_), custom_call_target="tpu_custom_call" | custom-call | tf_op jit(solution)/shard_map/place/pallas_call | solution.py:507
  (2 shorter events, 0.0 us)
Async XLA Ops:
  0.0 0.8 %copy-start = (f32[4,3,8,128]{3,2,1,0:T(8,128)S(1)}, f32[4,3,8,128]{3,2,1,0:T(8,128)}, u32[]{:S(2)}) copy-start(f32[4,3,8,128]{3,2,1,0:T(8,128)} %coords_ref.1) | copy-start | bytes 147460
  0.8 0.7 %copy-start.3 = (s32[4,8,1,32]{3,2,1,0:T(1,128)S(1)}, s32[4,8,1,32]{3,2,1,0:T(1,128)}, u32[]{:S(2)}) copy-start(s32[4,8,1,32]{3,2,1,0:T(1,128)} %counts_ref.1) | copy-start | bytes 12292
  1.5 20.5 %copy-start.2 = (s32[4,1024]{1,0:T(4,128)S(1)}, s32[4,1024]{1,0:T(4,128)}, u32[]{:S(2)}) copy-start(s32[4,1024]{1,0:T(4,128)} %listed_ref.1) | copy-start | bytes 49156
  1.7 10.5 %collective-permute-start = (f32[40,128]{1,0:T(8,128)S(1)}, f32[40,128]{1,0:T(8,128)S(1)}, u32[]{:S(2)}, u32[]{:S(2)}) collective-permute-start(f32[40,128]{1,0:T(8,128)S(1)} %get-tuple-element.20), channel_id=1, source_target_pairs={{0,8},{4,12},{8,16},{12,20},{16,24},{20,28},{24,0},{28,4},{1,9},{5... | collective-permute-start | bytes 61448 | tf_op jit(solution)/shard_map/ppermute | solution.py:424
  4.7 7.4 %collective-permute-start.1 = (f32[40,128]{1,0:T(8,128)S(1)}, f32[40,128]{1,0:T(8,128)S(1)}, u32[]{:S(2)}, u32[]{:S(2)}) collective-permute-start(f32[40,128]{1,0:T(8,128)S(1)} %get-tuple-element.21), channel_id=1, source_target_pairs={{0,16},{4,20},{8,24},{12,28},{16,0},{20,4},{24,8},{28,12},{1,17},{... | collective-permute-start | bytes 61448 | tf_op jit(solution)/shard_map/ppermute | solution.py:424
  7.3 4.9 %collective-permute-start.2 = (f32[40,128]{1,0:T(8,128)S(1)}, f32[40,128]{1,0:T(8,128)S(1)}, u32[]{:S(2)}, u32[]{:S(2)}) collective-permute-start(f32[40,128]{1,0:T(8,128)S(1)} %get-tuple-element.22), channel_id=1, source_target_pairs={{0,24},{4,28},{8,0},{12,4},{16,8},{20,12},{24,16},{28,20},{1,25},{... | collective-permute-start | bytes 61448 | tf_op jit(solution)/shard_map/ppermute | solution.py:424
  8.6 0.8 %copy-start.1 = (s32[4,1024,2]{1,2,0:T(2,128)S(1)}, s32[4,1024,2]{1,2,0:T(2,128)}, u32[]{:S(2)}) copy-start(s32[4,1024,2]{1,2,0:T(2,128)} %param.8) | copy-start | bytes 98308
  9.4 0.7 %copy-start.4 = (s32[46]{0:T(128)S(1)}, s32[46]{0:T(128)}, u32[]{:S(2)}) copy-start(s32[46]{0:T(128)} %lengths_ref.1) | copy-start | bytes 556
  12.2 5.6 %collective-permute-start.5 = (f32[136,128]{1,0:T(8,128)S(1)}, f32[136,128]{1,0:T(8,128)S(1)}, u32[]{:S(2)}, u32[]{:S(2)}) collective-permute-start(f32[136,128]{1,0:T(8,128)S(1)} %merge.1.own_ref.refs_0_), channel_id=1, source_target_pairs={{0,6},{1,7},{2,0},{3,1},{4,2},{5,3},{6,4},{7,5},{8,14},{9,15},{10,... | collective-permute-start | bytes 208904 | tf_op jit(solution)/shard_map/ppermute | solution.py:461
  14.7 4.3 %collective-permute-start.4 = (f32[136,128]{1,0:T(8,128)S(1)}, f32[136,128]{1,0:T(8,128)S(1)}, u32[]{:S(2)}, u32[]{:S(2)}) collective-permute-start(f32[136,128]{1,0:T(8,128)S(1)} %merge.1.own_ref.refs_0_), channel_id=1, source_target_pairs={{0,4},{1,5},{2,6},{3,7},{4,0},{5,1},{6,2},{7,3},{8,12},{9,13},{10,... | collective-permute-start | bytes 208904 | tf_op jit(solution)/shard_map/ppermute | solution.py:461
  15.2 5.2 %collective-permute-start.3 = (f32[136,128]{1,0:T(8,128)S(1)}, f32[136,128]{1,0:T(8,128)S(1)}, u32[]{:S(2)}, u32[]{:S(2)}) collective-permute-start(f32[136,128]{1,0:T(8,128)S(1)} %merge.1.own_ref.refs_0_), channel_id=1, source_target_pairs={{0,2},{1,3},{2,4},{3,5},{4,6},{5,7},{6,0},{7,1},{8,10},{9,11},{10,... | collective-permute-start | bytes 208904 | tf_op jit(solution)/shard_map/ppermute | solution.py:461
  20.4 1.6 %collective-permute-start.6 = (f32[544,128]{1,0:T(8,128)S(1)}, f32[544,128]{1,0:T(8,128)S(1)}, u32[]{:S(2)}, u32[]{:S(2)}) collective-permute-start(f32[544,128]{1,0:T(8,128)S(1)} %join.1.same_ref), channel_id=1, source_target_pairs={{0,1},{1,0},{2,3},{3,2},{4,5},{5,4},{6,7},{7,6},{8,9},{9,8},{10,11... | collective-permute-start | bytes 835592 | tf_op jit(solution)/shard_map/ppermute | solution.py:483
  44.5 5.5 %collective-permute-start.7 = (f32[3,8,128]{2,1,0:T(8,128)S(1)}, f32[3,8,128]{2,1,0:T(8,128)S(1)}, u32[]{:S(2)}, u32[]{:S(2)}) collective-permute-start(f32[3,8,128]{2,1,0:T(8,128)S(1)} %get-tuple-element.26), channel_id=1, source_target_pairs={{0,8},{4,12},{8,16},{12,20},{16,24},{20,28},{24,0},{28,4},{1,9},{5... | collective-permute-start | bytes 36872 | tf_op jit(solution)/shard_map/ppermute | solution.py:506
  45.3 4.8 %collective-permute-start.8 = (f32[3,8,128]{2,1,0:T(8,128)S(1)}, f32[3,8,128]{2,1,0:T(8,128)S(1)}, u32[]{:S(2)}, u32[]{:S(2)}) collective-permute-start(f32[3,8,128]{2,1,0:T(8,128)S(1)} %get-tuple-element.27), channel_id=1, source_target_pairs={{0,16},{4,20},{8,24},{12,28},{16,0},{20,4},{24,8},{28,12},{1,17},{... | collective-permute-start | bytes 36872 | tf_op jit(solution)/shard_map/ppermute | solution.py:506
  47.2 3.7 %collective-permute-start.9 = (f32[3,8,128]{2,1,0:T(8,128)S(1)}, f32[3,8,128]{2,1,0:T(8,128)S(1)}, u32[]{:S(2)}, u32[]{:S(2)}) collective-permute-start(f32[3,8,128]{2,1,0:T(8,128)S(1)} %get-tuple-element.28), channel_id=1, source_target_pairs={{0,24},{4,28},{8,0},{12,4},{16,8},{20,12},{24,16},{28,20},{1,25},{... | collective-permute-start | bytes 36872 | tf_op jit(solution)/shard_map/ppermute | solution.py:506

commit v6 on v5

--- a/solution.py
+++ b/solution.py
@@ -33,7 +33,7 @@
 
 
 class Sizes:
-    def __init__(self, n_row, n_col, structures, sweeps, width):
+    def __init__(self, n_row, n_col, structures, sweeps, width, listed):
         self.n_row, self.n_col, self.structures, self.sweeps = n_row, n_col, structures, sweeps
         self.width = width
         self.share = n_row // structures
@@ -43,10 +43,9 @@
         self.groups = n_row * n_col
         self.blocks = self.groups * sweeps
         self.slots = structures * sweeps
+        self.chunks = (2 * listed + self.slots + 2 * UNIT) // 128 + 1
+        self.band_chunks = (self.slots * width + UNIT) // 128 + 1
         self.rows = self.slots * 4 + sweeps
-
-    def at(self, block):
-        return modulo(block, self.groups) * self.sweeps + divide(block, self.groups)
 
 
 def pack_kernel(sizes, coords_ref, counts_ref, *out_refs):
@@ -105,10 +104,46 @@
         high = jnp.minimum(high, jnp.where(end > first_bead + 127, end, sizes.blocks * 128))
     low = jnp.maximum(low >> 7, block - (sizes.width - 1))
     high = jnp.minimum(jnp.minimum((high - 1) >> 7, block + (sizes.width - 1)), sizes.blocks - 1)
-    reach = []
-    for value in (low, high, (high - low + 2) >> 1):
-        reach.append(jnp.sum(jnp.where(slot_row == lane, value, 0), axis=0, keepdims=True))
-    steps = lax.div(jnp.sum(reach[2]) + (UNIT // 2 - 1), UNIT // 2)
+    in_band = (high - low + 2) >> 1
+    lower = (
+        lax.broadcasted_iota(jnp.int32, (slots, slots), 0) > lax.broadcasted_iota(jnp.int32, (slots, slots), 1)
+    ).astype(jnp.float32)
+
+    def below(value):
+        return jnp.dot(lower, value, precision=lax.Precision.HIGHEST, preferred_element_type=jnp.float32)
+
+    begin = below(in_band.astype(jnp.float32)).astype(jnp.int32)
+    band_total = jnp.max(begin + in_band)
+    chunks, band_chunks = sizes.chunks, sizes.band_chunks
+
+    def band(chunk, carry):
+        pair = chunk * 128 + lane
+        inside = (begin <= pair) & (pair < begin + in_band)
+
+        def pick(value):
+            return jnp.sum(jnp.where(inside, value, 0), axis=0, keepdims=True)
+
+        live = pick(1) > 0
+        slot = pick(slot_row)
+        near = pick(low - 2 * begin) + 2 * pair
+        last = pick(high)
+        here_block = pick(block)
+        for i in range(2):
+            second = jnp.where(live, jnp.minimum(near + i, last), 0)
+            first = jnp.minimum(here_block, second)
+            group = modulo(first, groups)
+            line = modulo(group, sizes.plane) * sweeps + divide(first, groups)
+            apart = jnp.abs(here_block - second)
+            place = line * 128 + divide(group, sizes.plane) * sizes.width + apart
+            state = jnp.where(live & (near + i <= last), jnp.where(apart == 0, 1, 0), 2)
+            code = second + (slot << 12) + (jnp.where(live, slot, slots) << 19) + (state << 26)
+            at = 2 * chunks + 2 * i * band_chunks + chunk
+            list_ref[pl.ds(at, 1), :] = code
+            list_ref[pl.ds(at + band_chunks, 1), :] = jnp.where(live, place, 0)
+        return carry
+
+    lax.fori_loop(0, lax.div(band_total + UNIT, 128) + 1, band, 0)
+    steps = lax.div(band_total + (UNIT // 2 - 1), UNIT // 2)
 
     half = pairs_ref.shape[2] // 128
     lines = 2 * half
@@ -116,7 +151,7 @@
     group = modulo(pairs, groups)
     mine = modulo(group, sizes.plane) == here
     slot = jnp.where(mine, divide(group, sizes.plane) * sweeps + divide(pairs, groups), -1)
-    other = sizes.at(pairs)
+    other = pairs
 
     def cut(value, line):
         side, at = line // half, line % half * 128
@@ -134,10 +169,7 @@
         picked.append((chosen, inner))
         running = running + counted[:, 128:]
     doubled = 2.0 * jnp.floor(0.5 * (running + 1.0))
-    lower = (
-        lax.broadcasted_iota(jnp.int32, (slots, slots), 0) > lax.broadcasted_iota(jnp.int32, (slots, slots), 1)
-    ).astype(jnp.float32)
-    base = jnp.dot(lower, doubled, precision=lax.Precision.HIGHEST, preferred_element_type=jnp.float32)
+    base = below(doubled)
     number = jnp.max(base + doubled).astype(jnp.int32)
     digit_row = lax.broadcasted_iota(jnp.int32, (POINT_ROWS, 128), 0)
     ranks = []
@@ -153,7 +185,6 @@
         ):
             digits = jnp.where(digit_row == place, digit, digits)
         digits_ref[line] = digits.astype(jnp.float32).astype(jnp.bfloat16)
-    chunks = (list_ref.shape[0] - 8) // 2
     spot = lax.broadcasted_iota(jnp.int32, (128, 128), 0)
 
     def compact(chunk, carry):
@@ -172,18 +203,16 @@
         found = found.astype(jnp.int32)
         at = found[2:3]
         code = found[0:1] + (found[1:2] << 5) + ((slots + at) << 12) + (at << 19)
-        list_ref[pl.ds(chunk, 1), :] = jnp.where(found[5:6] > 0, code, slots << 19)
+        list_ref[pl.ds(chunk, 1), :] = jnp.where(found[5:6] > 0, code, (slots << 19) + (2 << 26))
         list_ref[pl.ds(chunks + chunk, 1), :] = (
             sizes.plane * sweeps * 128 + found[3:4] + found[4:5] * 128
         )
         return carry
 
     lax.fori_loop(0, lax.div(number + 2 * UNIT - 1, 128) + 1, compact, 0)
-    end = 2 * chunks
+    end = 2 * chunks + 4 * band_chunks
     list_ref[end : end + 1] = jnp.full((1, 128), number)
-    list_ref[end + 1 : end + 2] = reach[0]
-    list_ref[end + 2 : end + 3] = reach[1]
-    list_ref[end + 3 : end + 4] = jnp.full((1, 128), steps)
+    list_ref[end + 1 : end + 2] = jnp.full((1, 128), steps)
 
 
 def own_kernel(sizes, edges_ref, own_ref, first_ref, marks_ref):
@@ -199,7 +228,7 @@
         for u in range(sweeps):
             bead = (u * groups + group) * 128 + lane
             inside = (bead >= edges_ref[0]) & (bead < edges_ref[1])
-            marks_ref[group * sweeps + u] = inside.astype(jnp.float32).astype(jnp.bfloat16)
+            marks_ref[u * groups + group] = inside.astype(jnp.float32).astype(jnp.bfloat16)
         return carry
 
     lax.fori_loop(0, groups, mark, 0)
@@ -236,7 +265,7 @@
 
 
 def tile_kernel(sizes, list_ref, listed_ref, first_ref, marks_ref, same_ref, across_ref, *refs):
-    structures, sweeps, slots = sizes.structures, sizes.sweeps, sizes.slots
+    structures, sweeps, slots, groups = sizes.structures, sizes.sweeps, sizes.slots, sizes.groups
     out_refs = refs[:structures]
     second_ref, counts_ref, held_ref, sums_ref, picks_ref, state_ref, total_ref, gain_ref = refs[structures:]
     row_here = lax.axis_index("row")
@@ -271,7 +300,7 @@
                     ):
                         points = jnp.where(row < 4, top, bottom)
                         features = jnp.concatenate([points, jnp.where(row < 3, top, ones)], axis=0)
-                        second_ref[group * sweeps + 2 * pair + odd] = features.astype(jnp.bfloat16)
+                        second_ref[(2 * pair + odd) * groups + group] = features.astype(jnp.bfloat16)
     listed_base = sizes.plane * sweeps
     chosen = lax.broadcasted_iota(jnp.int32, (structures, 128), 0) == family
     for k in range(listed_ref.shape[1] // 128):
@@ -279,13 +308,11 @@
         counts_ref[listed_base + k : listed_base + k + 1] = jnp.sum(line, axis=0, keepdims=True).astype(
             jnp.float32
         )
-    chunks = (list_ref.shape[0] - 8) // 2
+    chunks, band_chunks = sizes.chunks, sizes.band_chunks
+    end = 2 * chunks + 4 * band_chunks
 
     total_ref[...] = jnp.zeros_like(total_ref)
     spare = 1.0 / (1.0 + jnp.exp(jnp.float32(-CONTACT_SHIFT)))
-
-    here = lax.rem(row_here, sizes.share) * sizes.n_col + column_here
-    groups = sizes.groups
 
     def step(ending, beginning):
         sums = sums_ref[pl.ds(0, UNIT, stride=8), :]
@@ -294,8 +321,8 @@
         chance = 64.0 * 128.0 + 0.5 * jnp.sum(sums, axis=1, keepdims=True)
         count = jnp.sum(picks_ref[...], axis=1, keepdims=True)
         state = state_ref[...]
-        chance = jnp.where(state == 1.0, 0.5 * (chance - 128.0 * spare), chance)
-        weight = jnp.where(state == 2.0, 0.0, 1.0 - count / (BACKGROUND + chance / 128.0))
+        chance = jnp.where(state == 1, 0.5 * (chance - 128.0 * spare), chance)
+        weight = jnp.where(state == 2, 0.0, 1.0 - count / (BACKGROUND + chance / 128.0))
         for t in range(0, UNIT, 2):
             left, right = (second_ref[ending[t + i] & 4095] for i in range(2))
             blank = jnp.zeros_like(left)
@@ -310,7 +337,7 @@
                 weight[t : t + 1, : 2 * POINT_ROWS],
                 weight[t + 1 : t + 2, : 2 * POINT_ROWS],
             )
-            total_ref[ending[t] >> 19] += scale * product
+            total_ref[(ending[t] >> 19) & 127] += scale * product
         for t in range(0, UNIT, 2):
             seconds = [beginning[t + i][0] & 4095 for i in range(2)]
             logit = jnp.dot(
@@ -325,48 +352,31 @@
             for i in range(2):
                 part = bend[:, i * 128 : (i + 1) * 128]
                 sums_ref[(t + i) * 8 : (t + i + 1) * 8] = jnp.sum(part.reshape(16, 8, 128), axis=0)
-                code, place, state = beginning[t + i]
+                code, place = beginning[t + i]
                 picked = counts_ref[pl.ds(place >> 7, 1), :]
                 picks_ref[t + i : t + i + 1] = jnp.where(lane == (place & 127), picked, 0.0)
-                state_ref[t + i : t + i + 1] = jnp.full((1, 128), state)
-        return tuple(code for code, _, _ in beginning)
-
-    def band_step(turn, carry):
-        slot, other, ending = carry
-        beginning = []
-        for _ in range(UNIT // 2):
-            block = modulo(slot, sweeps) * groups + divide(slot, sweeps) * sizes.plane + here
-            high = list_ref[2 * chunks + 2, slot]
-            for i in range(2):
-                second = jnp.minimum(other + i, high)
-                first = jnp.minimum(block, second)
-                group = modulo(first, groups)
-                line = modulo(group, sizes.plane) * sweeps + divide(first, groups)
-                apart = jnp.abs(block - second)
-                place = line * 128 + divide(group, sizes.plane) * sizes.width + apart
-                live = (other + i <= high) & (slot < slots)
-                code = sizes.at(second) + (jnp.minimum(slot, slots - 1) << 12) + (slot << 19)
-                state = jnp.where(live, (apart == 0).astype(jnp.float32), 2.0)
-                beginning.append((code, place, state))
-            over = other + 2 > high
-            slot = jnp.minimum(slot + over.astype(jnp.int32), slots)
-            other = jnp.where(over, list_ref[2 * chunks + 1, slot], other + 2)
-        return slot, other, step(ending, beginning)
-
-    def listed_step(turn, ending):
+                state_ref[t + i : t + i + 1] = jnp.full((1, 128), code >> 26)
+        return tuple(code for code, _ in beginning)
+
+    def band_step(turn, ending):
+        line = 2 * chunks + (turn * (UNIT // 2) >> 7)
+        at = turn * (UNIT // 2) & 127
         beginning = []
         for t in range(UNIT):
-            at = turn * UNIT + t
-            code = list_ref[at >> 7, at & 127]
-            state = jnp.where(code >> 19 < slots, 0.0, 2.0)
-            beginning.append((code, list_ref[chunks + (at >> 7), at & 127], state))
+            row = line + t % 2 * 2 * band_chunks
+            beginning.append((list_ref[row, at + t // 2], list_ref[row + band_chunks, at + t // 2]))
+        return step(ending, beginning)
+
+    def listed_step(turn, ending):
+        line = turn * UNIT >> 7
+        at = turn * UNIT & 127
+        beginning = [(list_ref[line, at + t], list_ref[chunks + line, at + t]) for t in range(UNIT)]
         return step(ending, beginning)
 
     idle = (jnp.int32(slots << 19),) * UNIT
     sums_ref[...] = jnp.zeros_like(sums_ref)
-    carry = (jnp.int32(0), list_ref[2 * chunks + 1, 0], idle)
-    ending = lax.fori_loop(0, list_ref[2 * chunks + 3, 0], band_step, carry)[2]
-    listed_steps = lax.div(list_ref[2 * chunks, 0] + UNIT - 1, UNIT)
+    ending = lax.fori_loop(0, list_ref[end + 1, 0], band_step, idle)
+    listed_steps = lax.div(list_ref[end, 0] + UNIT - 1, UNIT)
     lax.fori_loop(0, listed_steps + 1, listed_step, ending)
 
     def collect(slot, carry):
@@ -404,7 +414,7 @@
     structures, _, sweeps, block_size = coords.shape
     width = band_counts.shape[3]
     listed = inter_pairs.shape[1]
-    sizes = Sizes(n_row, n_col, structures, sweeps, width)
+    sizes = Sizes(n_row, n_col, structures, sweeps, width, listed)
     share, slots, blocks = sizes.share, sizes.slots, sizes.blocks
 
     messages = pl.pallas_call(
@@ -422,12 +432,12 @@
     received = [messages[0]]
     for k in range(1, structures):
         received.append(lax.ppermute(messages[k], "row", deal[k]))
-    chunks = -(-(2 * listed + slots + 2 * UNIT) // block_size)
+    lines = 2 * sizes.chunks + 4 * sizes.band_chunks + 8
     labels = -(-chrom_lengths.shape[0] // 16) * 16
     tiles, edges = pl.pallas_call(
         functools.partial(list_kernel, sizes),
         out_shape=[
-            jax.ShapeDtypeStruct((2 * chunks + 8, block_size), jnp.int32),
+            jax.ShapeDtypeStruct((lines, block_size), jnp.int32),
             jax.ShapeDtypeStruct((2, labels, block_size), jnp.int32),
         ],
         in_specs=[SMEM, VMEM],
@@ -493,7 +503,7 @@
             pltpu.VMEM((UNIT // 2, block_size, 2 * block_size), jnp.bfloat16),
             pltpu.VMEM((UNIT * 8, block_size), jnp.float32),
             pltpu.VMEM((UNIT, block_size), jnp.float32),
-            pltpu.VMEM((UNIT, block_size), jnp.float32),
+            pltpu.VMEM((UNIT, block_size), jnp.int32),
             pltpu.VMEM((slots + 1, block_size, 2 * POINT_ROWS), jnp.float32),
             pltpu.VMEM((slots * POINT_ROWS, block_size), jnp.float32),
         ],

time: 52.1 us -> 50.8 us (0.975)
  Pallas kernels: 27.3 us -> 26.1 us
    pallas_call x1, Pallas kernels: 22.5 us -> 20.8 us  [on_device(): pl.pallas_call(functools.partial(tile_kernel, sizes), out_shape=[jax.Shap...]
  transfers between devices with their start and end apart: 10 -> 10, of which waited for: 5 -> 5; matrix products, arithmetic and copies ran while one was open for 0% -> 0% of each run, Pallas kernels for 8% -> 9%
where the time goes in v6:
time: 50.8 us; the launch traced here: 50.1 us
  Pallas kernels  26.1 us (51%)
  starting transfers between devices  14.5 us (29%)
  waiting for transfers between devices  6.43 us (13%)
  local copies, waits for them, and re-layouts  2.93 us (6%)
    pallas_call x1, Pallas kernels, on_device(): pl.pallas_call(functools.partial(tile_kernel, sizes), out_shape=[jax.Shap...  20.8 us
    ppermute x3, starting transfers between devices, on_device(): received.append(lax.ppermute(messages[k], 'row', deal[k]))  6.96 us
    ppermute x3, starting transfers between devices, on_device(): arrived.append(lax.ppermute(gains[k], 'row', deal[k]))  3.87 us
    ppermute x3, starting transfers between devices, on_device(): pieces.append(lax.ppermute(own_row, AXES, moves))  3.6 us
    unnamed x10, local copies, waits for them, and re-layouts  2.93 us
    ppermute x3, waiting for transfers between devices, on_device(): pieces.append(lax.ppermute(own_row, AXES, moves))  2.64 us
    pallas_call x1, Pallas kernels, on_device(): pl.pallas_call(functools.partial(list_kernel, sizes), out_shape=[jax.Shap...  2.57 us
    ppermute x3, waiting for transfers between devices, on_device(): arrived.append(lax.ppermute(gains[k], 'row', deal[k]))  2.23 us
  transfers between devices with their start and end apart: 10, of which 5 were waited for; matrix products, arithmetic and copies ran while one was open for 0% of the time, Pallas kernels for 9%

profile of v6, /device:TPU:0, one launch (start us, length us, event | category | flops | bytes accessed | tf_op | source)
XLA Modules:
  0.0 50.1 jit_solution(7407784247782685477)
XLA Ops:
  0.0 0.0 copy-start
  0.0 0.8 %copy-done = f32[4,3,8,128]{3,2,1,0:T(8,128)S(1)} copy-done((f32[4,3,8,128]{3,2,1,0:T(8,128)S(1)}, f32[4,3,8,128]{3,2,1,0:T(8,128)}, u32[]{:S(2)}) %copy-start) | copy-done | bytes 49176
  0.8 0.0 copy-start.3
  0.8 0.7 %copy-done.3 = s32[4,8,1,32]{3,2,1,0:T(1,128)S(1)} copy-done((s32[4,8,1,32]{3,2,1,0:T(1,128)S(1)}, s32[4,8,1,32]{3,2,1,0:T(1,128)}, u32[]{:S(2)}) %copy-start.3) | copy-done | bytes 4120
  1.5 0.0 copy-start.2
  1.5 0.1 pack.1
  1.7 3.0 %collective-permute-start = (f32[40,128]{1,0:T(8,128)S(1)}, f32[40,128]{1,0:T(8,128)S(1)}, u32[]{:S(2)}, u32[]{:S(2)}) collective-permute-start(f32[40,128]{1,0:T(8,128)S(1)} %get-tuple-element.20), channel_id=1, source_target_pairs={{0,8},{4,12},{8,16},{12,20},{16,24},{20,28},{24,0},{28,4},{1,9},{5... | collective-permute-start | bytes 61448 | tf_op jit(solution)/shard_map/ppermute | solution.py:434
  4.7 2.6 %collective-permute-start.1 = (f32[40,128]{1,0:T(8,128)S(1)}, f32[40,128]{1,0:T(8,128)S(1)}, u32[]{:S(2)}, u32[]{:S(2)}) collective-permute-start(f32[40,128]{1,0:T(8,128)S(1)} %get-tuple-element.21), channel_id=1, source_target_pairs={{0,16},{4,20},{8,24},{12,28},{16,0},{20,4},{24,8},{28,12},{1,17},{... | collective-permute-start | bytes 61448 | tf_op jit(solution)/shard_map/ppermute | solution.py:434
  7.3 1.3 %collective-permute-start.2 = (f32[40,128]{1,0:T(8,128)S(1)}, f32[40,128]{1,0:T(8,128)S(1)}, u32[]{:S(2)}, u32[]{:S(2)}) collective-permute-start(f32[40,128]{1,0:T(8,128)S(1)} %get-tuple-element.22), channel_id=1, source_target_pairs={{0,24},{4,28},{8,0},{12,4},{16,8},{20,12},{24,16},{28,20},{1,25},{... | collective-permute-start | bytes 61448 | tf_op jit(solution)/shard_map/ppermute | solution.py:434
  8.6 0.0 copy-start.1
  8.6 0.8 %copy-done.1 = s32[4,1024,2]{1,2,0:T(2,128)S(1)} copy-done((s32[4,1024,2]{1,2,0:T(2,128)S(1)}, s32[4,1024,2]{1,2,0:T(2,128)}, u32[]{:S(2)}) %copy-start.1) | copy-done | bytes 32792
  9.4 0.0 copy-start.4
  9.4 0.7 %copy-done.4 = s32[46]{0:T(128)S(1)} copy-done((s32[46]{0:T(128)S(1)}, s32[46]{0:T(128)}, u32[]{:S(2)}) %copy-start.4) | copy-done | bytes 208
  10.0 2.6 %list_tiles.1 = (s32[78,128]{1,0:T(8,128)S(1)}, s32[2,48,128]{2,1,0:T(8,128)S(1)}) custom-call(s32[46]{0:T(128)S(1)} %copy-done.4, s32[4,2,1024]{2,1,0:T(2,128)S(1)} %bitcast.1), custom_call_target="tpu_custom_call" | custom-call | tf_op jit(solution)/shard_map/list_tiles/pallas_call | solution.py:437
  12.6 0.0 collective-permute-done.refs_1_
  12.6 0.0 collective-permute-done.1.refs_2_
  12.6 0.0 collective-permute-done.2.refs_3_
  12.7 2.5 %collective-permute-start.5 = (f32[136,128]{1,0:T(8,128)S(1)}, f32[136,128]{1,0:T(8,128)S(1)}, u32[]{:S(2)}, u32[]{:S(2)}) collective-permute-start(f32[136,128]{1,0:T(8,128)S(1)} %merge.1.own_ref.refs_0_), channel_id=1, source_target_pairs={{0,6},{1,7},{2,0},{3,1},{4,2},{5,3},{6,4},{7,5},{8,14},{9,15},{10,... | collective-permute-start | bytes 208904 | tf_op jit(solution)/shard_map/ppermute | solution.py:471
  15.2 0.5 %collective-permute-start.4 = (f32[136,128]{1,0:T(8,128)S(1)}, f32[136,128]{1,0:T(8,128)S(1)}, u32[]{:S(2)}, u32[]{:S(2)}) collective-permute-start(f32[136,128]{1,0:T(8,128)S(1)} %merge.1.own_ref.refs_0_), channel_id=1, source_target_pairs={{0,4},{1,5},{2,6},{3,7},{4,0},{5,1},{6,2},{7,3},{8,12},{9,13},{10,... | collective-permute-start | bytes 208904 | tf_op jit(solution)/shard_map/ppermute | solution.py:471
  15.7 0.6 %collective-permute-start.3 = (f32[136,128]{1,0:T(8,128)S(1)}, f32[136,128]{1,0:T(8,128)S(1)}, u32[]{:S(2)}, u32[]{:S(2)}) collective-permute-start(f32[136,128]{1,0:T(8,128)S(1)} %merge.1.own_ref.refs_0_), channel_id=1, source_target_pairs={{0,2},{1,3},{2,4},{3,5},{4,6},{5,7},{6,0},{7,1},{8,10},{9,11},{10,... | collective-permute-start | bytes 208904 | tf_op jit(solution)/shard_map/ppermute | solution.py:471
  16.3 2.0 %own_features.1 = (bf16[64,128,64]{2,1,0:T(8,128)(2,1)S(1)}, bf16[256,48,128]{2,1,0:T(8,128)(2,1)S(1)}) custom-call(s32[2,48,128]{2,1,0:T(8,128)S(1)} %get-tuple-element.18.edges_ref, f32[136,128]{1,0:T(8,128)S(1)} %merge.1.own_ref.refs_0_), custom_call_target="tpu_custom_call" | custom-call | tf_op jit(solution)/shard_map/own_features/pallas_call | solution.py:473
  18.2 0.0 collective-permute-done.5.refs_3_
  18.2 1.2 %collective-permute-done.4.refs_2_ = f32[136,128]{1,0:T(8,128)S(1)} collective-permute-done((f32[136,128]{1,0:T(8,128)S(1)}, f32[136,128]{1,0:T(8,128)S(1)}, u32[]{:S(2)}, u32[]{:S(2)}) %collective-permute-start.4) | collective-permute-done | bytes 69664 | tf_op jit(solution)/shard_map/ppermute | solution.py:471
  19.5 1.4 %collective-permute-done.3.refs_1_ = f32[136,128]{1,0:T(8,128)S(1)} collective-permute-done((f32[136,128]{1,0:T(8,128)S(1)}, f32[136,128]{1,0:T(8,128)S(1)}, u32[]{:S(2)}, u32[]{:S(2)}) %collective-permute-start.3) | collective-permute-done | bytes 69664 | tf_op jit(solution)/shard_map/ppermute | solution.py:471
  20.9 0.1 collective-permute-start.6
  21.0 1.5 %collective-permute-done.6.across_ref = f32[544,128]{1,0:T(8,128)S(1)} collective-permute-done((f32[544,128]{1,0:T(8,128)S(1)}, f32[544,128]{1,0:T(8,128)S(1)}, u32[]{:S(2)}, u32[]{:S(2)}) %collective-permute-start.6) | collective-permute-done | bytes 278560 | tf_op jit(solution)/shard_map/ppermute | solution.py:493
  22.5 0.0 copy-done.2
  22.5 20.8 %tiles.1 = (f32[3,8,128]{2,1,0:T(8,128)S(1)}, f32[3,8,128]{2,1,0:T(8,128)S(1)}, f32[3,8,128]{2,1,0:T(8,128)S(1)}, f32[3,8,128]{2,1,0:T(8,128)S(1)}) custom-call(s32[78,128]{1,0:T(8,128)S(1)} %get-tuple-element.17.after_ref.list_ref, s32[4,1024]{1,0:T(4,128)S(1)} %copy-done.2, bf16[64,128,64]{2,1,0:T(8,128)(2,1)S(1)} %get-tuple-element.23.first_ref, ...), custom_call_target="tpu_custom_call" | custom-call | tf_op jit(solution)/shard_map/tiles/pallas_call | solution.py:495
  43.3 0.1 collective-permute-start.7
  43.4 2.1 %collective-permute-start.8 = (f32[3,8,128]{2,1,0:T(8,128)S(1)}, f32[3,8,128]{2,1,0:T(8,128)S(1)}, u32[]{:S(2)}, u32[]{:S(2)}) collective-permute-start(f32[3,8,128]{2,1,0:T(8,128)S(1)} %get-tuple-element.27), channel_id=1, source_target_pairs={{0,16},{4,20},{8,24},{12,28},{16,0},{20,4},{24,8},{28,12},{1,17},{... | collective-permute-start | bytes 36872 | tf_op jit(solution)/shard_map/ppermute | solution.py:516
  45.5 1.7 %collective-permute-start.9 = (f32[3,8,128]{2,1,0:T(8,128)S(1)}, f32[3,8,128]{2,1,0:T(8,128)S(1)}, u32[]{:S(2)}, u32[]{:S(2)}) collective-permute-start(f32[3,8,128]{2,1,0:T(8,128)S(1)} %get-tuple-element.28), channel_id=1, source_target_pairs={{0,24},{4,28},{8,0},{12,4},{16,8},{20,12},{24,16},{28,20},{1,25},{... | collective-permute-start | bytes 36872 | tf_op jit(solution)/shard_map/ppermute | solution.py:516
  47.2 1.7 %collective-permute-done.7.refs_1_ = f32[3,8,128]{2,1,0:T(8,128)S(1)} collective-permute-done((f32[3,8,128]{2,1,0:T(8,128)S(1)}, f32[3,8,128]{2,1,0:T(8,128)S(1)}, u32[]{:S(2)}, u32[]{:S(2)}) %collective-permute-start.7) | collective-permute-done | bytes 12320 | tf_op jit(solution)/shard_map/ppermute | solution.py:516
  48.9 0.0 collective-permute-done.8.refs_2_
  48.9 0.6 %collective-permute-done.9.refs_3_ = f32[3,8,128]{2,1,0:T(8,128)S(1)} collective-permute-done((f32[3,8,128]{2,1,0:T(8,128)S(1)}, f32[3,8,128]{2,1,0:T(8,128)S(1)}, u32[]{:S(2)}, u32[]{:S(2)}) %collective-permute-start.9) | collective-permute-done | bytes 12320 | tf_op jit(solution)/shard_map/ppermute | solution.py:516
  49.4 0.6 %place.1 = f32[4,3,8,128]{3,2,1,0:T(8,128)} custom-call(f32[3,8,128]{2,1,0:T(8,128)S(1)} %get-tuple-element.25.refs_0_, f32[3,8,128]{2,1,0:T(8,128)S(1)} %collective-permute-done.7.refs_1_, f32[3,8,128]{2,1,0:T(8,128)S(1)} %collective-permute-done.8.refs_2_, f32[3,8,128]{2,1,0:T(8,128)S(1)} %collective-permute-done.9.refs_3_), custom_call_target="tpu_custom_call" | custom-call | tf_op jit(solution)/shard_map/place/pallas_call | solution.py:517
  (2 shorter events, 0.0 us)
Async XLA Ops:
  0.0 0.8 %copy-start = (f32[4,3,8,128]{3,2,1,0:T(8,128)S(1)}, f32[4,3,8,128]{3,2,1,0:T(8,128)}, u32[]{:S(2)}) copy-start(f32[4,3,8,128]{3,2,1,0:T(8,128)} %coords_ref.1) | copy-start | bytes 147460
  0.8 0.7 %copy-start.3 = (s32[4,8,1,32]{3,2,1,0:T(1,128)S(1)}, s32[4,8,1,32]{3,2,1,0:T(1,128)}, u32[]{:S(2)}) copy-start(s32[4,8,1,32]{3,2,1,0:T(1,128)} %counts_ref.1) | copy-start | bytes 12292
  1.5 21.0 %copy-start.2 = (s32[4,1024]{1,0:T(4,128)S(1)}, s32[4,1024]{1,0:T(4,128)}, u32[]{:S(2)}) copy-start(s32[4,1024]{1,0:T(4,128)} %listed_ref.1) | copy-start | bytes 49156
  1.7 11.0 %collective-permute-start = (f32[40,128]{1,0:T(8,128)S(1)}, f32[40,128]{1,0:T(8,128)S(1)}, u32[]{:S(2)}, u32[]{:S(2)}) collective-permute-start(f32[40,128]{1,0:T(8,128)S(1)} %get-tuple-element.20), channel_id=1, source_target_pairs={{0,8},{4,12},{8,16},{12,20},{16,24},{20,28},{24,0},{28,4},{1,9},{5... | collective-permute-start | bytes 61448 | tf_op jit(solution)/shard_map/ppermute | solution.py:434
  4.7 7.9 %collective-permute-start.1 = (f32[40,128]{1,0:T(8,128)S(1)}, f32[40,128]{1,0:T(8,128)S(1)}, u32[]{:S(2)}, u32[]{:S(2)}) collective-permute-start(f32[40,128]{1,0:T(8,128)S(1)} %get-tuple-element.21), channel_id=1, source_target_pairs={{0,16},{4,20},{8,24},{12,28},{16,0},{20,4},{24,8},{28,12},{1,17},{... | collective-permute-start | bytes 61448 | tf_op jit(solution)/shard_map/ppermute | solution.py:434
  7.3 5.4 %collective-permute-start.2 = (f32[40,128]{1,0:T(8,128)S(1)}, f32[40,128]{1,0:T(8,128)S(1)}, u32[]{:S(2)}, u32[]{:S(2)}) collective-permute-start(f32[40,128]{1,0:T(8,128)S(1)} %get-tuple-element.22), channel_id=1, source_target_pairs={{0,24},{4,28},{8,0},{12,4},{16,8},{20,12},{24,16},{28,20},{1,25},{... | collective-permute-start | bytes 61448 | tf_op jit(solution)/shard_map/ppermute | solution.py:434
  8.6 0.8 %copy-start.1 = (s32[4,1024,2]{1,2,0:T(2,128)S(1)}, s32[4,1024,2]{1,2,0:T(2,128)}, u32[]{:S(2)}) copy-start(s32[4,1024,2]{1,2,0:T(2,128)} %param.8) | copy-start | bytes 98308
  9.4 0.7 %copy-start.4 = (s32[46]{0:T(128)S(1)}, s32[46]{0:T(128)}, u32[]{:S(2)}) copy-start(s32[46]{0:T(128)} %lengths_ref.1) | copy-start | bytes 556
  12.7 5.6 %collective-permute-start.5 = (f32[136,128]{1,0:T(8,128)S(1)}, f32[136,128]{1,0:T(8,128)S(1)}, u32[]{:S(2)}, u32[]{:S(2)}) collective-permute-start(f32[136,128]{1,0:T(8,128)S(1)} %merge.1.own_ref.refs_0_), channel_id=1, source_target_pairs={{0,6},{1,7},{2,0},{3,1},{4,2},{5,3},{6,4},{7,5},{8,14},{9,15},{10,... | collective-permute-start | bytes 208904 | tf_op jit(solution)/shard_map/ppermute | solution.py:471
  15.2 4.3 %collective-permute-start.4 = (f32[136,128]{1,0:T(8,128)S(1)}, f32[136,128]{1,0:T(8,128)S(1)}, u32[]{:S(2)}, u32[]{:S(2)}) collective-permute-start(f32[136,128]{1,0:T(8,128)S(1)} %merge.1.own_ref.refs_0_), channel_id=1, source_target_pairs={{0,4},{1,5},{2,6},{3,7},{4,0},{5,1},{6,2},{7,3},{8,12},{9,13},{10,... | collective-permute-start | bytes 208904 | tf_op jit(solution)/shard_map/ppermute | solution.py:471
  15.7 5.2 %collective-permute-start.3 = (f32[136,128]{1,0:T(8,128)S(1)}, f32[136,128]{1,0:T(8,128)S(1)}, u32[]{:S(2)}, u32[]{:S(2)}) collective-permute-start(f32[136,128]{1,0:T(8,128)S(1)} %merge.1.own_ref.refs_0_), channel_id=1, source_target_pairs={{0,2},{1,3},{2,4},{3,5},{4,6},{5,7},{6,0},{7,1},{8,10},{9,11},{10,... | collective-permute-start | bytes 208904 | tf_op jit(solution)/shard_map/ppermute | solution.py:471
  20.9 1.6 %collective-permute-start.6 = (f32[544,128]{1,0:T(8,128)S(1)}, f32[544,128]{1,0:T(8,128)S(1)}, u32[]{:S(2)}, u32[]{:S(2)}) collective-permute-start(f32[544,128]{1,0:T(8,128)S(1)} %join.1.same_ref), channel_id=1, source_target_pairs={{0,1},{1,0},{2,3},{3,2},{4,5},{5,4},{6,7},{7,6},{8,9},{9,8},{10,11... | collective-permute-start | bytes 835592 | tf_op jit(solution)/shard_map/ppermute | solution.py:493
  43.3 5.5 %collective-permute-start.7 = (f32[3,8,128]{2,1,0:T(8,128)S(1)}, f32[3,8,128]{2,1,0:T(8,128)S(1)}, u32[]{:S(2)}, u32[]{:S(2)}) collective-permute-start(f32[3,8,128]{2,1,0:T(8,128)S(1)} %get-tuple-element.26), channel_id=1, source_target_pairs={{0,8},{4,12},{8,16},{12,20},{16,24},{20,28},{24,0},{28,4},{1,9},{5... | collective-permute-start | bytes 36872 | tf_op jit(solution)/shard_map/ppermute | solution.py:516
  43.4 5.5 %collective-permute-start.8 = (f32[3,8,128]{2,1,0:T(8,128)S(1)}, f32[3,8,128]{2,1,0:T(8,128)S(1)}, u32[]{:S(2)}, u32[]{:S(2)}) collective-permute-start(f32[3,8,128]{2,1,0:T(8,128)S(1)} %get-tuple-element.27), channel_id=1, source_target_pairs={{0,16},{4,20},{8,24},{12,28},{16,0},{20,4},{24,8},{28,12},{1,17},{... | collective-permute-start | bytes 36872 | tf_op jit(solution)/shard_map/ppermute | solution.py:516
  45.5 3.9 %collective-permute-start.9 = (f32[3,8,128]{2,1,0:T(8,128)S(1)}, f32[3,8,128]{2,1,0:T(8,128)S(1)}, u32[]{:S(2)}, u32[]{:S(2)}) collective-permute-start(f32[3,8,128]{2,1,0:T(8,128)S(1)} %get-tuple-element.28), channel_id=1, source_target_pairs={{0,24},{4,28},{8,0},{12,4},{16,8},{20,12},{24,16},{28,20},{1,25},{... | collective-permute-start | bytes 36872 | tf_op jit(solution)/shard_map/ppermute | solution.py:516

commit v7 on v6

--- a/solution.py
+++ b/solution.py
@@ -82,7 +82,14 @@
         refs[-1][k * rows : (k + 1) * rows] = ref[...]
 
 
-def list_kernel(sizes, lengths_ref, pairs_ref, list_ref, edges_ref, digits_ref):
+def below(value):
+    rows = value.shape[0]
+    row = lax.broadcasted_iota(jnp.int32, (rows, rows), 0)
+    lower = (row > lax.broadcasted_iota(jnp.int32, (rows, rows), 1)).astype(jnp.float32)
+    return jnp.dot(lower, value, precision=lax.Precision.HIGHEST, preferred_element_type=jnp.float32)
+
+
+def band_kernel(sizes, lengths_ref, list_ref, edges_ref):
     slots, sweeps, groups = sizes.slots, sizes.sweeps, sizes.groups
     family = lax.div(lax.axis_index("row"), sizes.share)
     here = lax.rem(lax.axis_index("row"), sizes.share) * sizes.n_col + lax.axis_index("col")
@@ -105,16 +112,9 @@
     low = jnp.maximum(low >> 7, block - (sizes.width - 1))
     high = jnp.minimum(jnp.minimum((high - 1) >> 7, block + (sizes.width - 1)), sizes.blocks - 1)
     in_band = (high - low + 2) >> 1
-    lower = (
-        lax.broadcasted_iota(jnp.int32, (slots, slots), 0) > lax.broadcasted_iota(jnp.int32, (slots, slots), 1)
-    ).astype(jnp.float32)
-
-    def below(value):
-        return jnp.dot(lower, value, precision=lax.Precision.HIGHEST, preferred_element_type=jnp.float32)
-
     begin = below(in_band.astype(jnp.float32)).astype(jnp.int32)
     band_total = jnp.max(begin + in_band)
-    chunks, band_chunks = sizes.chunks, sizes.band_chunks
+    chunks = sizes.band_chunks
 
     def band(chunk, carry):
         pair = chunk * 128 + lane
@@ -137,13 +137,22 @@
             place = line * 128 + divide(group, sizes.plane) * sizes.width + apart
             state = jnp.where(live & (near + i <= last), jnp.where(apart == 0, 1, 0), 2)
             code = second + (slot << 12) + (jnp.where(live, slot, slots) << 19) + (state << 26)
-            at = 2 * chunks + 2 * i * band_chunks + chunk
+            at = 2 * i * chunks + chunk
             list_ref[pl.ds(at, 1), :] = code
-            list_ref[pl.ds(at + band_chunks, 1), :] = jnp.where(live, place, 0)
+            list_ref[pl.ds(at + chunks, 1), :] = jnp.where(live, place, 0)
         return carry
 
     lax.fori_loop(0, lax.div(band_total + UNIT, 128) + 1, band, 0)
     steps = lax.div(band_total + (UNIT // 2 - 1), UNIT // 2)
+    list_ref[4 * chunks : 4 * chunks + 1] = jnp.full((1, 128), steps)
+
+
+def list_kernel(sizes, pairs_ref, after_ref, list_ref, digits_ref):
+    slots, sweeps, groups, chunks = sizes.slots, sizes.sweeps, sizes.groups, sizes.chunks
+    family = lax.div(lax.axis_index("row"), sizes.share)
+    here = lax.rem(lax.axis_index("row"), sizes.share) * sizes.n_col + lax.axis_index("col")
+    lane = lax.broadcasted_iota(jnp.int32, (1, 128), 1)
+    slot_row = lax.broadcasted_iota(jnp.int32, (slots, 128), 0)
 
     half = pairs_ref.shape[2] // 128
     lines = 2 * half
@@ -210,9 +219,7 @@
         return carry
 
     lax.fori_loop(0, lax.div(number + 2 * UNIT - 1, 128) + 1, compact, 0)
-    end = 2 * chunks + 4 * band_chunks
-    list_ref[end : end + 1] = jnp.full((1, 128), number)
-    list_ref[end + 1 : end + 2] = jnp.full((1, 128), steps)
+    list_ref[2 * chunks : 2 * chunks + 1] = jnp.full((1, 128), number)
 
 
 def own_kernel(sizes, edges_ref, own_ref, first_ref, marks_ref):
@@ -264,10 +271,10 @@
     lax.fori_loop(0, sizes.structures, fill, 0)
 
 
-def tile_kernel(sizes, list_ref, listed_ref, first_ref, marks_ref, same_ref, across_ref, *refs):
+def tile_kernel(sizes, band_ref, list_ref, listed_ref, first_ref, marks_ref, same_ref, across_ref, *refs):
     structures, sweeps, slots, groups = sizes.structures, sizes.sweeps, sizes.slots, sizes.groups
     out_refs = refs[:structures]
-    second_ref, counts_ref, held_ref, sums_ref, picks_ref, state_ref, total_ref, gain_ref = refs[structures:]
+    second_ref, counts_ref, held_ref, sums_ref, picks_ref, state_ref, total_ref = refs[structures:]
     row_here = lax.axis_index("row")
     column_here = lax.axis_index("col")
     family = lax.div(row_here, sizes.share)
@@ -276,7 +283,6 @@
     lane = lax.broadcasted_iota(jnp.int32, (1, 128), 1)
     row = lax.broadcasted_iota(jnp.int32, (8, 128), 0)
     ones = jnp.where((row == 3) | (row == 4), 1.0, 0.0)
-    narrow = lax.broadcasted_iota(jnp.int32, (1, 2 * POINT_ROWS), 1)
 
     for core, piece_ref in ((core_here, same_ref), (1 - core_here, across_ref)):
         for k in range(sizes.chips):
@@ -309,12 +315,11 @@
             jnp.float32
         )
     chunks, band_chunks = sizes.chunks, sizes.band_chunks
-    end = 2 * chunks + 4 * band_chunks
 
     total_ref[...] = jnp.zeros_like(total_ref)
     spare = 1.0 / (1.0 + jnp.exp(jnp.float32(-CONTACT_SHIFT)))
 
-    def step(ending, beginning):
+    def finish(ending):
         sums = sums_ref[pl.ds(0, UNIT, stride=8), :]
         for k in range(1, 8):
             sums = sums + sums_ref[pl.ds(k, UNIT, stride=8), :]
@@ -330,14 +335,14 @@
                 [jnp.concatenate([left, blank], axis=1), jnp.concatenate([blank, right], axis=1)], axis=0
             )
             product = lax.dot_general(
-                held_ref[t // 2], both, (((1,), (1,)), ((), ())), preferred_element_type=jnp.float32
-            )
-            scale = jnp.where(
-                narrow < POINT_ROWS,
-                weight[t : t + 1, : 2 * POINT_ROWS],
-                weight[t + 1 : t + 2, : 2 * POINT_ROWS],
-            )
-            total_ref[(ending[t] >> 19) & 127] += scale * product
+                both, held_ref[t // 2], (((1,), (1,)), ((), ())), preferred_element_type=jnp.float32
+            )
+            at = pl.multiple_of(((ending[t] >> 19) & 127) * POINT_ROWS, POINT_ROWS)
+            total_ref[pl.ds(at, POINT_ROWS), :] += (
+                weight[t : t + 1] * product[:POINT_ROWS] + weight[t + 1 : t + 2] * product[POINT_ROWS:]
+            )
+
+    def begin(beginning):
         for t in range(0, UNIT, 2):
             seconds = [beginning[t + i][0] & 4095 for i in range(2)]
             logit = jnp.dot(
@@ -359,47 +364,41 @@
         return tuple(code for code, _ in beginning)
 
     def band_step(turn, ending):
-        line = 2 * chunks + (turn * (UNIT // 2) >> 7)
+        line = turn * (UNIT // 2) >> 7
         at = turn * (UNIT // 2) & 127
         beginning = []
         for t in range(UNIT):
             row = line + t % 2 * 2 * band_chunks
-            beginning.append((list_ref[row, at + t // 2], list_ref[row + band_chunks, at + t // 2]))
-        return step(ending, beginning)
+            beginning.append((band_ref[row, at + t // 2], band_ref[row + band_chunks, at + t // 2]))
+        finish(ending)
+        return begin(beginning)
 
     def listed_step(turn, ending):
         line = turn * UNIT >> 7
         at = turn * UNIT & 127
         beginning = [(list_ref[line, at + t], list_ref[chunks + line, at + t]) for t in range(UNIT)]
-        return step(ending, beginning)
+        finish(ending)
+        return begin(beginning)
 
     idle = (jnp.int32(slots << 19),) * UNIT
     sums_ref[...] = jnp.zeros_like(sums_ref)
-    ending = lax.fori_loop(0, list_ref[end + 1, 0], band_step, idle)
-    listed_steps = lax.div(list_ref[end, 0] + UNIT - 1, UNIT)
-    lax.fori_loop(0, listed_steps + 1, listed_step, ending)
-
-    def collect(slot, carry):
-        turned = jnp.transpose(total_ref[slot])
-        gain_ref[pl.ds(pl.multiple_of(slot * POINT_ROWS, POINT_ROWS), POINT_ROWS), :] = (
-            turned[:POINT_ROWS] + turned[POINT_ROWS:]
-        )
-        return carry
-
-    lax.fori_loop(0, slots, collect, 0, unroll=4)
+    ending = lax.fori_loop(0, band_ref[4 * band_chunks, 0], band_step, idle)
+    listed_steps = lax.div(list_ref[2 * chunks, 0] + UNIT - 1, UNIT)
+    finish(lax.fori_loop(0, listed_steps, listed_step, ending))
+
     scale = -2.0 * CONTACT_SLOPE / 128.0 / 4.0
     for k in range(structures):
         origin = lax.rem(family + k, structures)
         turn = (structures - k) % structures
         first = origin * sweeps * POINT_ROWS
-        mass = gain_ref[pl.ds(first + 11, sweeps, stride=POINT_ROWS), :]
+        mass = total_ref[pl.ds(first + 11, sweeps, stride=POINT_ROWS), :]
         for place in range(3):
             point = same_ref[pl.ds(turn * sweeps * 4 + place, sweeps, stride=4), :]
             high = rounded(point)
             near = high + rounded(point - high)
             pull = (
-                gain_ref[pl.ds(first + place, sweeps, stride=POINT_ROWS), :]
-                + gain_ref[pl.ds(first + place + 4, sweeps, stride=POINT_ROWS), :]
+                total_ref[pl.ds(first + place, sweeps, stride=POINT_ROWS), :]
+                + total_ref[pl.ds(first + place + 4, sweeps, stride=POINT_ROWS), :]
             )
             out_refs[k][place] = scale * (near * mass - pull)
 
@@ -432,20 +431,18 @@
     received = [messages[0]]
     for k in range(1, structures):
         received.append(lax.ppermute(messages[k], "row", deal[k]))
-    lines = 2 * sizes.chunks + 4 * sizes.band_chunks + 8
     labels = -(-chrom_lengths.shape[0] // 16) * 16
-    tiles, edges = pl.pallas_call(
-        functools.partial(list_kernel, sizes),
+    band, edges = pl.pallas_call(
+        functools.partial(band_kernel, sizes),
         out_shape=[
-            jax.ShapeDtypeStruct((lines, block_size), jnp.int32),
+            jax.ShapeDtypeStruct((4 * sizes.band_chunks + 8, block_size), jnp.int32),
             jax.ShapeDtypeStruct((2, labels, block_size), jnp.int32),
         ],
-        in_specs=[SMEM, VMEM],
+        in_specs=[SMEM],
         out_specs=[VMEM] * 2,
-        scratch_shapes=[pltpu.VMEM((2 * listed // block_size, POINT_ROWS, block_size), jnp.bfloat16)],
         compiler_params=SMALL,
-        name="list_tiles",
-    )(chrom_lengths, jnp.transpose(inter_pairs, (0, 2, 1)))
+        name="band_tiles",
+    )(chrom_lengths)
 
     own_row = pl.pallas_call(
         functools.partial(merge_kernel, 4 * sweeps),
@@ -454,7 +451,7 @@
         out_specs=VMEM,
         compiler_params=SMALL,
         name="merge",
-    )(tiles, *received)
+    )(band, *received)
 
     def device(family, chip, core):
         row = family * share + chip // sizes.half
@@ -492,10 +489,21 @@
     )(marks, *pieces)
     across = lax.ppermute(same, "col", [(i, i ^ 1) for i in range(n_col)])
 
+    tiles = pl.pallas_call(
+        functools.partial(list_kernel, sizes),
+        out_shape=jax.ShapeDtypeStruct((2 * sizes.chunks + 8, block_size), jnp.int32),
+        in_specs=[VMEM, ANY],
+        out_specs=VMEM,
+        scratch_shapes=[pltpu.VMEM((2 * listed // block_size, POINT_ROWS, block_size), jnp.bfloat16)],
+        cost_estimate=pl.CostEstimate(flops=1 << 28, bytes_accessed=1 << 22, transcendentals=0),
+        compiler_params=SMALL,
+        name="list_tiles",
+    )(jnp.transpose(inter_pairs, (0, 2, 1)), same)
+
     gains = pl.pallas_call(
         functools.partial(tile_kernel, sizes),
         out_shape=[jax.ShapeDtypeStruct((3, sweeps, block_size), jnp.float32)] * structures,
-        in_specs=[SMEM] + [VMEM] * 5,
+        in_specs=[SMEM] * 2 + [VMEM] * 5,
         out_specs=[VMEM] * structures,
         scratch_shapes=[
             pltpu.VMEM((blocks, POINT_ROWS, block_size), jnp.bfloat16),
@@ -504,12 +512,11 @@
             pltpu.VMEM((UNIT * 8, block_size), jnp.float32),
             pltpu.VMEM((UNIT, block_size), jnp.float32),
             pltpu.VMEM((UNIT, block_size), jnp.int32),
-            pltpu.VMEM((slots + 1, block_size, 2 * POINT_ROWS), jnp.float32),
-            pltpu.VMEM((slots * POINT_ROWS, block_size), jnp.float32),
+            pltpu.VMEM(((slots + 1) * POINT_ROWS, block_size), jnp.float32),
         ],
         compiler_params=pltpu.CompilerParams(vmem_limit_bytes=40 * 1024 * 1024),
         name="tiles",
-    )(tiles, inter_counts, own, marks, same, across)
+    )(band, tiles, inter_counts, own, marks, same, across)
 
     arrived = [gains[0]]
     for k in range(1, structures):

time: 50.8 us -> 50 us (0.984); the launches traced: 50.1 us -> 51 us
  local copies, waits for them, and re-layouts: 2.93 us -> 2.18 us
  starting transfers between devices: 14.5 us -> 15.2 us
  waiting for transfers between devices: 6.43 us -> 7.05 us
    ppermute x3, waiting for transfers between devices: 2.23 us -> 3.69 us  [on_device(): arrived.append(lax.ppermute(gains[k], 'row', deal[k]))]
    ppermute x1, waiting for transfers between devices: 1.55 us -> 0.15 us  [on_device(): across = lax.ppermute(same, 'col', [(i, i ^ 1) for i in range(n_col)])]
    unnamed x10, local copies, waits for them, and re-layouts: 2.93 us -> 2.18 us
    ppermute x3, starting transfers between devices: 3.87 us -> 4.61 us  [on_device(): arrived.append(lax.ppermute(gains[k], 'row', deal[k]))]
    ppermute x3, waiting for transfers between devices: 0.01 us -> 0.57 us  [on_device(): received.append(lax.ppermute(messages[k], 'row', deal[k]))]
    pallas_call x1 -> x2, Pallas kernels: 2.57 us -> 2.57 us  [the longest x1 1.39 us: on_device(): pl.pallas_call(functools.partial(list_kernel, sizes), out_shape=jax.Shape...]
  transfers between devices with their start and end apart: 10 -> 10, of which waited for: 5 -> 7; matrix products, arithmetic and copies ran while one was open for 0% -> 0% of each run, Pallas kernels for 9% -> 9%
where the time goes in v7:
time: 50 us; the launch traced here: 51 us
  Pallas kernels  26.4 us (53%)
  starting transfers between devices  15.2 us (30%)
  waiting for transfers between devices  7.05 us (14%)
  local copies, waits for them, and re-layouts  2.18 us (4%)
    pallas_call x1, Pallas kernels, on_device(): pl.pallas_call(functools.partial(tile_kernel, sizes), out_shape=[jax.Shap...  21.1 us
    ppermute x3, starting transfers between devices, on_device(): received.append(lax.ppermute(messages[k], 'row', deal[k]))  6.96 us
    ppermute x3, starting transfers between devices, on_device(): arrived.append(lax.ppermute(gains[k], 'row', deal[k]))  4.61 us
    ppermute x3, waiting for transfers between devices, on_device(): arrived.append(lax.ppermute(gains[k], 'row', deal[k]))  3.69 us
    ppermute x3, starting transfers between devices, on_device(): pieces.append(lax.ppermute(own_row, AXES, moves))  3.6 us
    ppermute x3, waiting for transfers between devices, on_device(): pieces.append(lax.ppermute(own_row, AXES, moves))  2.64 us
    unnamed x10, local copies, waits for them, and re-layouts  2.18 us
    pallas_call x1, Pallas kernels, on_device(): pl.pallas_call(functools.partial(own_kernel, sizes), out_shape=[jax.Shape...  1.96 us
  transfers between devices with their start and end apart: 10, of which 7 were waited for; matrix products, arithmetic and copies ran while one was open for 0% of the time, Pallas kernels for 9%

profile of v7, /device:TPU:0, one launch (start us, length us, event | category | flops | bytes accessed | tf_op | source)
XLA Modules:
  0.0 51.0 jit_solution(3387545836866194222)
XLA Ops:
  0.0 0.0 copy-start
  0.0 0.8 %copy-done = f32[4,3,8,128]{3,2,1,0:T(8,128)S(1)} copy-done((f32[4,3,8,128]{3,2,1,0:T(8,128)S(1)}, f32[4,3,8,128]{3,2,1,0:T(8,128)}, u32[]{:S(2)}) %copy-start) | copy-done | bytes 49176
  0.8 0.0 copy-start.2
  0.8 0.7 %copy-done.2 = s32[4,8,1,32]{3,2,1,0:T(1,128)S(1)} copy-done((s32[4,8,1,32]{3,2,1,0:T(1,128)S(1)}, s32[4,8,1,32]{3,2,1,0:T(1,128)}, u32[]{:S(2)}) %copy-start.2) | copy-done | bytes 4120
  1.5 0.0 copy-start.3
  1.5 0.0 copy-start.1
  1.5 0.1 pack.1
  1.7 3.0 %collective-permute-start = (f32[40,128]{1,0:T(8,128)S(1)}, f32[40,128]{1,0:T(8,128)S(1)}, u32[]{:S(2)}, u32[]{:S(2)}) collective-permute-start(f32[40,128]{1,0:T(8,128)S(1)} %get-tuple-element.20), channel_id=1, source_target_pairs={{0,8},{4,12},{8,16},{12,20},{16,24},{20,28},{24,0},{28,4},{1,9},{5... | collective-permute-start | bytes 61448 | tf_op jit(solution)/shard_map/ppermute | solution.py:433
  4.7 2.6 %collective-permute-start.1 = (f32[40,128]{1,0:T(8,128)S(1)}, f32[40,128]{1,0:T(8,128)S(1)}, u32[]{:S(2)}, u32[]{:S(2)}) collective-permute-start(f32[40,128]{1,0:T(8,128)S(1)} %get-tuple-element.21), channel_id=1, source_target_pairs={{0,16},{4,20},{8,24},{12,28},{16,0},{20,4},{24,8},{28,12},{1,17},{... | collective-permute-start | bytes 61448 | tf_op jit(solution)/shard_map/ppermute | solution.py:433
  7.3 1.3 %collective-permute-start.2 = (f32[40,128]{1,0:T(8,128)S(1)}, f32[40,128]{1,0:T(8,128)S(1)}, u32[]{:S(2)}, u32[]{:S(2)}) collective-permute-start(f32[40,128]{1,0:T(8,128)S(1)} %get-tuple-element.22), channel_id=1, source_target_pairs={{0,24},{4,28},{8,0},{12,4},{16,8},{20,12},{24,16},{28,20},{1,25},{... | collective-permute-start | bytes 61448 | tf_op jit(solution)/shard_map/ppermute | solution.py:433
  8.6 0.0 copy-start.4
  8.6 0.7 %copy-done.4 = s32[46]{0:T(128)S(1)} copy-done((s32[46]{0:T(128)S(1)}, s32[46]{0:T(128)}, u32[]{:S(2)}) %copy-start.4) | copy-done | bytes 208
  9.3 1.2 %band_tiles.1 = (s32[44,128]{1,0:T(8,128)S(1)}, s32[2,48,128]{2,1,0:T(8,128)S(1)}) custom-call(s32[46]{0:T(128)S(1)} %copy-done.4), custom_call_target="tpu_custom_call" | custom-call | tf_op jit(solution)/shard_map/band_tiles/pallas_call | solution.py:435
  10.5 0.0 collective-permute-done.refs_1_
  10.5 0.0 collective-permute-done.1.refs_2_
  10.5 0.6 %collective-permute-done.2.refs_3_ = f32[40,128]{1,0:T(8,128)S(1)} collective-permute-done((f32[40,128]{1,0:T(8,128)S(1)}, f32[40,128]{1,0:T(8,128)S(1)}, u32[]{:S(2)}, u32[]{:S(2)}) %collective-permute-start.2) | collective-permute-done | bytes 20512 | tf_op jit(solution)/shard_map/ppermute | solution.py:433
  11.1 2.5 %collective-permute-start.5 = (f32[136,128]{1,0:T(8,128)S(1)}, f32[136,128]{1,0:T(8,128)S(1)}, u32[]{:S(2)}, u32[]{:S(2)}) collective-permute-start(f32[136,128]{1,0:T(8,128)S(1)} %merge.1.own_ref.refs_0_), channel_id=1, source_target_pairs={{0,6},{1,7},{2,0},{3,1},{4,2},{5,3},{6,4},{7,5},{8,14},{9,15},{10,... | collective-permute-start | bytes 208904 | tf_op jit(solution)/shard_map/ppermute | solution.py:468
  13.6 0.5 collective-permute-start.4
  14.1 0.6 %collective-permute-start.3 = (f32[136,128]{1,0:T(8,128)S(1)}, f32[136,128]{1,0:T(8,128)S(1)}, u32[]{:S(2)}, u32[]{:S(2)}) collective-permute-start(f32[136,128]{1,0:T(8,128)S(1)} %merge.1.own_ref.refs_0_), channel_id=1, source_target_pairs={{0,2},{1,3},{2,4},{3,5},{4,6},{5,7},{6,0},{7,1},{8,10},{9,11},{10,... | collective-permute-start | bytes 208904 | tf_op jit(solution)/shard_map/ppermute | solution.py:468
  14.7 2.0 %own_features.1 = (bf16[64,128,64]{2,1,0:T(8,128)(2,1)S(1)}, bf16[256,48,128]{2,1,0:T(8,128)(2,1)S(1)}) custom-call(s32[2,48,128]{2,1,0:T(8,128)S(1)} %get-tuple-element.18.edges_ref, f32[136,128]{1,0:T(8,128)S(1)} %merge.1.own_ref.refs_0_), custom_call_target="tpu_custom_call" | custom-call | tf_op jit(solution)/shard_map/own_features/pallas_call | solution.py:470
  16.6 0.0 collective-permute-done.5.refs_3_
  16.6 1.2 %collective-permute-done.4.refs_2_ = f32[136,128]{1,0:T(8,128)S(1)} collective-permute-done((f32[136,128]{1,0:T(8,128)S(1)}, f32[136,128]{1,0:T(8,128)S(1)}, u32[]{:S(2)}, u32[]{:S(2)}) %collective-permute-start.4) | collective-permute-done | bytes 69664 | tf_op jit(solution)/shard_map/ppermute | solution.py:468
  17.9 1.4 %collective-permute-done.3.refs_1_ = f32[136,128]{1,0:T(8,128)S(1)} collective-permute-done((f32[136,128]{1,0:T(8,128)S(1)}, f32[136,128]{1,0:T(8,128)S(1)}, u32[]{:S(2)}, u32[]{:S(2)}) %collective-permute-start.3) | collective-permute-done | bytes 69664 | tf_op jit(solution)/shard_map/ppermute | solution.py:468
  19.3 0.1 collective-permute-start.6
  19.4 0.0 copy-done.3
  19.4 1.4 %list_tiles.1.list_ref = s32[42,128]{1,0:T(8,128)S(1)} custom-call(s32[4,2,1024]{2,1,0:T(2,128)S(1)} %bitcast.1, f32[544,128]{1,0:T(8,128)S(1)} %join.1.after_ref.same_ref), custom_call_target="tpu_custom_call" | custom-call | flops 268435456 | bytes 4194304 | tf_op jit(solution)/shard_map/list_tiles/pallas_call | solution.py:492
  20.8 0.1 collective-permute-done.6.across_ref
  20.9 0.0 copy-done.1
  20.9 21.1 %tiles.1 = (f32[3,8,128]{2,1,0:T(8,128)S(1)}, f32[3,8,128]{2,1,0:T(8,128)S(1)}, f32[3,8,128]{2,1,0:T(8,128)S(1)}, f32[3,8,128]{2,1,0:T(8,128)S(1)}) custom-call(s32[44,128]{1,0:T(8,128)S(1)} %get-tuple-element.17.after_ref.band_ref, s32[42,128]{1,0:T(8,128)S(1)} %list_tiles.1.list_ref, s32[4,1024]{1,0:T(4,128)S(1)} %copy-done.1, ...), custom_call_target="tpu_custom_call" | custom-call | tf_op jit(solution)/shard_map/tiles/pallas_call | solution.py:503
  42.0 0.1 collective-permute-start.7
  42.1 4.5 %collective-permute-start.8 = (f32[3,8,128]{2,1,0:T(8,128)S(1)}, f32[3,8,128]{2,1,0:T(8,128)S(1)}, u32[]{:S(2)}, u32[]{:S(2)}) collective-permute-start(f32[3,8,128]{2,1,0:T(8,128)S(1)} %get-tuple-element.27), channel_id=1, source_target_pairs={{0,16},{4,20},{8,24},{12,28},{16,0},{20,4},{24,8},{28,12},{1,17},{... | collective-permute-start | bytes 36872 | tf_op jit(solution)/shard_map/ppermute | solution.py:523
  46.6 0.0 collective-permute-start.9
  46.6 1.1 %collective-permute-done.7.refs_1_ = f32[3,8,128]{2,1,0:T(8,128)S(1)} collective-permute-done((f32[3,8,128]{2,1,0:T(8,128)S(1)}, f32[3,8,128]{2,1,0:T(8,128)S(1)}, u32[]{:S(2)}, u32[]{:S(2)}) %collective-permute-start.7) | collective-permute-done | bytes 12320 | tf_op jit(solution)/shard_map/ppermute | solution.py:523
  47.7 0.6 %collective-permute-done.8.refs_2_ = f32[3,8,128]{2,1,0:T(8,128)S(1)} collective-permute-done((f32[3,8,128]{2,1,0:T(8,128)S(1)}, f32[3,8,128]{2,1,0:T(8,128)S(1)}, u32[]{:S(2)}, u32[]{:S(2)}) %collective-permute-start.8) | collective-permute-done | bytes 12320 | tf_op jit(solution)/shard_map/ppermute | solution.py:523
  48.3 2.0 %collective-permute-done.9.refs_3_ = f32[3,8,128]{2,1,0:T(8,128)S(1)} collective-permute-done((f32[3,8,128]{2,1,0:T(8,128)S(1)}, f32[3,8,128]{2,1,0:T(8,128)S(1)}, u32[]{:S(2)}, u32[]{:S(2)}) %collective-permute-start.9) | collective-permute-done | bytes 12320 | tf_op jit(solution)/shard_map/ppermute | solution.py:523
  50.3 0.6 %place.1 = f32[4,3,8,128]{3,2,1,0:T(8,128)} custom-call(f32[3,8,128]{2,1,0:T(8,128)S(1)} %get-tuple-element.25.refs_0_, f32[3,8,128]{2,1,0:T(8,128)S(1)} %collective-permute-done.7.refs_1_, f32[3,8,128]{2,1,0:T(8,128)S(1)} %collective-permute-done.8.refs_2_, f32[3,8,128]{2,1,0:T(8,128)S(1)} %collective-permute-done.9.refs_3_), custom_call_target="tpu_custom_call" | custom-call | tf_op jit(solution)/shard_map/place/pallas_call | solution.py:524
  (2 shorter events, 0.0 us)
Async XLA Ops:
  0.0 0.8 %copy-start = (f32[4,3,8,128]{3,2,1,0:T(8,128)S(1)}, f32[4,3,8,128]{3,2,1,0:T(8,128)}, u32[]{:S(2)}) copy-start(f32[4,3,8,128]{3,2,1,0:T(8,128)} %coords_ref.1) | copy-start | bytes 147460
  0.8 0.7 %copy-start.2 = (s32[4,8,1,32]{3,2,1,0:T(1,128)S(1)}, s32[4,8,1,32]{3,2,1,0:T(1,128)}, u32[]{:S(2)}) copy-start(s32[4,8,1,32]{3,2,1,0:T(1,128)} %counts_ref.1) | copy-start | bytes 12292
  1.5 17.9 %copy-start.3 = (s32[4,1024,2]{1,2,0:T(2,128)S(1)}, s32[4,1024,2]{1,2,0:T(2,128)}, u32[]{:S(2)}) copy-start(s32[4,1024,2]{1,2,0:T(2,128)} %param.8) | copy-start | bytes 98308
  1.5 19.4 %copy-start.1 = (s32[4,1024]{1,0:T(4,128)S(1)}, s32[4,1024]{1,0:T(4,128)}, u32[]{:S(2)}) copy-start(s32[4,1024]{1,0:T(4,128)} %listed_ref.1) | copy-start | bytes 49156
  1.7 8.8 %collective-permute-start = (f32[40,128]{1,0:T(8,128)S(1)}, f32[40,128]{1,0:T(8,128)S(1)}, u32[]{:S(2)}, u32[]{:S(2)}) collective-permute-start(f32[40,128]{1,0:T(8,128)S(1)} %get-tuple-element.20), channel_id=1, source_target_pairs={{0,8},{4,12},{8,16},{12,20},{16,24},{20,28},{24,0},{28,4},{1,9},{5... | collective-permute-start | bytes 61448 | tf_op jit(solution)/shard_map/ppermute | solution.py:433
  4.7 5.8 %collective-permute-start.1 = (f32[40,128]{1,0:T(8,128)S(1)}, f32[40,128]{1,0:T(8,128)S(1)}, u32[]{:S(2)}, u32[]{:S(2)}) collective-permute-start(f32[40,128]{1,0:T(8,128)S(1)} %get-tuple-element.21), channel_id=1, source_target_pairs={{0,16},{4,20},{8,24},{12,28},{16,0},{20,4},{24,8},{28,12},{1,17},{... | collective-permute-start | bytes 61448 | tf_op jit(solution)/shard_map/ppermute | solution.py:433
  7.3 3.8 %collective-permute-start.2 = (f32[40,128]{1,0:T(8,128)S(1)}, f32[40,128]{1,0:T(8,128)S(1)}, u32[]{:S(2)}, u32[]{:S(2)}) collective-permute-start(f32[40,128]{1,0:T(8,128)S(1)} %get-tuple-element.22), channel_id=1, source_target_pairs={{0,24},{4,28},{8,0},{12,4},{16,8},{20,12},{24,16},{28,20},{1,25},{... | collective-permute-start | bytes 61448 | tf_op jit(solution)/shard_map/ppermute | solution.py:433
  8.6 0.7 %copy-start.4 = (s32[46]{0:T(128)S(1)}, s32[46]{0:T(128)}, u32[]{:S(2)}) copy-start(s32[46]{0:T(128)} %lengths_ref.1) | copy-start | bytes 556
  11.1 5.6 %collective-permute-start.5 = (f32[136,128]{1,0:T(8,128)S(1)}, f32[136,128]{1,0:T(8,128)S(1)}, u32[]{:S(2)}, u32[]{:S(2)}) collective-permute-start(f32[136,128]{1,0:T(8,128)S(1)} %merge.1.own_ref.refs_0_), channel_id=1, source_target_pairs={{0,6},{1,7},{2,0},{3,1},{4,2},{5,3},{6,4},{7,5},{8,14},{9,15},{10,... | collective-permute-start | bytes 208904 | tf_op jit(solution)/shard_map/ppermute | solution.py:468
  13.6 4.3 %collective-permute-start.4 = (f32[136,128]{1,0:T(8,128)S(1)}, f32[136,128]{1,0:T(8,128)S(1)}, u32[]{:S(2)}, u32[]{:S(2)}) collective-permute-start(f32[136,128]{1,0:T(8,128)S(1)} %merge.1.own_ref.refs_0_), channel_id=1, source_target_pairs={{0,4},{1,5},{2,6},{3,7},{4,0},{5,1},{6,2},{7,3},{8,12},{9,13},{10,... | collective-permute-start | bytes 208904 | tf_op jit(solution)/shard_map/ppermute | solution.py:468
  14.1 5.2 %collective-permute-start.3 = (f32[136,128]{1,0:T(8,128)S(1)}, f32[136,128]{1,0:T(8,128)S(1)}, u32[]{:S(2)}, u32[]{:S(2)}) collective-permute-start(f32[136,128]{1,0:T(8,128)S(1)} %merge.1.own_ref.refs_0_), channel_id=1, source_target_pairs={{0,2},{1,3},{2,4},{3,5},{4,6},{5,7},{6,0},{7,1},{8,10},{9,11},{10,... | collective-permute-start | bytes 208904 | tf_op jit(solution)/shard_map/ppermute | solution.py:468
  19.3 1.6 %collective-permute-start.6 = (f32[544,128]{1,0:T(8,128)S(1)}, f32[544,128]{1,0:T(8,128)S(1)}, u32[]{:S(2)}, u32[]{:S(2)}) collective-permute-start(f32[544,128]{1,0:T(8,128)S(1)} %join.1.after_ref.same_ref), channel_id=1, source_target_pairs={{0,1},{1,0},{2,3},{3,2},{4,5},{5,4},{6,7},{7,6},{8,9},{9,8},{10,11... | collective-permute-start | bytes 835592 | tf_op jit(solution)/shard_map/ppermute | solution.py:490
  42.0 5.7 %collective-permute-start.7 = (f32[3,8,128]{2,1,0:T(8,128)S(1)}, f32[3,8,128]{2,1,0:T(8,128)S(1)}, u32[]{:S(2)}, u32[]{:S(2)}) collective-permute-start(f32[3,8,128]{2,1,0:T(8,128)S(1)} %get-tuple-element.26), channel_id=1, source_target_pairs={{0,8},{4,12},{8,16},{12,20},{16,24},{20,28},{24,0},{28,4},{1,9},{5... | collective-permute-start | bytes 36872 | tf_op jit(solution)/shard_map/ppermute | solution.py:523
  42.1 6.2 %collective-permute-start.8 = (f32[3,8,128]{2,1,0:T(8,128)S(1)}, f32[3,8,128]{2,1,0:T(8,128)S(1)}, u32[]{:S(2)}, u32[]{:S(2)}) collective-permute-start(f32[3,8,128]{2,1,0:T(8,128)S(1)} %get-tuple-element.27), channel_id=1, source_target_pairs={{0,16},{4,20},{8,24},{12,28},{16,0},{20,4},{24,8},{28,12},{1,17},{... | collective-permute-start | bytes 36872 | tf_op jit(solution)/shard_map/ppermute | solution.py:523
  46.6 3.7 %collective-permute-start.9 = (f32[3,8,128]{2,1,0:T(8,128)S(1)}, f32[3,8,128]{2,1,0:T(8,128)S(1)}, u32[]{:S(2)}, u32[]{:S(2)}) collective-permute-start(f32[3,8,128]{2,1,0:T(8,128)S(1)} %get-tuple-element.28), channel_id=1, source_target_pairs={{0,24},{4,28},{8,0},{12,4},{16,8},{20,12},{24,16},{28,20},{1,25},{... | collective-permute-start | bytes 36872 | tf_op jit(solution)/shard_map/ppermute | solution.py:523

commit v8 on v7

--- a/solution.py
+++ b/solution.py
@@ -11,7 +11,7 @@
 CONTACT_SLOPE = 0.5
 BACKGROUND = 0.5
 FAR = 32.0
-UNIT = 32
+UNIT = 64
 POINT_ROWS = 16
 AXES = ("row", "col")
 VMEM = pl.BlockSpec(memory_space=pltpu.VMEM)
@@ -274,7 +274,7 @@
 def tile_kernel(sizes, band_ref, list_ref, listed_ref, first_ref, marks_ref, same_ref, across_ref, *refs):
     structures, sweeps, slots, groups = sizes.structures, sizes.sweeps, sizes.slots, sizes.groups
     out_refs = refs[:structures]
-    second_ref, counts_ref, held_ref, sums_ref, picks_ref, state_ref, total_ref = refs[structures:]
+    second_ref, counts_ref, held_ref, sums_ref, picks_ref, state_ref, total_ref, gain_ref = refs[structures:]
     row_here = lax.axis_index("row")
     column_here = lax.axis_index("col")
     family = lax.div(row_here, sizes.share)
@@ -283,6 +283,7 @@
     lane = lax.broadcasted_iota(jnp.int32, (1, 128), 1)
     row = lax.broadcasted_iota(jnp.int32, (8, 128), 0)
     ones = jnp.where((row == 3) | (row == 4), 1.0, 0.0)
+    narrow = lax.broadcasted_iota(jnp.int32, (1, 2 * POINT_ROWS), 1)
 
     for core, piece_ref in ((core_here, same_ref), (1 - core_here, across_ref)):
         for k in range(sizes.chips):
@@ -335,12 +336,14 @@
                 [jnp.concatenate([left, blank], axis=1), jnp.concatenate([blank, right], axis=1)], axis=0
             )
             product = lax.dot_general(
-                both, held_ref[t // 2], (((1,), (1,)), ((), ())), preferred_element_type=jnp.float32
-            )
-            at = pl.multiple_of(((ending[t] >> 19) & 127) * POINT_ROWS, POINT_ROWS)
-            total_ref[pl.ds(at, POINT_ROWS), :] += (
-                weight[t : t + 1] * product[:POINT_ROWS] + weight[t + 1 : t + 2] * product[POINT_ROWS:]
-            )
+                held_ref[t // 2], both, (((1,), (1,)), ((), ())), preferred_element_type=jnp.float32
+            )
+            scale = jnp.where(
+                narrow < POINT_ROWS,
+                weight[t : t + 1, : 2 * POINT_ROWS],
+                weight[t + 1 : t + 2, : 2 * POINT_ROWS],
+            )
+            total_ref[(ending[t] >> 19) & 127] += scale * product
 
     def begin(beginning):
         for t in range(0, UNIT, 2):
@@ -386,19 +389,27 @@
     listed_steps = lax.div(list_ref[2 * chunks, 0] + UNIT - 1, UNIT)
     finish(lax.fori_loop(0, listed_steps, listed_step, ending))
 
+    def collect(slot, carry):
+        turned = jnp.transpose(total_ref[slot])
+        gain_ref[pl.ds(pl.multiple_of(slot * POINT_ROWS, POINT_ROWS), POINT_ROWS), :] = (
+            turned[:POINT_ROWS] + turned[POINT_ROWS:]
+        )
+        return carry
+
+    lax.fori_loop(0, slots, collect, 0, unroll=8)
     scale = -2.0 * CONTACT_SLOPE / 128.0 / 4.0
     for k in range(structures):
         origin = lax.rem(family + k, structures)
         turn = (structures - k) % structures
         first = origin * sweeps * POINT_ROWS
-        mass = total_ref[pl.ds(first + 11, sweeps, stride=POINT_ROWS), :]
+        mass = gain_ref[pl.ds(first + 11, sweeps, stride=POINT_ROWS), :]
         for place in range(3):
             point = same_ref[pl.ds(turn * sweeps * 4 + place, sweeps, stride=4), :]
             high = rounded(point)
             near = high + rounded(point - high)
             pull = (
-                total_ref[pl.ds(first + place, sweeps, stride=POINT_ROWS), :]
-                + total_ref[pl.ds(first + place + 4, sweeps, stride=POINT_ROWS), :]
+                gain_ref[pl.ds(first + place, sweeps, stride=POINT_ROWS), :]
+                + gain_ref[pl.ds(first + place + 4, sweeps, stride=POINT_ROWS), :]
             )
             out_refs[k][place] = scale * (near * mass - pull)
 
@@ -512,7 +523,8 @@
             pltpu.VMEM((UNIT * 8, block_size), jnp.float32),
             pltpu.VMEM((UNIT, block_size), jnp.float32),
             pltpu.VMEM((UNIT, block_size), jnp.int32),
-            pltpu.VMEM(((slots + 1) * POINT_ROWS, block_size), jnp.float32),
+            pltpu.VMEM((slots + 1, block_size, 2 * POINT_ROWS), jnp.float32),
+            pltpu.VMEM((slots * POINT_ROWS, block_size), jnp.float32),
         ],
         compiler_params=pltpu.CompilerParams(vmem_limit_bytes=40 * 1024 * 1024),
         name="tiles",

time: 50 us -> 50.4 us (level); the launches traced: 51 us -> 50.1 us
  starting transfers between devices: 15.2 us -> 14.5 us
    ppermute x3, starting transfers between devices: 4.61 us -> 3.89 us  [on_device(): arrived.append(lax.ppermute(gains[k], 'row', deal[k]))]
  transfers between devices with their start and end apart: 10 -> 10, of which waited for: 7 -> 6; matrix products, arithmetic and copies ran while one was open for 0% -> 0% of each run, Pallas kernels for 9% -> 10%
where the time goes in v8:
time: 50.4 us; the launch traced here: 50.1 us
  Pallas kernels  26.5 us (53%)
  starting transfers between devices  14.5 us (29%)
  waiting for transfers between devices  6.78 us (13%)
  local copies, waits for them, and re-layouts  2.18 us (4%)
    pallas_call x1, Pallas kernels, on_device(): pl.pallas_call(functools.partial(tile_kernel, sizes), out_shape=[jax.Shap...  20.9 us
    ppermute x3, starting transfers between devices, on_device(): received.append(lax.ppermute(messages[k], 'row', deal[k]))  6.96 us
    ppermute x3, starting transfers between devices, on_device(): arrived.append(lax.ppermute(gains[k], 'row', deal[k]))  3.89 us
    ppermute x3, starting transfers between devices, on_device(): pieces.append(lax.ppermute(own_row, AXES, moves))  3.6 us
    ppermute x3, waiting for transfers between devices, on_device(): arrived.append(lax.ppermute(gains[k], 'row', deal[k]))  3.59 us
    ppermute x3, waiting for transfers between devices, on_device(): pieces.append(lax.ppermute(own_row, AXES, moves))  2.64 us
    unnamed x10, local copies, waits for them, and re-layouts  2.18 us
    pallas_call x1, Pallas kernels, on_device(): pl.pallas_call(functools.partial(own_kernel, sizes), out_shape=[jax.Shape...  1.96 us
  transfers between devices with their start and end apart: 10, of which 6 were waited for; matrix products, arithmetic and copies ran while one was open for 0% of the time, Pallas kernels for 10%

profile of v8, /device:TPU:0, one launch (start us, length us, event | category | flops | bytes accessed | tf_op | source)
XLA Modules:
  0.0 50.1 jit_solution(11005061876303866474)
XLA Ops:
  0.0 0.0 copy-start
  0.0 0.8 %copy-done = f32[4,3,8,128]{3,2,1,0:T(8,128)S(1)} copy-done((f32[4,3,8,128]{3,2,1,0:T(8,128)S(1)}, f32[4,3,8,128]{3,2,1,0:T(8,128)}, u32[]{:S(2)}) %copy-start) | copy-done | bytes 49176
  0.8 0.0 copy-start.2
  0.8 0.7 %copy-done.2 = s32[4,8,1,32]{3,2,1,0:T(1,128)S(1)} copy-done((s32[4,8,1,32]{3,2,1,0:T(1,128)S(1)}, s32[4,8,1,32]{3,2,1,0:T(1,128)}, u32[]{:S(2)}) %copy-start.2) | copy-done | bytes 4120
  1.5 0.0 copy-start.3
  1.5 0.0 copy-start.1
  1.5 0.1 pack.1
  1.7 3.0 %collective-permute-start = (f32[40,128]{1,0:T(8,128)S(1)}, f32[40,128]{1,0:T(8,128)S(1)}, u32[]{:S(2)}, u32[]{:S(2)}) collective-permute-start(f32[40,128]{1,0:T(8,128)S(1)} %get-tuple-element.20), channel_id=1, source_target_pairs={{0,8},{4,12},{8,16},{12,20},{16,24},{20,28},{24,0},{28,4},{1,9},{5... | collective-permute-start | bytes 61448 | tf_op jit(solution)/shard_map/ppermute | solution.py:444
  4.7 2.6 %collective-permute-start.1 = (f32[40,128]{1,0:T(8,128)S(1)}, f32[40,128]{1,0:T(8,128)S(1)}, u32[]{:S(2)}, u32[]{:S(2)}) collective-permute-start(f32[40,128]{1,0:T(8,128)S(1)} %get-tuple-element.21), channel_id=1, source_target_pairs={{0,16},{4,20},{8,24},{12,28},{16,0},{20,4},{24,8},{28,12},{1,17},{... | collective-permute-start | bytes 61448 | tf_op jit(solution)/shard_map/ppermute | solution.py:444
  7.3 1.3 %collective-permute-start.2 = (f32[40,128]{1,0:T(8,128)S(1)}, f32[40,128]{1,0:T(8,128)S(1)}, u32[]{:S(2)}, u32[]{:S(2)}) collective-permute-start(f32[40,128]{1,0:T(8,128)S(1)} %get-tuple-element.22), channel_id=1, source_target_pairs={{0,24},{4,28},{8,0},{12,4},{16,8},{20,12},{24,16},{28,20},{1,25},{... | collective-permute-start | bytes 61448 | tf_op jit(solution)/shard_map/ppermute | solution.py:444
  8.6 0.0 copy-start.4
  8.6 0.7 %copy-done.4 = s32[46]{0:T(128)S(1)} copy-done((s32[46]{0:T(128)S(1)}, s32[46]{0:T(128)}, u32[]{:S(2)}) %copy-start.4) | copy-done | bytes 208
  9.3 1.2 %band_tiles.1 = (s32[44,128]{1,0:T(8,128)S(1)}, s32[2,48,128]{2,1,0:T(8,128)S(1)}) custom-call(s32[46]{0:T(128)S(1)} %copy-done.4), custom_call_target="tpu_custom_call" | custom-call | tf_op jit(solution)/shard_map/band_tiles/pallas_call | solution.py:446
  10.5 0.0 collective-permute-done.refs_1_
  10.5 0.0 collective-permute-done.1.refs_2_
  10.5 0.5 %collective-permute-done.2.refs_3_ = f32[40,128]{1,0:T(8,128)S(1)} collective-permute-done((f32[40,128]{1,0:T(8,128)S(1)}, f32[40,128]{1,0:T(8,128)S(1)}, u32[]{:S(2)}, u32[]{:S(2)}) %collective-permute-start.2) | collective-permute-done | bytes 20512 | tf_op jit(solution)/shard_map/ppermute | solution.py:444
  11.1 2.5 %collective-permute-start.5 = (f32[136,128]{1,0:T(8,128)S(1)}, f32[136,128]{1,0:T(8,128)S(1)}, u32[]{:S(2)}, u32[]{:S(2)}) collective-permute-start(f32[136,128]{1,0:T(8,128)S(1)} %merge.1.own_ref.refs_0_), channel_id=1, source_target_pairs={{0,6},{1,7},{2,0},{3,1},{4,2},{5,3},{6,4},{7,5},{8,14},{9,15},{10,... | collective-permute-start | bytes 208904 | tf_op jit(solution)/shard_map/ppermute | solution.py:479
  13.6 0.5 %collective-permute-start.4 = (f32[136,128]{1,0:T(8,128)S(1)}, f32[136,128]{1,0:T(8,128)S(1)}, u32[]{:S(2)}, u32[]{:S(2)}) collective-permute-start(f32[136,128]{1,0:T(8,128)S(1)} %merge.1.own_ref.refs_0_), channel_id=1, source_target_pairs={{0,4},{1,5},{2,6},{3,7},{4,0},{5,1},{6,2},{7,3},{8,12},{9,13},{10,... | collective-permute-start | bytes 208904 | tf_op jit(solution)/shard_map/ppermute | solution.py:479
  14.1 0.6 %collective-permute-start.3 = (f32[136,128]{1,0:T(8,128)S(1)}, f32[136,128]{1,0:T(8,128)S(1)}, u32[]{:S(2)}, u32[]{:S(2)}) collective-permute-start(f32[136,128]{1,0:T(8,128)S(1)} %merge.1.own_ref.refs_0_), channel_id=1, source_target_pairs={{0,2},{1,3},{2,4},{3,5},{4,6},{5,7},{6,0},{7,1},{8,10},{9,11},{10,... | collective-permute-start | bytes 208904 | tf_op jit(solution)/shard_map/ppermute | solution.py:479
  14.7 2.0 %own_features.1 = (bf16[64,128,64]{2,1,0:T(8,128)(2,1)S(1)}, bf16[256,48,128]{2,1,0:T(8,128)(2,1)S(1)}) custom-call(s32[2,48,128]{2,1,0:T(8,128)S(1)} %get-tuple-element.18.edges_ref, f32[136,128]{1,0:T(8,128)S(1)} %merge.1.own_ref.refs_0_), custom_call_target="tpu_custom_call" | custom-call | tf_op jit(solution)/shard_map/own_features/pallas_call | solution.py:481
  16.6 0.0 collective-permute-done.5.refs_3_
  16.6 1.2 %collective-permute-done.4.refs_2_ = f32[136,128]{1,0:T(8,128)S(1)} collective-permute-done((f32[136,128]{1,0:T(8,128)S(1)}, f32[136,128]{1,0:T(8,128)S(1)}, u32[]{:S(2)}, u32[]{:S(2)}) %collective-permute-start.4) | collective-permute-done | bytes 69664 | tf_op jit(solution)/shard_map/ppermute | solution.py:479
  17.9 1.4 %collective-permute-done.3.refs_1_ = f32[136,128]{1,0:T(8,128)S(1)} collective-permute-done((f32[136,128]{1,0:T(8,128)S(1)}, f32[136,128]{1,0:T(8,128)S(1)}, u32[]{:S(2)}, u32[]{:S(2)}) %collective-permute-start.3) | collective-permute-done | bytes 69664 | tf_op jit(solution)/shard_map/ppermute | solution.py:479
  19.3 0.1 collective-permute-start.6
  19.4 0.0 copy-done.3
  19.4 1.7 %list_tiles.1.list_ref = s32[44,128]{1,0:T(8,128)S(1)} custom-call(s32[4,2,1024]{2,1,0:T(2,128)S(1)} %bitcast.1, f32[544,128]{1,0:T(8,128)S(1)} %join.1.after_ref.same_ref), custom_call_target="tpu_custom_call" | custom-call | flops 268435456 | bytes 4194304 | tf_op jit(solution)/shard_map/list_tiles/pallas_call | solution.py:503
  21.0 0.0 collective-permute-done.6.across_ref
  21.1 0.0 copy-done.1
  21.1 20.9 %tiles.1 = (f32[3,8,128]{2,1,0:T(8,128)S(1)}, f32[3,8,128]{2,1,0:T(8,128)S(1)}, f32[3,8,128]{2,1,0:T(8,128)S(1)}, f32[3,8,128]{2,1,0:T(8,128)S(1)}) custom-call(s32[44,128]{1,0:T(8,128)S(1)} %get-tuple-element.17.after_ref.band_ref, s32[44,128]{1,0:T(8,128)S(1)} %list_tiles.1.list_ref, s32[4,1024]{1,0:T(4,128)S(1)} %copy-done.1, ...), custom_call_target="tpu_custom_call" | custom-call | tf_op jit(solution)/shard_map/tiles/pallas_call | solution.py:514
  42.0 0.3 collective-permute-start.7
  42.3 3.5 %collective-permute-start.8 = (f32[3,8,128]{2,1,0:T(8,128)S(1)}, f32[3,8,128]{2,1,0:T(8,128)S(1)}, u32[]{:S(2)}, u32[]{:S(2)}) collective-permute-start(f32[3,8,128]{2,1,0:T(8,128)S(1)} %get-tuple-element.27), channel_id=1, source_target_pairs={{0,16},{4,20},{8,24},{12,28},{16,0},{20,4},{24,8},{28,12},{1,17},{... | collective-permute-start | bytes 36872 | tf_op jit(solution)/shard_map/ppermute | solution.py:535
  45.8 0.1 collective-permute-start.9
  45.9 1.7 %collective-permute-done.7.refs_1_ = f32[3,8,128]{2,1,0:T(8,128)S(1)} collective-permute-done((f32[3,8,128]{2,1,0:T(8,128)S(1)}, f32[3,8,128]{2,1,0:T(8,128)S(1)}, u32[]{:S(2)}, u32[]{:S(2)}) %collective-permute-start.7) | collective-permute-done | bytes 12320 | tf_op jit(solution)/shard_map/ppermute | solution.py:535
  47.6 0.2 collective-permute-done.8.refs_2_
  47.7 1.8 %collective-permute-done.9.refs_3_ = f32[3,8,128]{2,1,0:T(8,128)S(1)} collective-permute-done((f32[3,8,128]{2,1,0:T(8,128)S(1)}, f32[3,8,128]{2,1,0:T(8,128)S(1)}, u32[]{:S(2)}, u32[]{:S(2)}) %collective-permute-start.9) | collective-permute-done | bytes 12320 | tf_op jit(solution)/shard_map/ppermute | solution.py:535
  49.5 0.6 %place.1 = f32[4,3,8,128]{3,2,1,0:T(8,128)} custom-call(f32[3,8,128]{2,1,0:T(8,128)S(1)} %get-tuple-element.25.refs_0_, f32[3,8,128]{2,1,0:T(8,128)S(1)} %collective-permute-done.7.refs_1_, f32[3,8,128]{2,1,0:T(8,128)S(1)} %collective-permute-done.8.refs_2_, f32[3,8,128]{2,1,0:T(8,128)S(1)} %collective-permute-done.9.refs_3_), custom_call_target="tpu_custom_call" | custom-call | tf_op jit(solution)/shard_map/place/pallas_call | solution.py:536
  (2 shorter events, 0.0 us)
Async XLA Ops:
  0.0 0.8 %copy-start = (f32[4,3,8,128]{3,2,1,0:T(8,128)S(1)}, f32[4,3,8,128]{3,2,1,0:T(8,128)}, u32[]{:S(2)}) copy-start(f32[4,3,8,128]{3,2,1,0:T(8,128)} %coords_ref.1) | copy-start | bytes 147460
  0.8 0.7 %copy-start.2 = (s32[4,8,1,32]{3,2,1,0:T(1,128)S(1)}, s32[4,8,1,32]{3,2,1,0:T(1,128)}, u32[]{:S(2)}) copy-start(s32[4,8,1,32]{3,2,1,0:T(1,128)} %counts_ref.1) | copy-start | bytes 12292
  1.5 17.9 %copy-start.3 = (s32[4,1024,2]{1,2,0:T(2,128)S(1)}, s32[4,1024,2]{1,2,0:T(2,128)}, u32[]{:S(2)}) copy-start(s32[4,1024,2]{1,2,0:T(2,128)} %param.8) | copy-start | bytes 98308
  1.5 19.5 %copy-start.1 = (s32[4,1024]{1,0:T(4,128)S(1)}, s32[4,1024]{1,0:T(4,128)}, u32[]{:S(2)}) copy-start(s32[4,1024]{1,0:T(4,128)} %listed_ref.1) | copy-start | bytes 49156
  1.7 8.8 %collective-permute-start = (f32[40,128]{1,0:T(8,128)S(1)}, f32[40,128]{1,0:T(8,128)S(1)}, u32[]{:S(2)}, u32[]{:S(2)}) collective-permute-start(f32[40,128]{1,0:T(8,128)S(1)} %get-tuple-element.20), channel_id=1, source_target_pairs={{0,8},{4,12},{8,16},{12,20},{16,24},{20,28},{24,0},{28,4},{1,9},{5... | collective-permute-start | bytes 61448 | tf_op jit(solution)/shard_map/ppermute | solution.py:444
  4.7 5.8 %collective-permute-start.1 = (f32[40,128]{1,0:T(8,128)S(1)}, f32[40,128]{1,0:T(8,128)S(1)}, u32[]{:S(2)}, u32[]{:S(2)}) collective-permute-start(f32[40,128]{1,0:T(8,128)S(1)} %get-tuple-element.21), channel_id=1, source_target_pairs={{0,16},{4,20},{8,24},{12,28},{16,0},{20,4},{24,8},{28,12},{1,17},{... | collective-permute-start | bytes 61448 | tf_op jit(solution)/shard_map/ppermute | solution.py:444
  7.3 3.8 %collective-permute-start.2 = (f32[40,128]{1,0:T(8,128)S(1)}, f32[40,128]{1,0:T(8,128)S(1)}, u32[]{:S(2)}, u32[]{:S(2)}) collective-permute-start(f32[40,128]{1,0:T(8,128)S(1)} %get-tuple-element.22), channel_id=1, source_target_pairs={{0,24},{4,28},{8,0},{12,4},{16,8},{20,12},{24,16},{28,20},{1,25},{... | collective-permute-start | bytes 61448 | tf_op jit(solution)/shard_map/ppermute | solution.py:444
  8.6 0.7 %copy-start.4 = (s32[46]{0:T(128)S(1)}, s32[46]{0:T(128)}, u32[]{:S(2)}) copy-start(s32[46]{0:T(128)} %lengths_ref.1) | copy-start | bytes 556
  11.1 5.6 %collective-permute-start.5 = (f32[136,128]{1,0:T(8,128)S(1)}, f32[136,128]{1,0:T(8,128)S(1)}, u32[]{:S(2)}, u32[]{:S(2)}) collective-permute-start(f32[136,128]{1,0:T(8,128)S(1)} %merge.1.own_ref.refs_0_), channel_id=1, source_target_pairs={{0,6},{1,7},{2,0},{3,1},{4,2},{5,3},{6,4},{7,5},{8,14},{9,15},{10,... | collective-permute-start | bytes 208904 | tf_op jit(solution)/shard_map/ppermute | solution.py:479
  13.6 4.3 %collective-permute-start.4 = (f32[136,128]{1,0:T(8,128)S(1)}, f32[136,128]{1,0:T(8,128)S(1)}, u32[]{:S(2)}, u32[]{:S(2)}) collective-permute-start(f32[136,128]{1,0:T(8,128)S(1)} %merge.1.own_ref.refs_0_), channel_id=1, source_target_pairs={{0,4},{1,5},{2,6},{3,7},{4,0},{5,1},{6,2},{7,3},{8,12},{9,13},{10,... | collective-permute-start | bytes 208904 | tf_op jit(solution)/shard_map/ppermute | solution.py:479
  14.1 5.2 %collective-permute-start.3 = (f32[136,128]{1,0:T(8,128)S(1)}, f32[136,128]{1,0:T(8,128)S(1)}, u32[]{:S(2)}, u32[]{:S(2)}) collective-permute-start(f32[136,128]{1,0:T(8,128)S(1)} %merge.1.own_ref.refs_0_), channel_id=1, source_target_pairs={{0,2},{1,3},{2,4},{3,5},{4,6},{5,7},{6,0},{7,1},{8,10},{9,11},{10,... | collective-permute-start | bytes 208904 | tf_op jit(solution)/shard_map/ppermute | solution.py:479
  19.3 1.8 %collective-permute-start.6 = (f32[544,128]{1,0:T(8,128)S(1)}, f32[544,128]{1,0:T(8,128)S(1)}, u32[]{:S(2)}, u32[]{:S(2)}) collective-permute-start(f32[544,128]{1,0:T(8,128)S(1)} %join.1.after_ref.same_ref), channel_id=1, source_target_pairs={{0,1},{1,0},{2,3},{3,2},{4,5},{5,4},{6,7},{7,6},{8,9},{9,8},{10,11... | collective-permute-start | bytes 835592 | tf_op jit(solution)/shard_map/ppermute | solution.py:501
  42.0 5.5 %collective-permute-start.7 = (f32[3,8,128]{2,1,0:T(8,128)S(1)}, f32[3,8,128]{2,1,0:T(8,128)S(1)}, u32[]{:S(2)}, u32[]{:S(2)}) collective-permute-start(f32[3,8,128]{2,1,0:T(8,128)S(1)} %get-tuple-element.26), channel_id=1, source_target_pairs={{0,8},{4,12},{8,16},{12,20},{16,24},{20,28},{24,0},{28,4},{1,9},{5... | collective-permute-start | bytes 36872 | tf_op jit(solution)/shard_map/ppermute | solution.py:535
  42.3 5.4 %collective-permute-start.8 = (f32[3,8,128]{2,1,0:T(8,128)S(1)}, f32[3,8,128]{2,1,0:T(8,128)S(1)}, u32[]{:S(2)}, u32[]{:S(2)}) collective-permute-start(f32[3,8,128]{2,1,0:T(8,128)S(1)} %get-tuple-element.27), channel_id=1, source_target_pairs={{0,16},{4,20},{8,24},{12,28},{16,0},{20,4},{24,8},{28,12},{1,17},{... | collective-permute-start | bytes 36872 | tf_op jit(solution)/shard_map/ppermute | solution.py:535
  45.8 3.7 %collective-permute-start.9 = (f32[3,8,128]{2,1,0:T(8,128)S(1)}, f32[3,8,128]{2,1,0:T(8,128)S(1)}, u32[]{:S(2)}, u32[]{:S(2)}) collective-permute-start(f32[3,8,128]{2,1,0:T(8,128)S(1)} %get-tuple-element.28), channel_id=1, source_target_pairs={{0,24},{4,28},{8,0},{12,4},{16,8},{20,12},{24,16},{28,20},{1,25},{... | collective-permute-start | bytes 36872 | tf_op jit(solution)/shard_map/ppermute | solution.py:535

commit v9 on v8

--- a/solution.py
+++ b/solution.py
@@ -11,7 +11,7 @@
 CONTACT_SLOPE = 0.5
 BACKGROUND = 0.5
 FAR = 32.0
-UNIT = 64
+UNIT = 32
 POINT_ROWS = 16
 AXES = ("row", "col")
 VMEM = pl.BlockSpec(memory_space=pltpu.VMEM)

time: 50.4 us -> 50 us (level)
  Pallas kernels: 26.5 us -> 24.9 us
  starting transfers between devices: 14.5 us -> 15.2 us
    pallas_call x1, Pallas kernels: 20.9 us -> 19.6 us  [on_device(): pl.pallas_call(functools.partial(tile_kernel, sizes), out_shape=[jax.Shap...]
    ppermute x3, starting transfers between devices: 3.89 us -> 4.57 us  [on_device(): arrived.append(lax.ppermute(gains[k], 'row', deal[k]))]
  transfers between devices with their start and end apart: 10 -> 10, of which waited for: 6 -> 7; matrix products, arithmetic and copies ran while one was open for 0% -> 0% of each run, Pallas kernels for 10% -> 9%
where the time goes in v9:
time: 50 us; the launch traced here: 49.4 us
  Pallas kernels  24.9 us (50%)
  starting transfers between devices  15.2 us (30%)
  waiting for transfers between devices  7.05 us (14%)
  local copies, waits for them, and re-layouts  2.18 us (4%)
    pallas_call x1, Pallas kernels, on_device(): pl.pallas_call(functools.partial(tile_kernel, sizes), out_shape=[jax.Shap...  19.6 us
    ppermute x3, starting transfers between devices, on_device(): received.append(lax.ppermute(messages[k], 'row', deal[k]))  6.96 us
    ppermute x3, starting transfers between devices, on_device(): arrived.append(lax.ppermute(gains[k], 'row', deal[k]))  4.57 us
    ppermute x3, waiting for transfers between devices, on_device(): arrived.append(lax.ppermute(gains[k], 'row', deal[k]))  3.69 us
    ppermute x3, starting transfers between devices, on_device(): pieces.append(lax.ppermute(own_row, AXES, moves))  3.6 us
    ppermute x3, waiting for transfers between devices, on_device(): pieces.append(lax.ppermute(own_row, AXES, moves))  2.64 us
    unnamed x10, local copies, waits for them, and re-layouts  2.18 us
    pallas_call x1, Pallas kernels, on_device(): pl.pallas_call(functools.partial(own_kernel, sizes), out_shape=[jax.Shape...  1.96 us
  transfers between devices with their start and end apart: 10, of which 7 were waited for; matrix products, arithmetic and copies ran while one was open for 0% of the time, Pallas kernels for 9%

profile of v9, /device:TPU:0, one launch (start us, length us, event | category | flops | bytes accessed | tf_op | source)
XLA Modules:
  0.0 49.4 jit_solution(8968019074772161506)
XLA Ops:
  0.0 0.0 copy-start
  0.0 0.8 %copy-done = f32[4,3,8,128]{3,2,1,0:T(8,128)S(1)} copy-done((f32[4,3,8,128]{3,2,1,0:T(8,128)S(1)}, f32[4,3,8,128]{3,2,1,0:T(8,128)}, u32[]{:S(2)}) %copy-start) | copy-done | bytes 49176
  0.8 0.0 copy-start.2
  0.8 0.7 %copy-done.2 = s32[4,8,1,32]{3,2,1,0:T(1,128)S(1)} copy-done((s32[4,8,1,32]{3,2,1,0:T(1,128)S(1)}, s32[4,8,1,32]{3,2,1,0:T(1,128)}, u32[]{:S(2)}) %copy-start.2) | copy-done | bytes 4120
  1.5 0.0 copy-start.3
  1.5 0.0 copy-start.1
  1.5 0.1 pack.1
  1.7 3.0 %collective-permute-start = (f32[40,128]{1,0:T(8,128)S(1)}, f32[40,128]{1,0:T(8,128)S(1)}, u32[]{:S(2)}, u32[]{:S(2)}) collective-permute-start(f32[40,128]{1,0:T(8,128)S(1)} %get-tuple-element.20), channel_id=1, source_target_pairs={{0,8},{4,12},{8,16},{12,20},{16,24},{20,28},{24,0},{28,4},{1,9},{5... | collective-permute-start | bytes 61448 | tf_op jit(solution)/shard_map/ppermute | solution.py:444
  4.7 2.6 %collective-permute-start.1 = (f32[40,128]{1,0:T(8,128)S(1)}, f32[40,128]{1,0:T(8,128)S(1)}, u32[]{:S(2)}, u32[]{:S(2)}) collective-permute-start(f32[40,128]{1,0:T(8,128)S(1)} %get-tuple-element.21), channel_id=1, source_target_pairs={{0,16},{4,20},{8,24},{12,28},{16,0},{20,4},{24,8},{28,12},{1,17},{... | collective-permute-start | bytes 61448 | tf_op jit(solution)/shard_map/ppermute | solution.py:444
  7.3 1.3 %collective-permute-start.2 = (f32[40,128]{1,0:T(8,128)S(1)}, f32[40,128]{1,0:T(8,128)S(1)}, u32[]{:S(2)}, u32[]{:S(2)}) collective-permute-start(f32[40,128]{1,0:T(8,128)S(1)} %get-tuple-element.22), channel_id=1, source_target_pairs={{0,24},{4,28},{8,0},{12,4},{16,8},{20,12},{24,16},{28,20},{1,25},{... | collective-permute-start | bytes 61448 | tf_op jit(solution)/shard_map/ppermute | solution.py:444
  8.6 0.0 copy-start.4
  8.6 0.7 %copy-done.4 = s32[46]{0:T(128)S(1)} copy-done((s32[46]{0:T(128)S(1)}, s32[46]{0:T(128)}, u32[]{:S(2)}) %copy-start.4) | copy-done | bytes 208
  9.3 1.2 %band_tiles.1 = (s32[44,128]{1,0:T(8,128)S(1)}, s32[2,48,128]{2,1,0:T(8,128)S(1)}) custom-call(s32[46]{0:T(128)S(1)} %copy-done.4), custom_call_target="tpu_custom_call" | custom-call | tf_op jit(solution)/shard_map/band_tiles/pallas_call | solution.py:446
  10.5 0.0 collective-permute-done.refs_1_
  10.5 0.0 collective-permute-done.1.refs_2_
  10.5 0.6 %collective-permute-done.2.refs_3_ = f32[40,128]{1,0:T(8,128)S(1)} collective-permute-done((f32[40,128]{1,0:T(8,128)S(1)}, f32[40,128]{1,0:T(8,128)S(1)}, u32[]{:S(2)}, u32[]{:S(2)}) %collective-permute-start.2) | collective-permute-done | bytes 20512 | tf_op jit(solution)/shard_map/ppermute | solution.py:444
  11.1 2.5 %collective-permute-start.5 = (f32[136,128]{1,0:T(8,128)S(1)}, f32[136,128]{1,0:T(8,128)S(1)}, u32[]{:S(2)}, u32[]{:S(2)}) collective-permute-start(f32[136,128]{1,0:T(8,128)S(1)} %merge.1.own_ref.refs_0_), channel_id=1, source_target_pairs={{0,6},{1,7},{2,0},{3,1},{4,2},{5,3},{6,4},{7,5},{8,14},{9,15},{10,... | collective-permute-start | bytes 208904 | tf_op jit(solution)/shard_map/ppermute | solution.py:479
  13.6 0.5 %collective-permute-start.4 = (f32[136,128]{1,0:T(8,128)S(1)}, f32[136,128]{1,0:T(8,128)S(1)}, u32[]{:S(2)}, u32[]{:S(2)}) collective-permute-start(f32[136,128]{1,0:T(8,128)S(1)} %merge.1.own_ref.refs_0_), channel_id=1, source_target_pairs={{0,4},{1,5},{2,6},{3,7},{4,0},{5,1},{6,2},{7,3},{8,12},{9,13},{10,... | collective-permute-start | bytes 208904 | tf_op jit(solution)/shard_map/ppermute | solution.py:479
  14.1 0.6 %collective-permute-start.3 = (f32[136,128]{1,0:T(8,128)S(1)}, f32[136,128]{1,0:T(8,128)S(1)}, u32[]{:S(2)}, u32[]{:S(2)}) collective-permute-start(f32[136,128]{1,0:T(8,128)S(1)} %merge.1.own_ref.refs_0_), channel_id=1, source_target_pairs={{0,2},{1,3},{2,4},{3,5},{4,6},{5,7},{6,0},{7,1},{8,10},{9,11},{10,... | collective-permute-start | bytes 208904 | tf_op jit(solution)/shard_map/ppermute | solution.py:479
  14.7 2.0 %own_features.1 = (bf16[64,128,64]{2,1,0:T(8,128)(2,1)S(1)}, bf16[256,48,128]{2,1,0:T(8,128)(2,1)S(1)}) custom-call(s32[2,48,128]{2,1,0:T(8,128)S(1)} %get-tuple-element.18.edges_ref, f32[136,128]{1,0:T(8,128)S(1)} %merge.1.own_ref.refs_0_), custom_call_target="tpu_custom_call" | custom-call | tf_op jit(solution)/shard_map/own_features/pallas_call | solution.py:481
  16.6 0.0 collective-permute-done.5.refs_3_
  16.6 1.2 %collective-permute-done.4.refs_2_ = f32[136,128]{1,0:T(8,128)S(1)} collective-permute-done((f32[136,128]{1,0:T(8,128)S(1)}, f32[136,128]{1,0:T(8,128)S(1)}, u32[]{:S(2)}, u32[]{:S(2)}) %collective-permute-start.4) | collective-permute-done | bytes 69664 | tf_op jit(solution)/shard_map/ppermute | solution.py:479
  17.9 1.4 %collective-permute-done.3.refs_1_ = f32[136,128]{1,0:T(8,128)S(1)} collective-permute-done((f32[136,128]{1,0:T(8,128)S(1)}, f32[136,128]{1,0:T(8,128)S(1)}, u32[]{:S(2)}, u32[]{:S(2)}) %collective-permute-start.3) | collective-permute-done | bytes 69664 | tf_op jit(solution)/shard_map/ppermute | solution.py:479
  19.3 0.1 collective-permute-start.6
  19.4 0.0 copy-done.3
  19.4 1.4 %list_tiles.1.list_ref = s32[42,128]{1,0:T(8,128)S(1)} custom-call(s32[4,2,1024]{2,1,0:T(2,128)S(1)} %bitcast.1, f32[544,128]{1,0:T(8,128)S(1)} %join.1.after_ref.same_ref), custom_call_target="tpu_custom_call" | custom-call | flops 268435456 | bytes 4194304 | tf_op jit(solution)/shard_map/list_tiles/pallas_call | solution.py:503
  20.8 0.1 collective-permute-done.6.across_ref
  20.9 0.0 copy-done.1
  20.9 19.6 %tiles.1 = (f32[3,8,128]{2,1,0:T(8,128)S(1)}, f32[3,8,128]{2,1,0:T(8,128)S(1)}, f32[3,8,128]{2,1,0:T(8,128)S(1)}, f32[3,8,128]{2,1,0:T(8,128)S(1)}) custom-call(s32[44,128]{1,0:T(8,128)S(1)} %get-tuple-element.17.after_ref.band_ref, s32[42,128]{1,0:T(8,128)S(1)} %list_tiles.1.list_ref, s32[4,1024]{1,0:T(4,128)S(1)} %copy-done.1, ...), custom_call_target="tpu_custom_call" | custom-call | tf_op jit(solution)/shard_map/tiles/pallas_call | solution.py:514
  40.5 0.3 collective-permute-start.7
  40.8 4.3 %collective-permute-start.8 = (f32[3,8,128]{2,1,0:T(8,128)S(1)}, f32[3,8,128]{2,1,0:T(8,128)S(1)}, u32[]{:S(2)}, u32[]{:S(2)}) collective-permute-start(f32[3,8,128]{2,1,0:T(8,128)S(1)} %get-tuple-element.27), channel_id=1, source_target_pairs={{0,16},{4,20},{8,24},{12,28},{16,0},{20,4},{24,8},{28,12},{1,17},{... | collective-permute-start | bytes 36872 | tf_op jit(solution)/shard_map/ppermute | solution.py:535
  45.1 0.0 collective-permute-start.9
  45.1 1.3 %collective-permute-done.7.refs_1_ = f32[3,8,128]{2,1,0:T(8,128)S(1)} collective-permute-done((f32[3,8,128]{2,1,0:T(8,128)S(1)}, f32[3,8,128]{2,1,0:T(8,128)S(1)}, u32[]{:S(2)}, u32[]{:S(2)}) %collective-permute-start.7) | collective-permute-done | bytes 12320 | tf_op jit(solution)/shard_map/ppermute | solution.py:535
  46.3 0.5 collective-permute-done.8.refs_2_
  46.8 2.0 %collective-permute-done.9.refs_3_ = f32[3,8,128]{2,1,0:T(8,128)S(1)} collective-permute-done((f32[3,8,128]{2,1,0:T(8,128)S(1)}, f32[3,8,128]{2,1,0:T(8,128)S(1)}, u32[]{:S(2)}, u32[]{:S(2)}) %collective-permute-start.9) | collective-permute-done | bytes 12320 | tf_op jit(solution)/shard_map/ppermute | solution.py:535
  48.8 0.6 %place.1 = f32[4,3,8,128]{3,2,1,0:T(8,128)} custom-call(f32[3,8,128]{2,1,0:T(8,128)S(1)} %get-tuple-element.25.refs_0_, f32[3,8,128]{2,1,0:T(8,128)S(1)} %collective-permute-done.7.refs_1_, f32[3,8,128]{2,1,0:T(8,128)S(1)} %collective-permute-done.8.refs_2_, f32[3,8,128]{2,1,0:T(8,128)S(1)} %collective-permute-done.9.refs_3_), custom_call_target="tpu_custom_call" | custom-call | tf_op jit(solution)/shard_map/place/pallas_call | solution.py:536
  (2 shorter events, 0.0 us)
Async XLA Ops:
  0.0 0.8 %copy-start = (f32[4,3,8,128]{3,2,1,0:T(8,128)S(1)}, f32[4,3,8,128]{3,2,1,0:T(8,128)}, u32[]{:S(2)}) copy-start(f32[4,3,8,128]{3,2,1,0:T(8,128)} %coords_ref.1) | copy-start | bytes 147460
  0.8 0.7 %copy-start.2 = (s32[4,8,1,32]{3,2,1,0:T(1,128)S(1)}, s32[4,8,1,32]{3,2,1,0:T(1,128)}, u32[]{:S(2)}) copy-start(s32[4,8,1,32]{3,2,1,0:T(1,128)} %counts_ref.1) | copy-start | bytes 12292
  1.5 17.9 %copy-start.3 = (s32[4,1024,2]{1,2,0:T(2,128)S(1)}, s32[4,1024,2]{1,2,0:T(2,128)}, u32[]{:S(2)}) copy-start(s32[4,1024,2]{1,2,0:T(2,128)} %param.8) | copy-start | bytes 98308
  1.5 19.4 %copy-start.1 = (s32[4,1024]{1,0:T(4,128)S(1)}, s32[4,1024]{1,0:T(4,128)}, u32[]{:S(2)}) copy-start(s32[4,1024]{1,0:T(4,128)} %listed_ref.1) | copy-start | bytes 49156
  1.7 8.8 %collective-permute-start = (f32[40,128]{1,0:T(8,128)S(1)}, f32[40,128]{1,0:T(8,128)S(1)}, u32[]{:S(2)}, u32[]{:S(2)}) collective-permute-start(f32[40,128]{1,0:T(8,128)S(1)} %get-tuple-element.20), channel_id=1, source_target_pairs={{0,8},{4,12},{8,16},{12,20},{16,24},{20,28},{24,0},{28,4},{1,9},{5... | collective-permute-start | bytes 61448 | tf_op jit(solution)/shard_map/ppermute | solution.py:444
  4.7 5.8 %collective-permute-start.1 = (f32[40,128]{1,0:T(8,128)S(1)}, f32[40,128]{1,0:T(8,128)S(1)}, u32[]{:S(2)}, u32[]{:S(2)}) collective-permute-start(f32[40,128]{1,0:T(8,128)S(1)} %get-tuple-element.21), channel_id=1, source_target_pairs={{0,16},{4,20},{8,24},{12,28},{16,0},{20,4},{24,8},{28,12},{1,17},{... | collective-permute-start | bytes 61448 | tf_op jit(solution)/shard_map/ppermute | solution.py:444
  7.3 3.8 %collective-permute-start.2 = (f32[40,128]{1,0:T(8,128)S(1)}, f32[40,128]{1,0:T(8,128)S(1)}, u32[]{:S(2)}, u32[]{:S(2)}) collective-permute-start(f32[40,128]{1,0:T(8,128)S(1)} %get-tuple-element.22), channel_id=1, source_target_pairs={{0,24},{4,28},{8,0},{12,4},{16,8},{20,12},{24,16},{28,20},{1,25},{... | collective-permute-start | bytes 61448 | tf_op jit(solution)/shard_map/ppermute | solution.py:444
  8.6 0.7 %copy-start.4 = (s32[46]{0:T(128)S(1)}, s32[46]{0:T(128)}, u32[]{:S(2)}) copy-start(s32[46]{0:T(128)} %lengths_ref.1) | copy-start | bytes 556
  11.1 5.6 %collective-permute-start.5 = (f32[136,128]{1,0:T(8,128)S(1)}, f32[136,128]{1,0:T(8,128)S(1)}, u32[]{:S(2)}, u32[]{:S(2)}) collective-permute-start(f32[136,128]{1,0:T(8,128)S(1)} %merge.1.own_ref.refs_0_), channel_id=1, source_target_pairs={{0,6},{1,7},{2,0},{3,1},{4,2},{5,3},{6,4},{7,5},{8,14},{9,15},{10,... | collective-permute-start | bytes 208904 | tf_op jit(solution)/shard_map/ppermute | solution.py:479
  13.6 4.3 %collective-permute-start.4 = (f32[136,128]{1,0:T(8,128)S(1)}, f32[136,128]{1,0:T(8,128)S(1)}, u32[]{:S(2)}, u32[]{:S(2)}) collective-permute-start(f32[136,128]{1,0:T(8,128)S(1)} %merge.1.own_ref.refs_0_), channel_id=1, source_target_pairs={{0,4},{1,5},{2,6},{3,7},{4,0},{5,1},{6,2},{7,3},{8,12},{9,13},{10,... | collective-permute-start | bytes 208904 | tf_op jit(solution)/shard_map/ppermute | solution.py:479
  14.1 5.2 %collective-permute-start.3 = (f32[136,128]{1,0:T(8,128)S(1)}, f32[136,128]{1,0:T(8,128)S(1)}, u32[]{:S(2)}, u32[]{:S(2)}) collective-permute-start(f32[136,128]{1,0:T(8,128)S(1)} %merge.1.own_ref.refs_0_), channel_id=1, source_target_pairs={{0,2},{1,3},{2,4},{3,5},{4,6},{5,7},{6,0},{7,1},{8,10},{9,11},{10,... | collective-permute-start | bytes 208904 | tf_op jit(solution)/shard_map/ppermute | solution.py:479
  19.3 1.6 %collective-permute-start.6 = (f32[544,128]{1,0:T(8,128)S(1)}, f32[544,128]{1,0:T(8,128)S(1)}, u32[]{:S(2)}, u32[]{:S(2)}) collective-permute-start(f32[544,128]{1,0:T(8,128)S(1)} %join.1.after_ref.same_ref), channel_id=1, source_target_pairs={{0,1},{1,0},{2,3},{3,2},{4,5},{5,4},{6,7},{7,6},{8,9},{9,8},{10,11... | collective-permute-start | bytes 835592 | tf_op jit(solution)/shard_map/ppermute | solution.py:501
  40.5 5.8 %collective-permute-start.7 = (f32[3,8,128]{2,1,0:T(8,128)S(1)}, f32[3,8,128]{2,1,0:T(8,128)S(1)}, u32[]{:S(2)}, u32[]{:S(2)}) collective-permute-start(f32[3,8,128]{2,1,0:T(8,128)S(1)} %get-tuple-element.26), channel_id=1, source_target_pairs={{0,8},{4,12},{8,16},{12,20},{16,24},{20,28},{24,0},{28,4},{1,9},{5... | collective-permute-start | bytes 36872 | tf_op jit(solution)/shard_map/ppermute | solution.py:535
  40.8 6.0 %collective-permute-start.8 = (f32[3,8,128]{2,1,0:T(8,128)S(1)}, f32[3,8,128]{2,1,0:T(8,128)S(1)}, u32[]{:S(2)}, u32[]{:S(2)}) collective-permute-start(f32[3,8,128]{2,1,0:T(8,128)S(1)} %get-tuple-element.27), channel_id=1, source_target_pairs={{0,16},{4,20},{8,24},{12,28},{16,0},{20,4},{24,8},{28,12},{1,17},{... | collective-permute-start | bytes 36872 | tf_op jit(solution)/shard_map/ppermute | solution.py:535
  45.1 3.7 %collective-permute-start.9 = (f32[3,8,128]{2,1,0:T(8,128)S(1)}, f32[3,8,128]{2,1,0:T(8,128)S(1)}, u32[]{:S(2)}, u32[]{:S(2)}) collective-permute-start(f32[3,8,128]{2,1,0:T(8,128)S(1)} %get-tuple-element.28), channel_id=1, source_target_pairs={{0,24},{4,28},{8,0},{12,4},{16,8},{20,12},{24,16},{28,20},{1,25},{... | collective-permute-start | bytes 36872 | tf_op jit(solution)/shard_map/ppermute | solution.py:535

commit v10 on v8

--- a/solution.py
+++ b/solution.py
@@ -12,6 +12,7 @@
 BACKGROUND = 0.5
 FAR = 32.0
 UNIT = 64
+SHORT = 32
 POINT_ROWS = 16
 AXES = ("row", "col")
 VMEM = pl.BlockSpec(memory_space=pltpu.VMEM)
@@ -321,15 +322,16 @@
     spare = 1.0 / (1.0 + jnp.exp(jnp.float32(-CONTACT_SHIFT)))
 
     def finish(ending):
-        sums = sums_ref[pl.ds(0, UNIT, stride=8), :]
+        unit = len(ending)
+        sums = sums_ref[pl.ds(0, unit, stride=8), :]
         for k in range(1, 8):
-            sums = sums + sums_ref[pl.ds(k, UNIT, stride=8), :]
+            sums = sums + sums_ref[pl.ds(k, unit, stride=8), :]
         chance = 64.0 * 128.0 + 0.5 * jnp.sum(sums, axis=1, keepdims=True)
-        count = jnp.sum(picks_ref[...], axis=1, keepdims=True)
-        state = state_ref[...]
+        count = jnp.sum(picks_ref[:unit], axis=1, keepdims=True)
+        state = state_ref[:unit]
         chance = jnp.where(state == 1, 0.5 * (chance - 128.0 * spare), chance)
         weight = jnp.where(state == 2, 0.0, 1.0 - count / (BACKGROUND + chance / 128.0))
-        for t in range(0, UNIT, 2):
+        for t in range(0, unit, 2):
             left, right = (second_ref[ending[t + i] & 4095] for i in range(2))
             blank = jnp.zeros_like(left)
             both = jnp.concatenate(
@@ -346,7 +348,7 @@
             total_ref[(ending[t] >> 19) & 127] += scale * product
 
     def begin(beginning):
-        for t in range(0, UNIT, 2):
+        for t in range(0, len(beginning), 2):
             seconds = [beginning[t + i][0] & 4095 for i in range(2)]
             logit = jnp.dot(
                 first_ref[(beginning[t][0] >> 12) & 127],
@@ -377,17 +379,17 @@
         return begin(beginning)
 
     def listed_step(turn, ending):
-        line = turn * UNIT >> 7
-        at = turn * UNIT & 127
-        beginning = [(list_ref[line, at + t], list_ref[chunks + line, at + t]) for t in range(UNIT)]
+        line = turn * SHORT >> 7
+        at = turn * SHORT & 127
+        beginning = [(list_ref[line, at + t], list_ref[chunks + line, at + t]) for t in range(SHORT)]
         finish(ending)
         return begin(beginning)
 
     idle = (jnp.int32(slots << 19),) * UNIT
     sums_ref[...] = jnp.zeros_like(sums_ref)
-    ending = lax.fori_loop(0, band_ref[4 * band_chunks, 0], band_step, idle)
-    listed_steps = lax.div(list_ref[2 * chunks, 0] + UNIT - 1, UNIT)
-    finish(lax.fori_loop(0, listed_steps, listed_step, ending))
+    finish(lax.fori_loop(0, band_ref[4 * band_chunks, 0], band_step, idle))
+    listed_steps = lax.div(list_ref[2 * chunks, 0] + SHORT - 1, SHORT)
+    finish(lax.fori_loop(0, listed_steps, listed_step, idle[:SHORT]))
 
     def collect(slot, carry):
         turned = jnp.transpose(total_ref[slot])

time: 50.4 us -> 50.5 us (level); the launches traced: 50.1 us -> 51.1 us
  starting transfers between devices: 14.5 us -> 15.2 us
    ppermute x3, starting transfers between devices: 3.89 us -> 4.56 us  [on_device(): arrived.append(lax.ppermute(gains[k], 'row', deal[k]))]
  transfers between devices with their start and end apart: 10 -> 10, of which waited for: 6 -> 6; matrix products, arithmetic and copies ran while one was open for 0% -> 0% of each run, Pallas kernels for 10% -> 9%
where the time goes in v10:
time: 50.5 us; the launch traced here: 51.1 us
  Pallas kernels  26.8 us (53%)
  starting transfers between devices  15.2 us (30%)
  waiting for transfers between devices  6.88 us (14%)
  local copies, waits for them, and re-layouts  2.18 us (4%)
    pallas_call x1, Pallas kernels, on_device(): pl.pallas_call(functools.partial(tile_kernel, sizes), out_shape=[jax.Shap...  21.2 us
    ppermute x3, starting transfers between devices, on_device(): received.append(lax.ppermute(messages[k], 'row', deal[k]))  6.96 us
    ppermute x3, starting transfers between devices, on_device(): arrived.append(lax.ppermute(gains[k], 'row', deal[k]))  4.56 us
    ppermute x3, waiting for transfers between devices, on_device(): arrived.append(lax.ppermute(gains[k], 'row', deal[k]))  3.69 us
    ppermute x3, starting transfers between devices, on_device(): pieces.append(lax.ppermute(own_row, AXES, moves))  3.6 us
    ppermute x3, waiting for transfers between devices, on_device(): pieces.append(lax.ppermute(own_row, AXES, moves))  2.64 us
    unnamed x10, local copies, waits for them, and re-layouts  2.18 us
    pallas_call x1, Pallas kernels, on_device(): pl.pallas_call(functools.partial(own_kernel, sizes), out_shape=[jax.Shape...  1.96 us
  transfers between devices with their start and end apart: 10, of which 6 were waited for; matrix products, arithmetic and copies ran while one was open for 0% of the time, Pallas kernels for 9%

profile of v10, /device:TPU:0, one launch (start us, length us, event | category | flops | bytes accessed | tf_op | source)
XLA Modules:
  0.0 51.1 jit_solution(7518298641163456460)
XLA Ops:
  0.0 0.0 copy-start
  0.0 0.8 %copy-done = f32[4,3,8,128]{3,2,1,0:T(8,128)S(1)} copy-done((f32[4,3,8,128]{3,2,1,0:T(8,128)S(1)}, f32[4,3,8,128]{3,2,1,0:T(8,128)}, u32[]{:S(2)}) %copy-start) | copy-done | bytes 49176
  0.8 0.0 copy-start.2
  0.8 0.7 %copy-done.2 = s32[4,8,1,32]{3,2,1,0:T(1,128)S(1)} copy-done((s32[4,8,1,32]{3,2,1,0:T(1,128)S(1)}, s32[4,8,1,32]{3,2,1,0:T(1,128)}, u32[]{:S(2)}) %copy-start.2) | copy-done | bytes 4120
  1.5 0.0 copy-start.3
  1.5 0.0 copy-start.1
  1.5 0.1 pack.1
  1.7 3.0 %collective-permute-start = (f32[40,128]{1,0:T(8,128)S(1)}, f32[40,128]{1,0:T(8,128)S(1)}, u32[]{:S(2)}, u32[]{:S(2)}) collective-permute-start(f32[40,128]{1,0:T(8,128)S(1)} %get-tuple-element.20), channel_id=1, source_target_pairs={{0,8},{4,12},{8,16},{12,20},{16,24},{20,28},{24,0},{28,4},{1,9},{5... | collective-permute-start | bytes 61448 | tf_op jit(solution)/shard_map/ppermute | solution.py:446
  4.7 2.6 %collective-permute-start.1 = (f32[40,128]{1,0:T(8,128)S(1)}, f32[40,128]{1,0:T(8,128)S(1)}, u32[]{:S(2)}, u32[]{:S(2)}) collective-permute-start(f32[40,128]{1,0:T(8,128)S(1)} %get-tuple-element.21), channel_id=1, source_target_pairs={{0,16},{4,20},{8,24},{12,28},{16,0},{20,4},{24,8},{28,12},{1,17},{... | collective-permute-start | bytes 61448 | tf_op jit(solution)/shard_map/ppermute | solution.py:446
  7.3 1.3 %collective-permute-start.2 = (f32[40,128]{1,0:T(8,128)S(1)}, f32[40,128]{1,0:T(8,128)S(1)}, u32[]{:S(2)}, u32[]{:S(2)}) collective-permute-start(f32[40,128]{1,0:T(8,128)S(1)} %get-tuple-element.22), channel_id=1, source_target_pairs={{0,24},{4,28},{8,0},{12,4},{16,8},{20,12},{24,16},{28,20},{1,25},{... | collective-permute-start | bytes 61448 | tf_op jit(solution)/shard_map/ppermute | solution.py:446
  8.6 0.0 copy-start.4
  8.6 0.7 %copy-done.4 = s32[46]{0:T(128)S(1)} copy-done((s32[46]{0:T(128)S(1)}, s32[46]{0:T(128)}, u32[]{:S(2)}) %copy-start.4) | copy-done | bytes 208
  9.3 1.2 %band_tiles.1 = (s32[44,128]{1,0:T(8,128)S(1)}, s32[2,48,128]{2,1,0:T(8,128)S(1)}) custom-call(s32[46]{0:T(128)S(1)} %copy-done.4), custom_call_target="tpu_custom_call" | custom-call | tf_op jit(solution)/shard_map/band_tiles/pallas_call | solution.py:448
  10.5 0.0 collective-permute-done.refs_1_
  10.5 0.0 collective-permute-done.1.refs_2_
  10.5 0.5 %collective-permute-done.2.refs_3_ = f32[40,128]{1,0:T(8,128)S(1)} collective-permute-done((f32[40,128]{1,0:T(8,128)S(1)}, f32[40,128]{1,0:T(8,128)S(1)}, u32[]{:S(2)}, u32[]{:S(2)}) %collective-permute-start.2) | collective-permute-done | bytes 20512 | tf_op jit(solution)/shard_map/ppermute | solution.py:446
  11.1 2.5 %collective-permute-start.5 = (f32[136,128]{1,0:T(8,128)S(1)}, f32[136,128]{1,0:T(8,128)S(1)}, u32[]{:S(2)}, u32[]{:S(2)}) collective-permute-start(f32[136,128]{1,0:T(8,128)S(1)} %merge.1.own_ref.refs_0_), channel_id=1, source_target_pairs={{0,6},{1,7},{2,0},{3,1},{4,2},{5,3},{6,4},{7,5},{8,14},{9,15},{10,... | collective-permute-start | bytes 208904 | tf_op jit(solution)/shard_map/ppermute | solution.py:481
  13.6 0.5 collective-permute-start.4
  14.1 0.6 %collective-permute-start.3 = (f32[136,128]{1,0:T(8,128)S(1)}, f32[136,128]{1,0:T(8,128)S(1)}, u32[]{:S(2)}, u32[]{:S(2)}) collective-permute-start(f32[136,128]{1,0:T(8,128)S(1)} %merge.1.own_ref.refs_0_), channel_id=1, source_target_pairs={{0,2},{1,3},{2,4},{3,5},{4,6},{5,7},{6,0},{7,1},{8,10},{9,11},{10,... | collective-permute-start | bytes 208904 | tf_op jit(solution)/shard_map/ppermute | solution.py:481
  14.7 2.0 %own_features.1 = (bf16[64,128,64]{2,1,0:T(8,128)(2,1)S(1)}, bf16[256,48,128]{2,1,0:T(8,128)(2,1)S(1)}) custom-call(s32[2,48,128]{2,1,0:T(8,128)S(1)} %get-tuple-element.18.edges_ref, f32[136,128]{1,0:T(8,128)S(1)} %merge.1.own_ref.refs_0_), custom_call_target="tpu_custom_call" | custom-call | tf_op jit(solution)/shard_map/own_features/pallas_call | solution.py:483
  16.6 0.0 collective-permute-done.5.refs_3_
  16.6 1.2 %collective-permute-done.4.refs_2_ = f32[136,128]{1,0:T(8,128)S(1)} collective-permute-done((f32[136,128]{1,0:T(8,128)S(1)}, f32[136,128]{1,0:T(8,128)S(1)}, u32[]{:S(2)}, u32[]{:S(2)}) %collective-permute-start.4) | collective-permute-done | bytes 69664 | tf_op jit(solution)/shard_map/ppermute | solution.py:481
  17.9 1.4 %collective-permute-done.3.refs_1_ = f32[136,128]{1,0:T(8,128)S(1)} collective-permute-done((f32[136,128]{1,0:T(8,128)S(1)}, f32[136,128]{1,0:T(8,128)S(1)}, u32[]{:S(2)}, u32[]{:S(2)}) %collective-permute-start.3) | collective-permute-done | bytes 69664 | tf_op jit(solution)/shard_map/ppermute | solution.py:481
  19.3 0.1 collective-permute-start.6
  19.4 0.0 copy-done.3
  19.4 1.7 %list_tiles.1.list_ref = s32[44,128]{1,0:T(8,128)S(1)} custom-call(s32[4,2,1024]{2,1,0:T(2,128)S(1)} %bitcast.1, f32[544,128]{1,0:T(8,128)S(1)} %join.1.after_ref.same_ref), custom_call_target="tpu_custom_call" | custom-call | flops 268435456 | bytes 4194304 | tf_op jit(solution)/shard_map/list_tiles/pallas_call | solution.py:505
  21.0 0.0 collective-permute-done.6.across_ref
  21.1 0.0 copy-done.1
  21.1 21.2 %tiles.1 = (f32[3,8,128]{2,1,0:T(8,128)S(1)}, f32[3,8,128]{2,1,0:T(8,128)S(1)}, f32[3,8,128]{2,1,0:T(8,128)S(1)}, f32[3,8,128]{2,1,0:T(8,128)S(1)}) custom-call(s32[44,128]{1,0:T(8,128)S(1)} %get-tuple-element.17.after_ref.band_ref, s32[44,128]{1,0:T(8,128)S(1)} %list_tiles.1.list_ref, s32[4,1024]{1,0:T(4,128)S(1)} %copy-done.1, ...), custom_call_target="tpu_custom_call" | custom-call | tf_op jit(solution)/shard_map/tiles/pallas_call | solution.py:516
  42.2 0.3 collective-permute-start.7
  42.5 4.3 %collective-permute-start.8 = (f32[3,8,128]{2,1,0:T(8,128)S(1)}, f32[3,8,128]{2,1,0:T(8,128)S(1)}, u32[]{:S(2)}, u32[]{:S(2)}) collective-permute-start(f32[3,8,128]{2,1,0:T(8,128)S(1)} %get-tuple-element.27), channel_id=1, source_target_pairs={{0,16},{4,20},{8,24},{12,28},{16,0},{20,4},{24,8},{28,12},{1,17},{... | collective-permute-start | bytes 36872 | tf_op jit(solution)/shard_map/ppermute | solution.py:537
  46.8 0.0 collective-permute-start.9
  46.8 1.1 %collective-permute-done.7.refs_1_ = f32[3,8,128]{2,1,0:T(8,128)S(1)} collective-permute-done((f32[3,8,128]{2,1,0:T(8,128)S(1)}, f32[3,8,128]{2,1,0:T(8,128)S(1)}, u32[]{:S(2)}, u32[]{:S(2)}) %collective-permute-start.7) | collective-permute-done | bytes 12320 | tf_op jit(solution)/shard_map/ppermute | solution.py:537
  47.9 0.6 %collective-permute-done.8.refs_2_ = f32[3,8,128]{2,1,0:T(8,128)S(1)} collective-permute-done((f32[3,8,128]{2,1,0:T(8,128)S(1)}, f32[3,8,128]{2,1,0:T(8,128)S(1)}, u32[]{:S(2)}, u32[]{:S(2)}) %collective-permute-start.8) | collective-permute-done | bytes 12320 | tf_op jit(solution)/shard_map/ppermute | solution.py:537
  48.5 2.0 %collective-permute-done.9.refs_3_ = f32[3,8,128]{2,1,0:T(8,128)S(1)} collective-permute-done((f32[3,8,128]{2,1,0:T(8,128)S(1)}, f32[3,8,128]{2,1,0:T(8,128)S(1)}, u32[]{:S(2)}, u32[]{:S(2)}) %collective-permute-start.9) | collective-permute-done | bytes 12320 | tf_op jit(solution)/shard_map/ppermute | solution.py:537
  50.5 0.6 %place.1 = f32[4,3,8,128]{3,2,1,0:T(8,128)} custom-call(f32[3,8,128]{2,1,0:T(8,128)S(1)} %get-tuple-element.25.refs_0_, f32[3,8,128]{2,1,0:T(8,128)S(1)} %collective-permute-done.7.refs_1_, f32[3,8,128]{2,1,0:T(8,128)S(1)} %collective-permute-done.8.refs_2_, f32[3,8,128]{2,1,0:T(8,128)S(1)} %collective-permute-done.9.refs_3_), custom_call_target="tpu_custom_call" | custom-call | tf_op jit(solution)/shard_map/place/pallas_call | solution.py:538
  (2 shorter events, 0.0 us)
Async XLA Ops:
  0.0 0.8 %copy-start = (f32[4,3,8,128]{3,2,1,0:T(8,128)S(1)}, f32[4,3,8,128]{3,2,1,0:T(8,128)}, u32[]{:S(2)}) copy-start(f32[4,3,8,128]{3,2,1,0:T(8,128)} %coords_ref.1) | copy-start | bytes 147460
  0.8 0.7 %copy-start.2 = (s32[4,8,1,32]{3,2,1,0:T(1,128)S(1)}, s32[4,8,1,32]{3,2,1,0:T(1,128)}, u32[]{:S(2)}) copy-start(s32[4,8,1,32]{3,2,1,0:T(1,128)} %counts_ref.1) | copy-start | bytes 12292
  1.5 17.9 %copy-start.3 = (s32[4,1024,2]{1,2,0:T(2,128)S(1)}, s32[4,1024,2]{1,2,0:T(2,128)}, u32[]{:S(2)}) copy-start(s32[4,1024,2]{1,2,0:T(2,128)} %param.8) | copy-start | bytes 98308
  1.5 19.5 %copy-start.1 = (s32[4,1024]{1,0:T(4,128)S(1)}, s32[4,1024]{1,0:T(4,128)}, u32[]{:S(2)}) copy-start(s32[4,1024]{1,0:T(4,128)} %listed_ref.1) | copy-start | bytes 49156
  1.7 8.8 %collective-permute-start = (f32[40,128]{1,0:T(8,128)S(1)}, f32[40,128]{1,0:T(8,128)S(1)}, u32[]{:S(2)}, u32[]{:S(2)}) collective-permute-start(f32[40,128]{1,0:T(8,128)S(1)} %get-tuple-element.20), channel_id=1, source_target_pairs={{0,8},{4,12},{8,16},{12,20},{16,24},{20,28},{24,0},{28,4},{1,9},{5... | collective-permute-start | bytes 61448 | tf_op jit(solution)/shard_map/ppermute | solution.py:446
  4.7 5.8 %collective-permute-start.1 = (f32[40,128]{1,0:T(8,128)S(1)}, f32[40,128]{1,0:T(8,128)S(1)}, u32[]{:S(2)}, u32[]{:S(2)}) collective-permute-start(f32[40,128]{1,0:T(8,128)S(1)} %get-tuple-element.21), channel_id=1, source_target_pairs={{0,16},{4,20},{8,24},{12,28},{16,0},{20,4},{24,8},{28,12},{1,17},{... | collective-permute-start | bytes 61448 | tf_op jit(solution)/shard_map/ppermute | solution.py:446
  7.3 3.8 %collective-permute-start.2 = (f32[40,128]{1,0:T(8,128)S(1)}, f32[40,128]{1,0:T(8,128)S(1)}, u32[]{:S(2)}, u32[]{:S(2)}) collective-permute-start(f32[40,128]{1,0:T(8,128)S(1)} %get-tuple-element.22), channel_id=1, source_target_pairs={{0,24},{4,28},{8,0},{12,4},{16,8},{20,12},{24,16},{28,20},{1,25},{... | collective-permute-start | bytes 61448 | tf_op jit(solution)/shard_map/ppermute | solution.py:446
  8.6 0.7 %copy-start.4 = (s32[46]{0:T(128)S(1)}, s32[46]{0:T(128)}, u32[]{:S(2)}) copy-start(s32[46]{0:T(128)} %lengths_ref.1) | copy-start | bytes 556
  11.1 5.6 %collective-permute-start.5 = (f32[136,128]{1,0:T(8,128)S(1)}, f32[136,128]{1,0:T(8,128)S(1)}, u32[]{:S(2)}, u32[]{:S(2)}) collective-permute-start(f32[136,128]{1,0:T(8,128)S(1)} %merge.1.own_ref.refs_0_), channel_id=1, source_target_pairs={{0,6},{1,7},{2,0},{3,1},{4,2},{5,3},{6,4},{7,5},{8,14},{9,15},{10,... | collective-permute-start | bytes 208904 | tf_op jit(solution)/shard_map/ppermute | solution.py:481
  13.6 4.3 %collective-permute-start.4 = (f32[136,128]{1,0:T(8,128)S(1)}, f32[136,128]{1,0:T(8,128)S(1)}, u32[]{:S(2)}, u32[]{:S(2)}) collective-permute-start(f32[136,128]{1,0:T(8,128)S(1)} %merge.1.own_ref.refs_0_), channel_id=1, source_target_pairs={{0,4},{1,5},{2,6},{3,7},{4,0},{5,1},{6,2},{7,3},{8,12},{9,13},{10,... | collective-permute-start | bytes 208904 | tf_op jit(solution)/shard_map/ppermute | solution.py:481
  14.1 5.2 %collective-permute-start.3 = (f32[136,128]{1,0:T(8,128)S(1)}, f32[136,128]{1,0:T(8,128)S(1)}, u32[]{:S(2)}, u32[]{:S(2)}) collective-permute-start(f32[136,128]{1,0:T(8,128)S(1)} %merge.1.own_ref.refs_0_), channel_id=1, source_target_pairs={{0,2},{1,3},{2,4},{3,5},{4,6},{5,7},{6,0},{7,1},{8,10},{9,11},{10,... | collective-permute-start | bytes 208904 | tf_op jit(solution)/shard_map/ppermute | solution.py:481
  19.3 1.8 %collective-permute-start.6 = (f32[544,128]{1,0:T(8,128)S(1)}, f32[544,128]{1,0:T(8,128)S(1)}, u32[]{:S(2)}, u32[]{:S(2)}) collective-permute-start(f32[544,128]{1,0:T(8,128)S(1)} %join.1.after_ref.same_ref), channel_id=1, source_target_pairs={{0,1},{1,0},{2,3},{3,2},{4,5},{5,4},{6,7},{7,6},{8,9},{9,8},{10,11... | collective-permute-start | bytes 835592 | tf_op jit(solution)/shard_map/ppermute | solution.py:503
  42.2 5.7 %collective-permute-start.7 = (f32[3,8,128]{2,1,0:T(8,128)S(1)}, f32[3,8,128]{2,1,0:T(8,128)S(1)}, u32[]{:S(2)}, u32[]{:S(2)}) collective-permute-start(f32[3,8,128]{2,1,0:T(8,128)S(1)} %get-tuple-element.26), channel_id=1, source_target_pairs={{0,8},{4,12},{8,16},{12,20},{16,24},{20,28},{24,0},{28,4},{1,9},{5... | collective-permute-start | bytes 36872 | tf_op jit(solution)/shard_map/ppermute | solution.py:537
  42.5 6.0 %collective-permute-start.8 = (f32[3,8,128]{2,1,0:T(8,128)S(1)}, f32[3,8,128]{2,1,0:T(8,128)S(1)}, u32[]{:S(2)}, u32[]{:S(2)}) collective-permute-start(f32[3,8,128]{2,1,0:T(8,128)S(1)} %get-tuple-element.27), channel_id=1, source_target_pairs={{0,16},{4,20},{8,24},{12,28},{16,0},{20,4},{24,8},{28,12},{1,17},{... | collective-permute-start | bytes 36872 | tf_op jit(solution)/shard_map/ppermute | solution.py:537
  46.8 3.7 %collective-permute-start.9 = (f32[3,8,128]{2,1,0:T(8,128)S(1)}, f32[3,8,128]{2,1,0:T(8,128)S(1)}, u32[]{:S(2)}, u32[]{:S(2)}) collective-permute-start(f32[3,8,128]{2,1,0:T(8,128)S(1)} %get-tuple-element.28), channel_id=1, source_target_pairs={{0,24},{4,28},{8,0},{12,4},{16,8},{20,12},{24,16},{28,20},{1,25},{... | collective-permute-start | bytes 36872 | tf_op jit(solution)/shard_map/ppermute | solution.py:537

commit v11 on v9

--- a/solution.py
+++ b/solution.py
@@ -320,7 +320,7 @@
     total_ref[...] = jnp.zeros_like(total_ref)
     spare = 1.0 / (1.0 + jnp.exp(jnp.float32(-CONTACT_SHIFT)))
 
-    def finish(ending):
+    def step(ending, beginning=None):
         sums = sums_ref[pl.ds(0, UNIT, stride=8), :]
         for k in range(1, 8):
             sums = sums + sums_ref[pl.ds(k, UNIT, stride=8), :]
@@ -344,9 +344,8 @@
                 weight[t + 1 : t + 2, : 2 * POINT_ROWS],
             )
             total_ref[(ending[t] >> 19) & 127] += scale * product
-
-    def begin(beginning):
-        for t in range(0, UNIT, 2):
+            if beginning is None:
+                continue
             seconds = [beginning[t + i][0] & 4095 for i in range(2)]
             logit = jnp.dot(
                 first_ref[(beginning[t][0] >> 12) & 127],
@@ -364,7 +363,7 @@
                 picked = counts_ref[pl.ds(place >> 7, 1), :]
                 picks_ref[t + i : t + i + 1] = jnp.where(lane == (place & 127), picked, 0.0)
                 state_ref[t + i : t + i + 1] = jnp.full((1, 128), code >> 26)
-        return tuple(code for code, _ in beginning)
+        return beginning and tuple(code for code, _ in beginning)
 
     def band_step(turn, ending):
         line = turn * (UNIT // 2) >> 7
@@ -373,21 +372,19 @@
         for t in range(UNIT):
             row = line + t % 2 * 2 * band_chunks
             beginning.append((band_ref[row, at + t // 2], band_ref[row + band_chunks, at + t // 2]))
-        finish(ending)
-        return begin(beginning)
+        return step(ending, beginning)
 
     def listed_step(turn, ending):
         line = turn * UNIT >> 7
         at = turn * UNIT & 127
         beginning = [(list_ref[line, at + t], list_ref[chunks + line, at + t]) for t in range(UNIT)]
-        finish(ending)
-        return begin(beginning)
+        return step(ending, beginning)
 
     idle = (jnp.int32(slots << 19),) * UNIT
     sums_ref[...] = jnp.zeros_like(sums_ref)
     ending = lax.fori_loop(0, band_ref[4 * band_chunks, 0], band_step, idle)
     listed_steps = lax.div(list_ref[2 * chunks, 0] + UNIT - 1, UNIT)
-    finish(lax.fori_loop(0, listed_steps, listed_step, ending))
+    step(lax.fori_loop(0, listed_steps, listed_step, ending))
 
     def collect(slot, carry):
         turned = jnp.transpose(total_ref[slot])

time: 50 us -> 48.7 us (0.974); the launches traced: 49.4 us -> 48.8 us
  starting transfers between devices: 15.2 us -> 14.5 us
    ppermute x3, starting transfers between devices: 4.57 us -> 3.88 us  [on_device(): arrived.append(lax.ppermute(gains[k], 'row', deal[k]))]
  transfers between devices with their start and end apart: 10 -> 10, of which waited for: 7 -> 6; matrix products, arithmetic and copies ran while one was open for 0% -> 0% of each run, Pallas kernels for 9% -> 9%
where the time goes in v11:
time: 48.7 us; the launch traced here: 48.8 us
  Pallas kernels  25.1 us (52%)
  starting transfers between devices  14.5 us (30%)
  waiting for transfers between devices  6.93 us (14%)
  local copies, waits for them, and re-layouts  2.18 us (4%)
    pallas_call x1, Pallas kernels, on_device(): pl.pallas_call(functools.partial(tile_kernel, sizes), out_shape=[jax.Shap...  19.8 us
    ppermute x3, starting transfers between devices, on_device(): received.append(lax.ppermute(messages[k], 'row', deal[k]))  6.96 us
    ppermute x3, starting transfers between devices, on_device(): arrived.append(lax.ppermute(gains[k], 'row', deal[k]))  3.88 us
    ppermute x3, starting transfers between devices, on_device(): pieces.append(lax.ppermute(own_row, AXES, moves))  3.6 us
    ppermute x3, waiting for transfers between devices, on_device(): arrived.append(lax.ppermute(gains[k], 'row', deal[k]))  3.58 us
    ppermute x3, waiting for transfers between devices, on_device(): pieces.append(lax.ppermute(own_row, AXES, moves))  2.64 us
    unnamed x10, local copies, waits for them, and re-layouts  2.18 us
    pallas_call x1, Pallas kernels, on_device(): pl.pallas_call(functools.partial(own_kernel, sizes), out_shape=[jax.Shape...  1.96 us
  transfers between devices with their start and end apart: 10, of which 6 were waited for; matrix products, arithmetic and copies ran while one was open for 0% of the time, Pallas kernels for 9%

profile of v11, /device:TPU:0, one launch (start us, length us, event | category | flops | bytes accessed | tf_op | source)
XLA Modules:
  0.0 48.8 jit_solution(2303075145193765448)
XLA Ops:
  0.0 0.0 copy-start
  0.0 0.8 %copy-done = f32[4,3,8,128]{3,2,1,0:T(8,128)S(1)} copy-done((f32[4,3,8,128]{3,2,1,0:T(8,128)S(1)}, f32[4,3,8,128]{3,2,1,0:T(8,128)}, u32[]{:S(2)}) %copy-start) | copy-done | bytes 49176
  0.8 0.0 copy-start.2
  0.8 0.7 %copy-done.2 = s32[4,8,1,32]{3,2,1,0:T(1,128)S(1)} copy-done((s32[4,8,1,32]{3,2,1,0:T(1,128)S(1)}, s32[4,8,1,32]{3,2,1,0:T(1,128)}, u32[]{:S(2)}) %copy-start.2) | copy-done | bytes 4120
  1.5 0.0 copy-start.3
  1.5 0.0 copy-start.1
  1.5 0.1 pack.1
  1.7 3.0 %collective-permute-start = (f32[40,128]{1,0:T(8,128)S(1)}, f32[40,128]{1,0:T(8,128)S(1)}, u32[]{:S(2)}, u32[]{:S(2)}) collective-permute-start(f32[40,128]{1,0:T(8,128)S(1)} %get-tuple-element.20), channel_id=1, source_target_pairs={{0,8},{4,12},{8,16},{12,20},{16,24},{20,28},{24,0},{28,4},{1,9},{5... | collective-permute-start | bytes 61448 | tf_op jit(solution)/shard_map/ppermute | solution.py:441
  4.7 2.6 %collective-permute-start.1 = (f32[40,128]{1,0:T(8,128)S(1)}, f32[40,128]{1,0:T(8,128)S(1)}, u32[]{:S(2)}, u32[]{:S(2)}) collective-permute-start(f32[40,128]{1,0:T(8,128)S(1)} %get-tuple-element.21), channel_id=1, source_target_pairs={{0,16},{4,20},{8,24},{12,28},{16,0},{20,4},{24,8},{28,12},{1,17},{... | collective-permute-start | bytes 61448 | tf_op jit(solution)/shard_map/ppermute | solution.py:441
  7.3 1.3 %collective-permute-start.2 = (f32[40,128]{1,0:T(8,128)S(1)}, f32[40,128]{1,0:T(8,128)S(1)}, u32[]{:S(2)}, u32[]{:S(2)}) collective-permute-start(f32[40,128]{1,0:T(8,128)S(1)} %get-tuple-element.22), channel_id=1, source_target_pairs={{0,24},{4,28},{8,0},{12,4},{16,8},{20,12},{24,16},{28,20},{1,25},{... | collective-permute-start | bytes 61448 | tf_op jit(solution)/shard_map/ppermute | solution.py:441
  8.6 0.0 copy-start.4
  8.6 0.7 %copy-done.4 = s32[46]{0:T(128)S(1)} copy-done((s32[46]{0:T(128)S(1)}, s32[46]{0:T(128)}, u32[]{:S(2)}) %copy-start.4) | copy-done | bytes 208
  9.3 1.2 %band_tiles.1 = (s32[44,128]{1,0:T(8,128)S(1)}, s32[2,48,128]{2,1,0:T(8,128)S(1)}) custom-call(s32[46]{0:T(128)S(1)} %copy-done.4), custom_call_target="tpu_custom_call" | custom-call | tf_op jit(solution)/shard_map/band_tiles/pallas_call | solution.py:443
  10.5 0.0 collective-permute-done.refs_1_
  10.5 0.0 collective-permute-done.1.refs_2_
  10.5 0.6 %collective-permute-done.2.refs_3_ = f32[40,128]{1,0:T(8,128)S(1)} collective-permute-done((f32[40,128]{1,0:T(8,128)S(1)}, f32[40,128]{1,0:T(8,128)S(1)}, u32[]{:S(2)}, u32[]{:S(2)}) %collective-permute-start.2) | collective-permute-done | bytes 20512 | tf_op jit(solution)/shard_map/ppermute | solution.py:441
  11.1 2.5 %collective-permute-start.5 = (f32[136,128]{1,0:T(8,128)S(1)}, f32[136,128]{1,0:T(8,128)S(1)}, u32[]{:S(2)}, u32[]{:S(2)}) collective-permute-start(f32[136,128]{1,0:T(8,128)S(1)} %merge.1.own_ref.refs_0_), channel_id=1, source_target_pairs={{0,6},{1,7},{2,0},{3,1},{4,2},{5,3},{6,4},{7,5},{8,14},{9,15},{10,... | collective-permute-start | bytes 208904 | tf_op jit(solution)/shard_map/ppermute | solution.py:476
  13.6 0.5 %collective-permute-start.4 = (f32[136,128]{1,0:T(8,128)S(1)}, f32[136,128]{1,0:T(8,128)S(1)}, u32[]{:S(2)}, u32[]{:S(2)}) collective-permute-start(f32[136,128]{1,0:T(8,128)S(1)} %merge.1.own_ref.refs_0_), channel_id=1, source_target_pairs={{0,4},{1,5},{2,6},{3,7},{4,0},{5,1},{6,2},{7,3},{8,12},{9,13},{10,... | collective-permute-start | bytes 208904 | tf_op jit(solution)/shard_map/ppermute | solution.py:476
  14.1 0.6 %collective-permute-start.3 = (f32[136,128]{1,0:T(8,128)S(1)}, f32[136,128]{1,0:T(8,128)S(1)}, u32[]{:S(2)}, u32[]{:S(2)}) collective-permute-start(f32[136,128]{1,0:T(8,128)S(1)} %merge.1.own_ref.refs_0_), channel_id=1, source_target_pairs={{0,2},{1,3},{2,4},{3,5},{4,6},{5,7},{6,0},{7,1},{8,10},{9,11},{10,... | collective-permute-start | bytes 208904 | tf_op jit(solution)/shard_map/ppermute | solution.py:476
  14.7 2.0 %own_features.1 = (bf16[64,128,64]{2,1,0:T(8,128)(2,1)S(1)}, bf16[256,48,128]{2,1,0:T(8,128)(2,1)S(1)}) custom-call(s32[2,48,128]{2,1,0:T(8,128)S(1)} %get-tuple-element.18.edges_ref, f32[136,128]{1,0:T(8,128)S(1)} %merge.1.own_ref.refs_0_), custom_call_target="tpu_custom_call" | custom-call | tf_op jit(solution)/shard_map/own_features/pallas_call | solution.py:478
  16.6 0.0 collective-permute-done.5.refs_3_
  16.6 1.2 %collective-permute-done.4.refs_2_ = f32[136,128]{1,0:T(8,128)S(1)} collective-permute-done((f32[136,128]{1,0:T(8,128)S(1)}, f32[136,128]{1,0:T(8,128)S(1)}, u32[]{:S(2)}, u32[]{:S(2)}) %collective-permute-start.4) | collective-permute-done | bytes 69664 | tf_op jit(solution)/shard_map/ppermute | solution.py:476
  17.9 1.4 %collective-permute-done.3.refs_1_ = f32[136,128]{1,0:T(8,128)S(1)} collective-permute-done((f32[136,128]{1,0:T(8,128)S(1)}, f32[136,128]{1,0:T(8,128)S(1)}, u32[]{:S(2)}, u32[]{:S(2)}) %collective-permute-start.3) | collective-permute-done | bytes 69664 | tf_op jit(solution)/shard_map/ppermute | solution.py:476
  19.3 0.1 collective-permute-start.6
  19.4 0.0 copy-done.3
  19.4 1.4 %list_tiles.1.list_ref = s32[42,128]{1,0:T(8,128)S(1)} custom-call(s32[4,2,1024]{2,1,0:T(2,128)S(1)} %bitcast.1, f32[544,128]{1,0:T(8,128)S(1)} %join.1.after_ref.same_ref), custom_call_target="tpu_custom_call" | custom-call | flops 268435456 | bytes 4194304 | tf_op jit(solution)/shard_map/list_tiles/pallas_call | solution.py:500
  20.8 0.1 collective-permute-done.6.across_ref
  20.9 0.0 copy-done.1
  20.9 19.8 %tiles.1 = (f32[3,8,128]{2,1,0:T(8,128)S(1)}, f32[3,8,128]{2,1,0:T(8,128)S(1)}, f32[3,8,128]{2,1,0:T(8,128)S(1)}, f32[3,8,128]{2,1,0:T(8,128)S(1)}) custom-call(s32[44,128]{1,0:T(8,128)S(1)} %get-tuple-element.17.after_ref.band_ref, s32[42,128]{1,0:T(8,128)S(1)} %list_tiles.1.list_ref, s32[4,1024]{1,0:T(4,128)S(1)} %copy-done.1, ...), custom_call_target="tpu_custom_call" | custom-call | tf_op jit(solution)/shard_map/tiles/pallas_call | solution.py:511
  40.7 0.3 collective-permute-start.7
  41.0 3.5 %collective-permute-start.8 = (f32[3,8,128]{2,1,0:T(8,128)S(1)}, f32[3,8,128]{2,1,0:T(8,128)S(1)}, u32[]{:S(2)}, u32[]{:S(2)}) collective-permute-start(f32[3,8,128]{2,1,0:T(8,128)S(1)} %get-tuple-element.27), channel_id=1, source_target_pairs={{0,16},{4,20},{8,24},{12,28},{16,0},{20,4},{24,8},{28,12},{1,17},{... | collective-permute-start | bytes 36872 | tf_op jit(solution)/shard_map/ppermute | solution.py:532
  44.5 0.1 collective-permute-start.9
  44.6 1.7 %collective-permute-done.7.refs_1_ = f32[3,8,128]{2,1,0:T(8,128)S(1)} collective-permute-done((f32[3,8,128]{2,1,0:T(8,128)S(1)}, f32[3,8,128]{2,1,0:T(8,128)S(1)}, u32[]{:S(2)}, u32[]{:S(2)}) %collective-permute-start.7) | collective-permute-done | bytes 12320 | tf_op jit(solution)/shard_map/ppermute | solution.py:532
  46.3 0.0 collective-permute-done.8.refs_2_
  46.3 1.9 %collective-permute-done.9.refs_3_ = f32[3,8,128]{2,1,0:T(8,128)S(1)} collective-permute-done((f32[3,8,128]{2,1,0:T(8,128)S(1)}, f32[3,8,128]{2,1,0:T(8,128)S(1)}, u32[]{:S(2)}, u32[]{:S(2)}) %collective-permute-start.9) | collective-permute-done | bytes 12320 | tf_op jit(solution)/shard_map/ppermute | solution.py:532
  48.2 0.6 %place.1 = f32[4,3,8,128]{3,2,1,0:T(8,128)} custom-call(f32[3,8,128]{2,1,0:T(8,128)S(1)} %get-tuple-element.25.refs_0_, f32[3,8,128]{2,1,0:T(8,128)S(1)} %collective-permute-done.7.refs_1_, f32[3,8,128]{2,1,0:T(8,128)S(1)} %collective-permute-done.8.refs_2_, f32[3,8,128]{2,1,0:T(8,128)S(1)} %collective-permute-done.9.refs_3_), custom_call_target="tpu_custom_call" | custom-call | tf_op jit(solution)/shard_map/place/pallas_call | solution.py:533
  (2 shorter events, 0.0 us)
Async XLA Ops:
  0.0 0.8 %copy-start = (f32[4,3,8,128]{3,2,1,0:T(8,128)S(1)}, f32[4,3,8,128]{3,2,1,0:T(8,128)}, u32[]{:S(2)}) copy-start(f32[4,3,8,128]{3,2,1,0:T(8,128)} %coords_ref.1) | copy-start | bytes 147460
  0.8 0.7 %copy-start.2 = (s32[4,8,1,32]{3,2,1,0:T(1,128)S(1)}, s32[4,8,1,32]{3,2,1,0:T(1,128)}, u32[]{:S(2)}) copy-start(s32[4,8,1,32]{3,2,1,0:T(1,128)} %counts_ref.1) | copy-start | bytes 12292
  1.5 17.9 %copy-start.3 = (s32[4,1024,2]{1,2,0:T(2,128)S(1)}, s32[4,1024,2]{1,2,0:T(2,128)}, u32[]{:S(2)}) copy-start(s32[4,1024,2]{1,2,0:T(2,128)} %param.8) | copy-start | bytes 98308
  1.5 19.4 %copy-start.1 = (s32[4,1024]{1,0:T(4,128)S(1)}, s32[4,1024]{1,0:T(4,128)}, u32[]{:S(2)}) copy-start(s32[4,1024]{1,0:T(4,128)} %listed_ref.1) | copy-start | bytes 49156
  1.7 8.8 %collective-permute-start = (f32[40,128]{1,0:T(8,128)S(1)}, f32[40,128]{1,0:T(8,128)S(1)}, u32[]{:S(2)}, u32[]{:S(2)}) collective-permute-start(f32[40,128]{1,0:T(8,128)S(1)} %get-tuple-element.20), channel_id=1, source_target_pairs={{0,8},{4,12},{8,16},{12,20},{16,24},{20,28},{24,0},{28,4},{1,9},{5... | collective-permute-start | bytes 61448 | tf_op jit(solution)/shard_map/ppermute | solution.py:441
  4.7 5.8 %collective-permute-start.1 = (f32[40,128]{1,0:T(8,128)S(1)}, f32[40,128]{1,0:T(8,128)S(1)}, u32[]{:S(2)}, u32[]{:S(2)}) collective-permute-start(f32[40,128]{1,0:T(8,128)S(1)} %get-tuple-element.21), channel_id=1, source_target_pairs={{0,16},{4,20},{8,24},{12,28},{16,0},{20,4},{24,8},{28,12},{1,17},{... | collective-permute-start | bytes 61448 | tf_op jit(solution)/shard_map/ppermute | solution.py:441
  7.3 3.8 %collective-permute-start.2 = (f32[40,128]{1,0:T(8,128)S(1)}, f32[40,128]{1,0:T(8,128)S(1)}, u32[]{:S(2)}, u32[]{:S(2)}) collective-permute-start(f32[40,128]{1,0:T(8,128)S(1)} %get-tuple-element.22), channel_id=1, source_target_pairs={{0,24},{4,28},{8,0},{12,4},{16,8},{20,12},{24,16},{28,20},{1,25},{... | collective-permute-start | bytes 61448 | tf_op jit(solution)/shard_map/ppermute | solution.py:441
  8.6 0.7 %copy-start.4 = (s32[46]{0:T(128)S(1)}, s32[46]{0:T(128)}, u32[]{:S(2)}) copy-start(s32[46]{0:T(128)} %lengths_ref.1) | copy-start | bytes 556
  11.1 5.6 %collective-permute-start.5 = (f32[136,128]{1,0:T(8,128)S(1)}, f32[136,128]{1,0:T(8,128)S(1)}, u32[]{:S(2)}, u32[]{:S(2)}) collective-permute-start(f32[136,128]{1,0:T(8,128)S(1)} %merge.1.own_ref.refs_0_), channel_id=1, source_target_pairs={{0,6},{1,7},{2,0},{3,1},{4,2},{5,3},{6,4},{7,5},{8,14},{9,15},{10,... | collective-permute-start | bytes 208904 | tf_op jit(solution)/shard_map/ppermute | solution.py:476
  13.6 4.3 %collective-permute-start.4 = (f32[136,128]{1,0:T(8,128)S(1)}, f32[136,128]{1,0:T(8,128)S(1)}, u32[]{:S(2)}, u32[]{:S(2)}) collective-permute-start(f32[136,128]{1,0:T(8,128)S(1)} %merge.1.own_ref.refs_0_), channel_id=1, source_target_pairs={{0,4},{1,5},{2,6},{3,7},{4,0},{5,1},{6,2},{7,3},{8,12},{9,13},{10,... | collective-permute-start | bytes 208904 | tf_op jit(solution)/shard_map/ppermute | solution.py:476
  14.1 5.2 %collective-permute-start.3 = (f32[136,128]{1,0:T(8,128)S(1)}, f32[136,128]{1,0:T(8,128)S(1)}, u32[]{:S(2)}, u32[]{:S(2)}) collective-permute-start(f32[136,128]{1,0:T(8,128)S(1)} %merge.1.own_ref.refs_0_), channel_id=1, source_target_pairs={{0,2},{1,3},{2,4},{3,5},{4,6},{5,7},{6,0},{7,1},{8,10},{9,11},{10,... | collective-permute-start | bytes 208904 | tf_op jit(solution)/shard_map/ppermute | solution.py:476
  19.3 1.6 %collective-permute-start.6 = (f32[544,128]{1,0:T(8,128)S(1)}, f32[544,128]{1,0:T(8,128)S(1)}, u32[]{:S(2)}, u32[]{:S(2)}) collective-permute-start(f32[544,128]{1,0:T(8,128)S(1)} %join.1.after_ref.same_ref), channel_id=1, source_target_pairs={{0,1},{1,0},{2,3},{3,2},{4,5},{5,4},{6,7},{7,6},{8,9},{9,8},{10,11... | collective-permute-start | bytes 835592 | tf_op jit(solution)/shard_map/ppermute | solution.py:498
  40.7 5.6 %collective-permute-start.7 = (f32[3,8,128]{2,1,0:T(8,128)S(1)}, f32[3,8,128]{2,1,0:T(8,128)S(1)}, u32[]{:S(2)}, u32[]{:S(2)}) collective-permute-start(f32[3,8,128]{2,1,0:T(8,128)S(1)} %get-tuple-element.26), channel_id=1, source_target_pairs={{0,8},{4,12},{8,16},{12,20},{16,24},{20,28},{24,0},{28,4},{1,9},{5... | collective-permute-start | bytes 36872 | tf_op jit(solution)/shard_map/ppermute | solution.py:532
  41.0 5.3 %collective-permute-start.8 = (f32[3,8,128]{2,1,0:T(8,128)S(1)}, f32[3,8,128]{2,1,0:T(8,128)S(1)}, u32[]{:S(2)}, u32[]{:S(2)}) collective-permute-start(f32[3,8,128]{2,1,0:T(8,128)S(1)} %get-tuple-element.27), channel_id=1, source_target_pairs={{0,16},{4,20},{8,24},{12,28},{16,0},{20,4},{24,8},{28,12},{1,17},{... | collective-permute-start | bytes 36872 | tf_op jit(solution)/shard_map/ppermute | solution.py:532
  44.5 3.7 %collective-permute-start.9 = (f32[3,8,128]{2,1,0:T(8,128)S(1)}, f32[3,8,128]{2,1,0:T(8,128)S(1)}, u32[]{:S(2)}, u32[]{:S(2)}) collective-permute-start(f32[3,8,128]{2,1,0:T(8,128)S(1)} %get-tuple-element.28), channel_id=1, source_target_pairs={{0,24},{4,28},{8,0},{12,4},{16,8},{20,12},{24,16},{28,20},{1,25},{... | collective-permute-start | bytes 36872 | tf_op jit(solution)/shard_map/ppermute | solution.py:532
